TPU v7x, 128 devices: a whole 4x4x4 slice. The times are simulated.
128 devices in a mesh: blk: 8 (over z_lo, y), group: 16 (over x, z_hi, core).
Axes of the slice: x: 4, y: 4, z: 4 (z_hi: 2, z_lo: 2; z = z_hi * 2 + z_lo), core: 2. Of those that a mesh axis runs over, the one named last changes fastest.
Arguments:
- micrograph: bfloat16 [3072, 6144], P('blk', 'group'), may hold values from -6 to 6
- templates: bfloat16 [8, 384, 384], P('blk'), may hold values from -450 to 450
- ref_bank: bfloat16 [128, 384, 384], P('group'), may hold values from -0.015625 to 0.015625
- peak_offsets: int32 [2048, 2], P(('blk', 'group')), may hold values from 0 to 383
- peak_template: int32 [2048], P(('blk', 'group')), may hold values from 0 to 7
- owners: int32 [2048, 1], P(('blk', 'group')), may hold values from 0 to 15; in each aligned block of 16 rows (0 to 15, 16 to 31, ...) at most 2 rows name the same one
Outputs:
- mip: float32 [3072, 6144], P('blk', 'group')
- zmap: float32 [3072, 6144], P('blk', 'group')
- refined: float32 [2048, 9], P(('blk', 'group'))
Inputs may be any that keep to these rules, and one draw needn't show every extreme that they name: `owners`: among the candidates of one device no owner is named more than 2 times.
All inputs are finite; a program needn't handle non-finite values.
Results may differ from a plain program's by a relative error of at most 0.013.
Values may be sent and summed in bfloat16 or wider, within the bound.
No kernel may reach another device: no remote copies, remote signals or barrier semaphores. Data moves between devices by JAX's collectives and lax.ppermute only.
A program may use at most 192 MiB of HBM per device.

v0:
```python
import math

import jax
import jax.numpy as jnp
import numpy as np
from jax import lax
from jax.experimental import pallas as pl
from jax.experimental.pallas import tpu as pltpu
from jax.sharding import Mesh
from jax.sharding import PartitionSpec as P

L = 384
H = 192
Q = 96
SLABS = 64
ROWS = 40
WIDE = 1280
BF = jnp.bfloat16
F32 = jnp.float32
MB = 1024 * 1024
ROWS_OF = ("zl", "y")
COLS_OF = ("x", "zh", "core")
CHIPS = ("zl", "y", "x", "zh")


def dot(a, b):
    return jnp.dot(a, b, preferred_element_type=F32)


def wave(a, b):
    angle = (np.multiply.outer(np.asarray(a), np.asarray(b)) % L) * (2.0 * math.pi / L)
    return np.cos(angle), np.sin(angle)


def bf(a):
    return np.asarray(a, np.float32).astype(jnp.bfloat16)


def make_tables():
    n = np.arange(L)
    cos, sin = wave(n, n)
    forward = np.concatenate([cos[:H], cos[H : H + 1], sin[1:H]], 0)
    halves = np.stack(
        [np.concatenate([forward[c * Q : c * Q + Q], forward[H + c * Q : H + c * Q + Q]], 0) for c in range(2)]
    )
    pair = np.concatenate([cos, sin], 1)
    inverse_cols = np.concatenate([pair, np.concatenate([-sin, cos], 1)], 0)
    weight = np.full((H,), 2.0)
    weight[0] = 1.0
    inverse_rows = np.concatenate([cos[:, :H] * weight, -2.0 * sin[:, :H]], 1)
    inverse_rows[:, H] = cos[:, H]
    reverse = np.zeros((L, L))
    reverse[(-n) % L, n] = 1.0
    pick = np.zeros((4, L, 128))
    for part in range(4):
        pick[part, n, 80 + 6 * part + n % 6] = 1.0
    lane = np.arange(128)
    ac = lane % 16
    live = (ac < 9).astype(np.float64)
    a, c = ac // 3 - 1, ac % 3 - 1
    col_cos, col_sin = wave(n, c)
    turn = np.zeros((SLABS, 16, L))
    shift = np.zeros((SLABS, 8, 128))
    extra = np.zeros((SLABS, 16, 128))
    for s in range(SLABS):
        for part in range(3):
            k = s + 64 * part
            kc, ks = wave([k], n)
            turn[s, part], turn[s, 3 + part] = kc[0], ks[0]
            ac_, as_ = wave([k], a)
            w = (1.0 if k == 0 else 2.0) * live
            shift[s, part], shift[s, 3 + part] = ac_[0] * w, as_[0] * w
        turn[s, 6] = cos[H]
        sign = np.where(a == 0, 1.0, -1.0) * live
        extra[s, :6] = sign * col_cos[6 * s : 6 * s + 6]
        extra[s, 8:14] = -sign * col_sin[6 * s : 6 * s + 6]
    return dict(
        forward=bf(forward),
        halves=bf(halves),
        pair=bf(pair),
        inverse_cols=bf(inverse_cols),
        inverse_rows=bf(inverse_rows),
        reverse=bf(reverse),
        pick=bf(pick.reshape(4 * L, 128)),
        col_cos=col_cos.astype(np.float32),
        col_sin=col_sin.astype(np.float32),
        turn=bf(turn),
        shift=shift.astype(np.float32),
        extra=extra.astype(np.float32),
    )


TAB = make_tables()


def full_spec(shape):
    zeros = (0,) * len(shape)
    return pl.BlockSpec(shape, lambda i, ids: zeros)


def iota(shape, dim):
    return lax.broadcasted_iota(jnp.int32, shape, dim)


def spectra_kernel(ids, tile, ref, meta, forward, pair, pick, msg, spec, flat):
    rows64 = iota((SLABS, L), 0)
    owned = (iota((SLABS, L), 1) // 6) == rows64
    first_row = rows64 == 0
    flat[...] = jnp.zeros_like(flat)
    lasts = []
    for which, image in enumerate((tile[...], ref[0])):
        first = dot(forward[...], image).astype(BF)
        second = dot(first, pair[...])
        real = second[:H, :L] - second[H:, L:]
        imag = -(second[:H, L:] + second[H:, :L])
        if which == 0:
            spec[0] = real.astype(BF)
            spec[1] = imag.astype(BF)
        for plane, (full, alone) in enumerate(((real, second[:64, :L]), (imag, -second[:64, L:]))):
            for part in range(3):
                block = full[64 * part : 64 * part + 64]
                if part == 0:
                    block = jnp.where(first_row, alone, block)
                for j in range(3):
                    row = 18 * which + 9 * plane + 3 * part + j
                    flat[pl.ds(row, SLABS, stride=ROWS), :] = block[:, 128 * j : 128 * j + 128]
        for last in (second[H : H + 1, :L], -second[H : H + 1, L:]):
            lasts.append(jnp.where(owned, jnp.broadcast_to(last, (SLABS, L)), 0.0).astype(BF))
    line = dot(jnp.concatenate(lasts, 1), pick[...])
    flat[pl.ds(36, SLABS, stride=ROWS), :] = line + meta[...]
    msg[...] = flat[...].reshape(SLABS, ROWS, 128).astype(BF)


def make_spectra(ids, tile, bank, meta):
    return pl.pallas_call(
        spectra_kernel,
        out_shape=(
            jax.ShapeDtypeStruct((SLABS, ROWS, 128), BF),
            jax.ShapeDtypeStruct((2, H, L), BF),
        ),
        grid_spec=pltpu.PrefetchScalarGridSpec(
            num_scalar_prefetch=1,
            grid=(1,),
            in_specs=[
                full_spec((L, L)),
                pl.BlockSpec((1, L, L), lambda i, ids: (ids[0], 0, 0)),
                full_spec((1, 128)),
                full_spec((L, L)),
                full_spec((L, 2 * L)),
                full_spec((4 * L, 128)),
            ],
            out_specs=[full_spec((SLABS, ROWS, 128)), full_spec((2, H, L))],
            scratch_shapes=[pltpu.VMEM((SLABS * ROWS, 128), F32)],
        ),
        compiler_params=pltpu.CompilerParams(vmem_limit_bytes=40 * MB),
        cost_estimate=pl.CostEstimate(flops=800_000_000, bytes_accessed=3 * MB, transcendentals=0),
        name="tile_spectra",
    )(ids, tile, bank, meta, TAB["forward"], TAB["pair"], TAB["pick"])


def template_kernel(ids, template, halves, pair, half):
    values = template[0].astype(F32)
    count = 1.0 / (L * L)
    centre = jnp.sum(values) * count
    spread = values - centre
    power = jnp.sum(spread * spread) * count
    scale = 1.0 / (L * jnp.sqrt(jnp.full((1, 1), power + 1e-06, F32)))
    normalized = (spread * scale).astype(BF)
    first = dot(halves[0], normalized).astype(BF)
    second = dot(first, pair[...])
    half[0] = (second[:Q, :L] - second[Q:, L:]).astype(BF)
    half[1] = (-(second[:Q, L:] + second[Q:, :L])).astype(BF)


def template_half(ids, templates):
    return pl.pallas_call(
        template_kernel,
        out_shape=jax.ShapeDtypeStruct((2, Q, L), BF),
        grid_spec=pltpu.PrefetchScalarGridSpec(
            num_scalar_prefetch=1,
            grid=(1,),
            in_specs=[
                full_spec((1, L, L)),
                pl.BlockSpec((1, H, L), lambda i, ids: (ids[1], 0, 0)),
                full_spec((L, 2 * L)),
            ],
            out_specs=full_spec((2, Q, L)),
        ),
        compiler_params=pltpu.CompilerParams(vmem_limit_bytes=40 * MB),
        cost_estimate=pl.CostEstimate(flops=200_000_000, bytes_accessed=2 * MB, transcendentals=0),
        name="template_spectrum",
    )(ids, templates, TAB["halves"], TAB["pair"])


def refine_kernel(
    ids, own, other, pair, turn, shift, extra, col_cos, col_sin, out, flat, tiles, refs, waves, comb
):
    slab = ids[2]
    lane64 = iota((SLABS, 128), 1)

    def spread(base, target, rows):
        for plane in range(2):
            for j in range(9):
                col = plane * WIDE + 128 * j
                target[rows, col : col + 128] = flat[
                    pl.ds(base + 9 * plane + j, SLABS, stride=ROWS), :
                ].astype(target.dtype)
        line = flat[pl.ds(36, SLABS, stride=ROWS), :]
        for plane in range(2):
            at = 80 + (12 if base else 0) + 6 * plane
            moved = jnp.where(lane64 < 6, pltpu.roll(line, 128 - at, axis=1), 0.0)
            col = plane * WIDE + 1152
            target[rows, col : col + 128] = moved.astype(target.dtype)
        return line

    flat[...] = other[...].astype(F32).reshape(SLABS * ROWS, 128)
    spread(18, refs, slice(64, 128))
    flat[...] = own[...].astype(F32).reshape(SLABS * ROWS, 128)
    spread(18, refs, slice(0, 64))
    meta = spread(0, tiles, slice(0, 64)).astype(BF)

    waves[:, : 2 * L] = pair[...]
    wanted = (iota((L, 128), 0) == iota((L, 128), 1) + 6 * slab).astype(BF)
    waves[:, 768:896] = dot(pair[:, :L], wanted).astype(BF)
    waves[:, 896:1024] = dot(pair[:, L:], wanted).astype(BF)

    for part in range(3):
        cos_a, sin_a = shift[0, part : part + 1], shift[0, 3 + part : 4 + part]
        rows = slice(L * part, L * part + L)
        comb[rows] = (cos_a * col_cos[...] - sin_a * col_sin[...]).astype(BF)
        rows = slice(WIDE + L * part, WIDE + L * part + L)
        comb[rows] = (-(sin_a * col_cos[...] + cos_a * col_sin[...])).astype(BF)
    pad = jnp.zeros((112, 128), F32)
    tail = jnp.zeros((8, 128), F32)
    comb[1152:1280] = jnp.concatenate([extra[0, :8], tail, pad], 0).astype(BF)
    comb[WIDE + 1152 : WIDE + 1280] = jnp.concatenate([extra[0, 8:], tail, pad], 0).astype(BF)

    row = iota((128, 128), 0)
    lane = iota((128, 128), 1)
    mine = (lane % 16) == (row % 16)
    field = lane // 16
    place = jnp.where(mine, 1.0, 0.0)
    w_x = jnp.where(field == 0, 128.0, jnp.where(field == 1, 1.0, 0.0)) * place
    w_y = jnp.where(field == 2, 128.0, jnp.where(field == 3, 1.0, 0.0)) * place
    w_t = jnp.where(field == 4, 1.0, 0.0) * place
    kept = (lane // 16) == (row % 8)
    lane_l = iota((128, L), 1).astype(F32)
    lane_t = lane.astype(F32)

    def chunk(q, carry):
        repeat = (iota((128, SLABS), 1) == 8 * q + iota((128, SLABS), 0) // 16).astype(BF)
        fields = dot(repeat, meta)
        ox = jnp.sum(fields * w_x, axis=1, keepdims=True)
        oy = jnp.sum(fields * w_y, axis=1, keepdims=True)
        choice = jnp.sum(fields * w_t, axis=1, keepdims=True)
        ref = dot((lane_t == choice).astype(BF), refs[...])
        wave_y = dot((lane_l == oy).astype(BF), waves[...])
        wave_x = lax.dot_general(
            (lane_l == ox).astype(BF), turn[0], (((1,), (1,)), ((), ())), preferred_element_type=F32
        )
        tile = tiles[pl.ds(pl.multiple_of(8 * q, 8), 8), :]
        total = jnp.zeros((128, 128), F32)
        for part in range(4):
            at = L * part
            size = L if part < 3 else 128
            tile_r = jnp.broadcast_to(tile[:, None, at : at + size], (8, 16, size)).reshape(128, size)
            tile_i = jnp.broadcast_to(
                tile[:, None, WIDE + at : WIDE + at + size], (8, 16, size)
            ).reshape(128, size)
            ref_r, ref_i = ref[:, at : at + size], ref[:, WIDE + at : WIDE + at + size]
            if part < 3:
                cos_y, sin_y = wave_y[:, :L], wave_y[:, L : 2 * L]
                cos_x, sin_x = wave_x[:, part : part + 1], wave_x[:, 3 + part : 4 + part]
                turn_r = cos_y * cos_x - sin_y * sin_x
                turn_i = sin_y * cos_x + cos_y * sin_x
            else:
                cos_x = wave_x[:, 6:7]
                turn_r = wave_y[:, 768:896] * cos_x
                turn_i = wave_y[:, 896:1024] * cos_x
            prod_r = tile_r * ref_r + tile_i * ref_i
            prod_i = tile_i * ref_r - tile_r * ref_i
            both_r = (prod_r * turn_r - prod_i * turn_i).astype(BF)
            both_i = (prod_r * turn_i + prod_i * turn_r).astype(BF)
            total += dot(both_r, comb[at : at + size])
            total += dot(both_i, comb[WIDE + at : WIDE + at + size])
        total = jnp.where(kept, total * (1.0 / (L * L)), 0.0)
        out[pl.ds(pl.multiple_of(16 * q, 16), 16), :] = jnp.sum(total.reshape(16, 8, 128), axis=1)
        return carry

    lax.fori_loop(0, 8, chunk, 0)


def refine(ids, own, other):
    by_slab = lambda i, ids: (ids[2], 0, 0)
    return pl.pallas_call(
        refine_kernel,
        out_shape=jax.ShapeDtypeStruct((128, 128), F32),
        grid_spec=pltpu.PrefetchScalarGridSpec(
            num_scalar_prefetch=1,
            grid=(1,),
            in_specs=[
                full_spec((SLABS, ROWS, 128)),
                full_spec((SLABS, ROWS, 128)),
                full_spec((L, 2 * L)),
                pl.BlockSpec((1, 16, L), by_slab),
                pl.BlockSpec((1, 8, 128), by_slab),
                pl.BlockSpec((1, 16, 128), by_slab),
                full_spec((L, 128)),
                full_spec((L, 128)),
            ],
            out_specs=full_spec((128, 128)),
            scratch_shapes=[
                pltpu.VMEM((SLABS * ROWS, 128), F32),
                pltpu.VMEM((SLABS, 2 * WIDE), F32),
                pltpu.VMEM((128, 2 * WIDE), BF),
                pltpu.VMEM((L, 1024), BF),
                pltpu.VMEM((2 * WIDE, 128), BF),
            ],
        ),
        compiler_params=pltpu.CompilerParams(vmem_limit_bytes=48 * MB),
        cost_estimate=pl.CostEstimate(flops=4_000_000_000, bytes_accessed=3 * MB, transcendentals=0),
        name="refine_slab",
    )(
        ids, own, other, TAB["pair"], TAB["turn"], TAB["shift"], TAB["extra"], TAB["col_cos"], TAB["col_sin"]
    )


def search_kernel(ids, spec, o0, o1, o2, o3, p0, p1, p2, p3, cols, rows, reverse, mip, zmap, prod, total, square):
    core = ids[1]
    mine = pl.ds(pl.multiple_of(core * Q, Q), Q)
    yours = pl.ds(pl.multiple_of((1 - core) * Q, Q), Q)
    index = [(own, oth, z) for own, oth in ((o0, p0), (o1, p1), (o2, p2), (o3, p3)) for z in range(2)]
    row16 = iota((16, L), 0)
    zero = jnp.zeros((16, L), F32)
    ends_r, ends_i = zero, zero
    for n, (own, oth, z) in enumerate(index):
        for ref, where in ((own, mine), (oth, yours)):
            tile_r, tile_i = spec[0, where, :].astype(F32), spec[1, where, :].astype(F32)
            t_r, t_i = ref[z, 0].astype(F32), ref[z, 1].astype(F32)
            prod[n, where, :L] = (tile_r * t_r + tile_i * t_i).astype(BF)
            prod[n, where, L:] = (tile_i * t_r - tile_r * t_i).astype(BF)
        top_r = jnp.where(core == 0, own[z, 0, :16].astype(F32), oth[z, 0, :16].astype(F32))
        top_i = jnp.where(core == 0, own[z, 1, :16].astype(F32), oth[z, 1, :16].astype(F32))
        ends_r = jnp.where(row16 == n, top_r[0:1], ends_r)
        ends_i = jnp.where(row16 == n, top_i[0:1], ends_i)
    ends_r = jnp.where(row16 == 8, spec[0, :16].astype(F32)[0:1], ends_r)
    ends_i = jnp.where(row16 == 8, spec[1, :16].astype(F32)[0:1], ends_i)
    back_r = dot(ends_r.astype(BF), reverse[...])
    back_i = dot(ends_i.astype(BF), reverse[...])
    low_r, low_i = 0.5 * (ends_r + back_r), 0.5 * (ends_i - back_i)
    top_r, top_i = -0.5 * (ends_i + back_i), 0.5 * (ends_r - back_r)

    def cross(a_r, a_i):
        s_r, s_i = a_r[8:9], a_i[8:9]
        return s_r * a_r + s_i * a_i, s_i * a_r - s_r * a_i

    low = cross(low_r, low_i)
    top = cross(top_r, top_i)
    line_r = low[0] - top[1]
    line_i = low[1] + top[0]
    for n in range(8):
        for at, line in ((0, line_r), (L, line_i)):
            old = prod[n, :16, at : at + L].astype(F32)
            prod[n, :16, at : at + L] = jnp.where(row16 == 0, line[n : n + 1], old).astype(BF)

    def step(pair, carry):
        both = []
        for k in range(2):
            middle = dot(prod[2 * pair + k], cols[...]).astype(BF)
            both.append(jnp.concatenate([middle[:, :L], middle[:, L:]], 0))
        corr = dot(rows[...], jnp.concatenate(both, 1)) * (1.0 / (L * L))
        one, two = corr[:, :L], corr[:, L:]
        largest = jnp.maximum(one, two)
        summed = one + two
        powers = one * one + two * two

        @pl.when(pair == 0)
        def _():
            mip[...] = largest
            total[...] = summed
            square[...] = powers

        @pl.when(pair > 0)
        def _():
            mip[...] = jnp.maximum(mip[...], largest)
            total[...] += summed
            square[...] += powers

        return carry

    lax.fori_loop(0, 4, step, 0)
    mean = total[...] * 0.125
    var = square[...] * 0.125 - mean * mean
    zmap[...] = (mip[...] - mean) * lax.rsqrt(jnp.maximum(var, 0.25))


def search(ids, spec, owns, others):
    piece = full_spec((2, 2, Q, L))
    return pl.pallas_call(
        search_kernel,
        out_shape=(jax.ShapeDtypeStruct((L, L), F32), jax.ShapeDtypeStruct((L, L), F32)),
        grid_spec=pltpu.PrefetchScalarGridSpec(
            num_scalar_prefetch=1,
            grid=(1,),
            in_specs=[full_spec((2, H, L))]
            + [piece] * 8
            + [full_spec((2 * L, 2 * L)), full_spec((L, L)), full_spec((L, L))],
            out_specs=[full_spec((L, L)), full_spec((L, L))],
            scratch_shapes=[
                pltpu.VMEM((8, H, 2 * L), BF),
                pltpu.VMEM((L, L), F32),
                pltpu.VMEM((L, L), F32),
            ],
        ),
        compiler_params=pltpu.CompilerParams(vmem_limit_bytes=48 * MB),
        cost_estimate=pl.CostEstimate(flops=4_000_000_000, bytes_accessed=6 * MB, transcendentals=0),
        name="search_templates",
    )(ids, spec, *owns, *others, TAB["inverse_cols"], TAB["inverse_rows"], TAB["reverse"])


def ring(count, step):
    return [(i, (i + step) % count) for i in range(count)]


def body(micrograph, templates, ref_bank, peak_offsets, peak_template, owners):
    blk = lax.axis_index(ROWS_OF)
    group = lax.axis_index(COLS_OF)
    core = lax.axis_index("core")
    ids = jnp.stack([blk, core, blk * 8 + group // 2]).astype(jnp.int32)
    owner = owners[:, 0]
    choice = peak_template * 8 + owner // 2 + 64 * ((owner % 2) ^ core)
    ox, oy = peak_offsets[:, 0], peak_offsets[:, 1]
    meta = jnp.concatenate([ox // 128, ox % 128, oy // 128, oy % 128, choice, jnp.zeros((48,), jnp.int32)])
    meta = meta.astype(F32).reshape(1, 128)

    def across(array):
        return lax.ppermute(array, "core", ring(2, 1))

    message, spec = make_spectra(ids, micrograph, ref_bank, meta)
    arrived = lax.all_to_all(message, CHIPS, 0, 0, tiled=True)
    half = template_half(ids, templates)
    near = lax.ppermute(half, "zl", ring(2, 1))
    both = jnp.stack([half, near])
    owns = [both] + [lax.ppermute(both, "y", ring(4, step)) for step in (1, 3, 2)]
    others = [across(one) for one in owns]
    scores = refine(ids, arrived, across(arrived))
    returned = lax.all_to_all(scores.reshape(SLABS, 2, 128), CHIPS, 0, 0, tiled=True)
    mip, zmap = search(ids, spec, owns, others)
    refined = jnp.sum(returned, 0).reshape(16, 16)[:, :9]
    return (mip, zmap, refined)


def solution(mesh):
    inner = Mesh(mesh.devices.reshape(2, 4, 4, 2, 2), ("zl", "y", "x", "zh", "core"))
    every = ROWS_OF + COLS_OF
    placed = (
        P(ROWS_OF, COLS_OF),
        P(ROWS_OF, None, None),
        P(COLS_OF, None, None),
        P(every, None),
        P(every),
        P(every, None),
    )
    return jax.shard_map(
        body,
        mesh=inner,
        in_specs=placed,
        out_specs=(P(ROWS_OF, COLS_OF), P(ROWS_OF, COLS_OF), P(every, None)),
        check_vma=False,
    )
```

profile of v0, /device:TPU:1, one launch (start us, length us, event | category | flops | bytes accessed | tf_op | source)
XLA Modules:
  0.0 90.0 jit_solution(3582621671620913818)
XLA Ops:
  0.6 0.8 fusion.1
  1.4 0.8 fusion.7
  2.4 1.7 %copy-done = bf16[8,384,384]{2,1,0:T(8,128)(2,1)S(1)} copy-done((bf16[8,384,384]{2,1,0:T(8,128)(2,1)S(1)}, bf16[8,384,384]{2,1,0:T(8,128)(2,1)}, u32[]{:S(2)}) %copy-start) | copy-done | bytes 2359320
  4.1 1.1 %copy-done.1 = bf16[384,768]{1,0:T(8,128)(2,1)S(1)} copy-done((bf16[384,768]{1,0:T(8,128)(2,1)S(1)}, bf16[384,768]{1,0:T(8,128)(2,1)}, u32[]{:S(2)}) %copy-start.1) | copy-done | bytes 589848
  5.1 1.0 %copy-done.3 = bf16[1536,128]{1,0:T(8,128)(2,1)S(1)} copy-done((bf16[1536,128]{1,0:T(8,128)(2,1)S(1)}, bf16[1536,128]{1,0:T(8,128)(2,1)}, u32[]{:S(2)}) %copy-start.3) | copy-done | bytes 393240
  6.1 1.0 %copy-done.4 = bf16[384,384]{1,0:T(8,128)(2,1)S(1)} copy-done((bf16[384,384]{1,0:T(8,128)(2,1)S(1)}, bf16[384,384]{1,0:T(8,128)(2,1)}, u32[]{:S(2)}) %copy-start.4) | copy-done | bytes 294936
  7.1 1.0 %copy-done.5 = bf16[384,384]{1,0:T(8,128)(2,1)S(1)} copy-done((bf16[384,384]{1,0:T(8,128)(2,1)S(1)}, bf16[384,384]{1,0:T(8,128)(2,1)}, u32[]{:S(2)}) %copy-start.5) | copy-done | bytes 294936
  8.0 2.0 %tile_spectra.1 = (bf16[64,40,128]{2,1,0:T(8,128)(2,1)S(1)}, bf16[2,192,384]{2,1,0:T(8,128)(2,1)S(1)}) custom-call(s32[3]{0:T(128)S(1)} %pad_add_fusion.ids, bf16[384,384]{1,0:T(8,128)(2,1)S(1)} %copy-done.4, bf16[8,384,384]{2,1,0:T(8,128)(2,1)S(1)} %copy-done, f32[1,128]{1,0:T(1,128)S(1)} %convert_element_type.10.meta, bf16[384,384]{1,0:T(8,128)(2,1)S(1)} %copy-done.5, ...), custom_call_target="tpu_custom_call" | custom-call | flops 800000000 | bytes 3145728 | tf_op jit(solution)/shard_map/tile_spectra/pallas_call | solution.py:135
  10.1 24.7 %all_to_all.10.own = bf16[64,40,128]{2,1,0:T(8,128)(2,1)S(1)} all-to-all(bf16[64,40,128]{2,1,0:T(8,128)(2,1)S(1)} %get-tuple-element.10), channel_id=1, replica_groups=mesh['zl'=2,'y'=4,'x'=4,'zh'=2,'core'=2] {'zl','y','x','zh'}, dimensions={0} | all-to-all | bytes 1310720 | tf_op jit(solution)/shard_map/all_to_all | solution.py:440
  34.8 2.6 %collective-permute-start.8 = (bf16[64,40,128]{2,1,0:T(8,128)(2,1)S(1)}, bf16[64,40,128]{2,1,0:T(8,128)(2,1)S(1)}, u32[]{:S(2)}, u32[]{:S(2)}) collective-permute-start(bf16[64,40,128]{2,1,0:T(8,128)(2,1)S(1)} %all_to_all.10.own), channel_id=1, source_target_pairs={{0,1},{1,0},{2,3},{3,2},{4,5},{5,4},{6,7},{7,6},{8,9},{9,8},{10,11... | collective-permute-start | bytes 1966088 | tf_op jit(solution)/shard_map/ppermute | solution.py:437
  37.4 1.6 %template_spectrum.1 = bf16[2,96,384]{2,1,0:T(8,128)(2,1)S(1)} custom-call(s32[3]{0:T(128)S(1)} %pad_add_fusion.ids, bf16[1,384,384]{2,1,0:T(8,128)(2,1)S(1)} %copy-done.6, bf16[2,192,384]{2,1,0:T(8,128)(2,1)S(1)} %copy-done.7, bf16[384,768]{1,0:T(8,128)(2,1)S(1)} %copy-done.1), custom_call_target="tpu_custom_call" | custom-call | flops 200000000 | bytes 2097152 | tf_op jit(solution)/shard_map/template_spectrum/pallas_call | solution.py:176
  39.7 5.0 %collective-permute-done = bf16[2,96,384]{2,1,0:T(8,128)(2,1)S(1)} collective-permute-done((bf16[2,96,384]{2,1,0:T(8,128)(2,1)S(1)}, bf16[2,96,384]{2,1,0:T(8,128)(2,1)S(1)}, u32[]{:S(2)}, u32[]{:S(2)}) %collective-permute-start) | collective-permute-done | bytes 147488 | tf_op jit(solution)/shard_map/ppermute | solution.py:442
  44.7 1.3 %collective-permute-start.3 = (bf16[2,2,96,384]{3,2,1,0:T(8,128)(2,1)S(1)}, bf16[2,2,96,384]{3,2,1,0:T(8,128)(2,1)S(1)}, u32[]{:S(2)}, u32[]{:S(2)}) collective-permute-start(bf16[2,2,96,384]{3,2,1,0:T(8,128)(2,1)S(1)} %pad_maximum_fusion.o0), channel_id=1, source_target_pairs={{0,32},{16,48},{32,0},{48,16},{1,33},{17,49},{33,1},{49,17},{2,34}... | collective-permute-start | bytes 884744 | tf_op jit(solution)/shard_map/ppermute | solution.py:444
  46.0 1.5 %collective-permute-start.2 = (bf16[2,2,96,384]{3,2,1,0:T(8,128)(2,1)S(1)}, bf16[2,2,96,384]{3,2,1,0:T(8,128)(2,1)S(1)}, u32[]{:S(2)}, u32[]{:S(2)}) collective-permute-start(bf16[2,2,96,384]{3,2,1,0:T(8,128)(2,1)S(1)} %pad_maximum_fusion.o0), channel_id=1, source_target_pairs={{0,48},{16,0},{32,16},{48,32},{1,49},{17,1},{33,17},{49,33},{2,50}... | collective-permute-start | bytes 884744 | tf_op jit(solution)/shard_map/ppermute | solution.py:444
  47.5 1.6 %collective-permute-start.4 = (bf16[2,2,96,384]{3,2,1,0:T(8,128)(2,1)S(1)}, bf16[2,2,96,384]{3,2,1,0:T(8,128)(2,1)S(1)}, u32[]{:S(2)}, u32[]{:S(2)}) collective-permute-start(bf16[2,2,96,384]{3,2,1,0:T(8,128)(2,1)S(1)} %pad_maximum_fusion.o0), channel_id=1, source_target_pairs={{0,1},{1,0},{2,3},{3,2},{4,5},{5,4},{6,7},{7,6},{8,9},{9,8},{10,11... | collective-permute-start | bytes 884744 | tf_op jit(solution)/shard_map/ppermute | solution.py:437
  49.1 5.0 %collective-permute-done.3.o3 = bf16[2,2,96,384]{3,2,1,0:T(8,128)(2,1)S(1)} collective-permute-done((bf16[2,2,96,384]{3,2,1,0:T(8,128)(2,1)S(1)}, bf16[2,2,96,384]{3,2,1,0:T(8,128)(2,1)S(1)}, u32[]{:S(2)}, u32[]{:S(2)}) %collective-permute-start.3) | collective-permute-done | bytes 294944 | tf_op jit(solution)/shard_map/ppermute | solution.py:444
  54.1 3.0 %collective-permute-start.7 = (bf16[2,2,96,384]{3,2,1,0:T(8,128)(2,1)S(1)}, bf16[2,2,96,384]{3,2,1,0:T(8,128)(2,1)S(1)}, u32[]{:S(2)}, u32[]{:S(2)}) collective-permute-start(bf16[2,2,96,384]{3,2,1,0:T(8,128)(2,1)S(1)} %collective-permute-done.3.o3), channel_id=1, source_target_pairs={{0,1},{1,0},{2,3},{3,2},{4,5},{5,4},{6,7},{7,6},{8,9},{9,8},{10,11... | collective-permute-start | bytes 884744 | tf_op jit(solution)/shard_map/ppermute | solution.py:437
  57.0 1.9 %collective-permute-done.2.o2 = bf16[2,2,96,384]{3,2,1,0:T(8,128)(2,1)S(1)} collective-permute-done((bf16[2,2,96,384]{3,2,1,0:T(8,128)(2,1)S(1)}, bf16[2,2,96,384]{3,2,1,0:T(8,128)(2,1)S(1)}, u32[]{:S(2)}, u32[]{:S(2)}) %collective-permute-start.2) | collective-permute-done | bytes 294944 | tf_op jit(solution)/shard_map/ppermute | solution.py:444
  58.9 1.6 %collective-permute-start.6 = (bf16[2,2,96,384]{3,2,1,0:T(8,128)(2,1)S(1)}, bf16[2,2,96,384]{3,2,1,0:T(8,128)(2,1)S(1)}, u32[]{:S(2)}, u32[]{:S(2)}) collective-permute-start(bf16[2,2,96,384]{3,2,1,0:T(8,128)(2,1)S(1)} %collective-permute-done.2.o2), channel_id=1, source_target_pairs={{0,1},{1,0},{2,3},{3,2},{4,5},{5,4},{6,7},{7,6},{8,9},{9,8},{10,11... | collective-permute-start | bytes 884744 | tf_op jit(solution)/shard_map/ppermute | solution.py:437
  60.4 1.1 %collective-permute-done.1.o1 = bf16[2,2,96,384]{3,2,1,0:T(8,128)(2,1)S(1)} collective-permute-done((bf16[2,2,96,384]{3,2,1,0:T(8,128)(2,1)S(1)}, bf16[2,2,96,384]{3,2,1,0:T(8,128)(2,1)S(1)}, u32[]{:S(2)}, u32[]{:S(2)}) %collective-permute-start.1) | collective-permute-done | bytes 294944 | tf_op jit(solution)/shard_map/ppermute | solution.py:444
  62.1 13.0 %refine_slab.1 = f32[128,128]{1,0:T(8,128)} custom-call(s32[3]{0:T(128)S(1)} %pad_add_fusion.ids, bf16[64,40,128]{2,1,0:T(8,128)(2,1)S(1)} %all_to_all.10.own, bf16[64,40,128]{2,1,0:T(8,128)(2,1)S(1)} %collective-permute-done.8.other, bf16[384,768]{1,0:T(8,128)(2,1)S(1)} %copy-done.2, bf16[64,16,384]{2,1,0:T(8,128)(2,1)S(1)} %copy-done.9, ...), custom_call_target="tpu_custom_call" | custom-call | flops 4000000000 | bytes 3145728 | tf_op jit(solution)/shard_map/refine_slab/pallas_call | solution.py:295
  75.1 4.8 %all-to-all-start.1 = ((f32[64,2,128]{2,1,0:T(2,128)}), f32[64,2,128]{2,1,0:T(2,128)S(1)}, u32[]{:S(2)}, u32[]{:S(2)}) async-start(f32[64,2,128]{2,1,0:T(2,128)} %bitcast.13), calls=%async_computation.1 | async-start | bytes 131072 | tf_op jit(solution)/shard_map/all_to_all | solution.py:447
  80.0 1.3 %copy-done.8 = bf16[768,768]{1,0:T(8,128)(2,1)S(1)} copy-done((bf16[768,768]{1,0:T(8,128)(2,1)S(1)}, bf16[768,768]{1,0:T(8,128)(2,1)}, u32[]{:S(2)}) %copy-start.8) | copy-done | bytes 1179672
  81.2 8.0 %search_templates.1 = (f32[384,384]{1,0:T(8,128)}, f32[384,384]{1,0:T(8,128)}) custom-call(s32[3]{0:T(128)S(1)} %pad_add_fusion.ids, bf16[2,192,384]{2,1,0:T(8,128)(2,1)S(1)} %get-tuple-element.7.spec, bf16[2,2,96,384]{3,2,1,0:T(8,128)(2,1)S(1)} %pad_maximum_fusion.o0, bf16[2,2,96,384]{3,2,1,0:T(8,128)(2,1)S(1)} %collective-permute-done.1.o1, ...), custom_call_target="tpu_custom_call" | custom-call | flops 4000000000 | bytes 6291456 | tf_op jit(solution)/shard_map/search_templates/pallas_call | solution.py:399
  (42 shorter events, 2.2 us)
Async XLA Ops:
  2.4 1.7 %copy-start = (bf16[8,384,384]{2,1,0:T(8,128)(2,1)S(1)}, bf16[8,384,384]{2,1,0:T(8,128)(2,1)}, u32[]{:S(2)}) copy-start(bf16[8,384,384]{2,1,0:T(8,128)(2,1)} %ref.1) | copy-start | bytes 7077892
  4.0 1.1 %copy-start.1 = (bf16[384,768]{1,0:T(8,128)(2,1)S(1)}, bf16[384,768]{1,0:T(8,128)(2,1)}, u32[]{:S(2)}) copy-start(bf16[384,768]{1,0:T(8,128)(2,1)} %constant.121.clone.pair) | copy-start | bytes 1769476
  5.1 1.0 %copy-start.3 = (bf16[1536,128]{1,0:T(8,128)(2,1)S(1)}, bf16[1536,128]{1,0:T(8,128)(2,1)}, u32[]{:S(2)}) copy-start(bf16[1536,128]{1,0:T(8,128)(2,1)} %constant.122.clone.pick) | copy-start | bytes 1179652
  8.0 29.4 %copy-start.6 = (bf16[1,384,384]{2,1,0:T(8,128)(2,1)S(1)}, bf16[1,384,384]{2,1,0:T(8,128)(2,1)}, u32[]{:S(2)}) copy-start(bf16[1,384,384]{2,1,0:T(8,128)(2,1)} %template.1) | copy-start | bytes 884740
  8.0 29.4 %copy-start.7 = (bf16[2,192,384]{2,1,0:T(8,128)(2,1)S(1)}, bf16[2,192,384]{2,1,0:T(8,128)(2,1)}, u32[]{:S(2)}) copy-start(bf16[2,192,384]{2,1,0:T(8,128)(2,1)} %constant.123.clone.halves) | copy-start | bytes 884740
  10.0 52.0 %copy-start.2 = (bf16[384,768]{1,0:T(8,128)(2,1)S(1)}, bf16[384,768]{1,0:T(8,128)(2,1)}, u32[]{:S(2)}) copy-start(bf16[384,768]{1,0:T(8,128)(2,1)} %constant.121.clone.pair) | copy-start | bytes 1769476
  10.0 52.0 %copy-start.9 = (bf16[64,16,384]{2,1,0:T(8,128)(2,1)S(1)}, bf16[64,16,384]{2,1,0:T(8,128)(2,1)}, u32[]{:S(2)}) copy-start(bf16[64,16,384]{2,1,0:T(8,128)(2,1)} %constant.124.clone.turn) | copy-start | bytes 2359300
  10.0 52.0 %copy-start.10 = (f32[64,16,128]{2,1,0:T(8,128)S(1)}, f32[64,16,128]{2,1,0:T(8,128)}, u32[]{:S(2)}) copy-start(f32[64,16,128]{2,1,0:T(8,128)} %constant.126.clone.extra) | copy-start | bytes 1572868
  10.1 52.0 %copy-start.13 = (f32[64,8,128]{2,1,0:T(8,128)S(1)}, f32[64,8,128]{2,1,0:T(8,128)}, u32[]{:S(2)}) copy-start(f32[64,8,128]{2,1,0:T(8,128)} %constant.125.clone.shift) | copy-start | bytes 786436
  10.1 52.0 %copy-start.14 = (f32[384,128]{1,0:T(8,128)S(1)}, f32[384,128]{1,0:T(8,128)}, u32[]{:S(2)}) copy-start(f32[384,128]{1,0:T(8,128)} %constant.128.clone.col_sin) | copy-start | bytes 589828
  10.1 52.0 %copy-start.15 = (f32[384,128]{1,0:T(8,128)S(1)}, f32[384,128]{1,0:T(8,128)}, u32[]{:S(2)}) copy-start(f32[384,128]{1,0:T(8,128)} %constant.127.clone.col_cos) | copy-start | bytes 589828
  34.8 27.2 %collective-permute-start.8 = (bf16[64,40,128]{2,1,0:T(8,128)(2,1)S(1)}, bf16[64,40,128]{2,1,0:T(8,128)(2,1)S(1)}, u32[]{:S(2)}, u32[]{:S(2)}) collective-permute-start(bf16[64,40,128]{2,1,0:T(8,128)(2,1)S(1)} %all_to_all.10.own), channel_id=1, source_target_pairs={{0,1},{1,0},{2,3},{3,2},{4,5},{5,4},{6,7},{7,6},{8,9},{9,8},{10,11... | collective-permute-start | bytes 1966088 | tf_op jit(solution)/shard_map/ppermute | solution.py:437
  39.1 5.6 %collective-permute-start = (bf16[2,96,384]{2,1,0:T(8,128)(2,1)S(1)}, bf16[2,96,384]{2,1,0:T(8,128)(2,1)S(1)}, u32[]{:S(2)}, u32[]{:S(2)}) collective-permute-start(bf16[2,96,384]{2,1,0:T(8,128)(2,1)S(1)} %template_spectrum.1), channel_id=1, source_target_pairs={{0,64},{64,0},{1,65},{65,1},{2,66},{66,2},{3,67},{67,3},{4,68},{68... | collective-permute-start | bytes 442376 | tf_op jit(solution)/shard_map/ppermute | solution.py:442
  44.7 35.3 %copy-start.11 = (bf16[384,384]{1,0:T(8,128)(2,1)S(1)}, bf16[384,384]{1,0:T(8,128)(2,1)}, u32[]{:S(2)}) copy-start(bf16[384,384]{1,0:T(8,128)(2,1)} %constant.131.clone.reverse) | copy-start | bytes 884740
  44.7 35.3 %copy-start.12 = (bf16[384,384]{1,0:T(8,128)(2,1)S(1)}, bf16[384,384]{1,0:T(8,128)(2,1)}, u32[]{:S(2)}) copy-start(bf16[384,384]{1,0:T(8,128)(2,1)} %constant.130.clone.rows) | copy-start | bytes 884740
  44.7 9.4 %collective-permute-start.3 = (bf16[2,2,96,384]{3,2,1,0:T(8,128)(2,1)S(1)}, bf16[2,2,96,384]{3,2,1,0:T(8,128)(2,1)S(1)}, u32[]{:S(2)}, u32[]{:S(2)}) collective-permute-start(bf16[2,2,96,384]{3,2,1,0:T(8,128)(2,1)S(1)} %pad_maximum_fusion.o0), channel_id=1, source_target_pairs={{0,32},{16,48},{32,0},{48,16},{1,33},{17,49},{33,1},{49,17},{2,34}... | collective-permute-start | bytes 884744 | tf_op jit(solution)/shard_map/ppermute | solution.py:444
  46.0 12.9 %collective-permute-start.2 = (bf16[2,2,96,384]{3,2,1,0:T(8,128)(2,1)S(1)}, bf16[2,2,96,384]{3,2,1,0:T(8,128)(2,1)S(1)}, u32[]{:S(2)}, u32[]{:S(2)}) collective-permute-start(bf16[2,2,96,384]{3,2,1,0:T(8,128)(2,1)S(1)} %pad_maximum_fusion.o0), channel_id=1, source_target_pairs={{0,48},{16,0},{32,16},{48,32},{1,49},{17,1},{33,17},{49,33},{2,50}... | collective-permute-start | bytes 884744 | tf_op jit(solution)/shard_map/ppermute | solution.py:444
  47.5 14.0 %collective-permute-start.1 = (bf16[2,2,96,384]{3,2,1,0:T(8,128)(2,1)S(1)}, bf16[2,2,96,384]{3,2,1,0:T(8,128)(2,1)S(1)}, u32[]{:S(2)}, u32[]{:S(2)}) collective-permute-start(bf16[2,2,96,384]{3,2,1,0:T(8,128)(2,1)S(1)} %pad_maximum_fusion.o0), channel_id=1, source_target_pairs={{0,16},{16,32},{32,48},{48,0},{1,17},{17,33},{33,49},{49,1},{2,18}... | collective-permute-start | bytes 884744 | tf_op jit(solution)/shard_map/ppermute | solution.py:444
  47.5 32.4 %collective-permute-start.4 = (bf16[2,2,96,384]{3,2,1,0:T(8,128)(2,1)S(1)}, bf16[2,2,96,384]{3,2,1,0:T(8,128)(2,1)S(1)}, u32[]{:S(2)}, u32[]{:S(2)}) collective-permute-start(bf16[2,2,96,384]{3,2,1,0:T(8,128)(2,1)S(1)} %pad_maximum_fusion.o0), channel_id=1, source_target_pairs={{0,1},{1,0},{2,3},{3,2},{4,5},{5,4},{6,7},{7,6},{8,9},{9,8},{10,11... | collective-permute-start | bytes 884744 | tf_op jit(solution)/shard_map/ppermute | solution.py:437
  54.1 25.9 %collective-permute-start.7 = (bf16[2,2,96,384]{3,2,1,0:T(8,128)(2,1)S(1)}, bf16[2,2,96,384]{3,2,1,0:T(8,128)(2,1)S(1)}, u32[]{:S(2)}, u32[]{:S(2)}) collective-permute-start(bf16[2,2,96,384]{3,2,1,0:T(8,128)(2,1)S(1)} %collective-permute-done.3.o3), channel_id=1, source_target_pairs={{0,1},{1,0},{2,3},{3,2},{4,5},{5,4},{6,7},{7,6},{8,9},{9,8},{10,11... | collective-permute-start | bytes 884744 | tf_op jit(solution)/shard_map/ppermute | solution.py:437
  58.9 21.0 %collective-permute-start.6 = (bf16[2,2,96,384]{3,2,1,0:T(8,128)(2,1)S(1)}, bf16[2,2,96,384]{3,2,1,0:T(8,128)(2,1)S(1)}, u32[]{:S(2)}, u32[]{:S(2)}) collective-permute-start(bf16[2,2,96,384]{3,2,1,0:T(8,128)(2,1)S(1)} %collective-permute-done.2.o2), channel_id=1, source_target_pairs={{0,1},{1,0},{2,3},{3,2},{4,5},{5,4},{6,7},{7,6},{8,9},{9,8},{10,11... | collective-permute-start | bytes 884744 | tf_op jit(solution)/shard_map/ppermute | solution.py:437
  61.5 18.4 %collective-permute-start.5 = (bf16[2,2,96,384]{3,2,1,0:T(8,128)(2,1)S(1)}, bf16[2,2,96,384]{3,2,1,0:T(8,128)(2,1)S(1)}, u32[]{:S(2)}, u32[]{:S(2)}) collective-permute-start(bf16[2,2,96,384]{3,2,1,0:T(8,128)(2,1)S(1)} %collective-permute-done.1.o1), channel_id=1, source_target_pairs={{0,1},{1,0},{2,3},{3,2},{4,5},{5,4},{6,7},{7,6},{8,9},{9,8},{10,11... | collective-permute-start | bytes 884744 | tf_op jit(solution)/shard_map/ppermute | solution.py:437
  75.1 14.1 %all-to-all-start.1 = ((f32[64,2,128]{2,1,0:T(2,128)}), f32[64,2,128]{2,1,0:T(2,128)S(1)}, u32[]{:S(2)}, u32[]{:S(2)}) async-start(f32[64,2,128]{2,1,0:T(2,128)} %bitcast.13), calls=%async_computation.1 | async-start | bytes 131072 | tf_op jit(solution)/shard_map/all_to_all | solution.py:447
  80.0 1.3 %copy-start.8 = (bf16[768,768]{1,0:T(8,128)(2,1)S(1)}, bf16[768,768]{1,0:T(8,128)(2,1)}, u32[]{:S(2)}) copy-start(bf16[768,768]{1,0:T(8,128)(2,1)} %constant.129.clone.cols) | copy-start | bytes 3538948
  (2 other events, 1.9 us)
where the time goes:
time: 90.4 us; the launch traced here: 90 us
  blocking collectives  24.7 us (27%)
  Pallas kernels  24.6 us (27%)
  starting transfers between devices  17.3 us (19%)
  waiting for transfers between devices  12.9 us (14%)
  local copies, waits for them, and re-layouts  7.76 us (9%)
  other arithmetic  1.73 us (2%)
    all_to_all x1, blocking collectives, body(): arrived = lax.all_to_all(message, CHIPS, 0, 0, tiled=True)  24.7 us
    pallas_call x1, Pallas kernels, refine(): pl.pallas_call(refine_kernel, out_shape=jax.ShapeDtypeStruct((128, 128),...  13 us
    ppermute x5, starting transfers between devices, across(): return lax.ppermute(array, 'core', ring(2, 1))  9.11 us
    pallas_call x1, Pallas kernels, search(): pl.pallas_call(search_kernel, out_shape=(jax.ShapeDtypeStruct((L, L), F32...  7.98 us
    ppermute x3, waiting for transfers between devices, body(): lax.ppermute(both, 'y', ring(4, step))  7.95 us
    unnamed x32, local copies, waits for them, and re-layouts  6.98 us
    ppermute x1, waiting for transfers between devices, body(): near = lax.ppermute(half, 'zl', ring(2, 1))  4.97 us
    all_to_all x1, starting transfers between devices, body(): lax.all_to_all(scores.reshape(SLABS, 2, 128), CHIPS, 0, 0, tiled=True)  4.8 us
  transfers between devices with their start and end apart: 10, of which 4 were waited for; matrix products, arithmetic and copies ran while one was open for 0% of the time, Pallas kernels for 25%

commit v1 on v0

v1 whole, which is shorter than its diff:
```python
import math

import jax
import jax.numpy as jnp
import numpy as np
from jax import lax
from jax.experimental import pallas as pl
from jax.experimental.pallas import tpu as pltpu
from jax.sharding import Mesh
from jax.sharding import PartitionSpec as P

L = 384
H = 192
Q = 96
SLABS = 64
ROWS = 40
WIDE = 1280
BF = jnp.bfloat16
F32 = jnp.float32
MB = 1024 * 1024
ROWS_OF = ("zl", "y")
COLS_OF = ("x", "zh", "core")
CHIPS = ("zl", "y", "x", "zh")


def dot(a, b):
    return jnp.dot(a, b, preferred_element_type=F32)


def wave(a, b):
    angle = (np.multiply.outer(np.asarray(a), np.asarray(b)) % L) * (2.0 * math.pi / L)
    return np.cos(angle), np.sin(angle)


def bf(a):
    return np.asarray(a, np.float32).astype(jnp.bfloat16)


def make_tables():
    n = np.arange(L)
    cos, sin = wave(n, n)
    forward = np.concatenate([cos[:H], cos[H : H + 1], sin[1:H]], 0)
    halves = np.stack(
        [np.concatenate([forward[c * Q : c * Q + Q], forward[H + c * Q : H + c * Q + Q]], 0) for c in range(2)]
    )
    pair = np.concatenate([cos, sin], 1)
    inverse_cols = np.concatenate([pair, np.concatenate([-sin, cos], 1)], 0)
    weight = np.full((H,), 2.0)
    weight[0] = 1.0
    inverse_rows = np.concatenate([cos[:, :H] * weight, -2.0 * sin[:, :H]], 1)
    inverse_rows[:, H] = cos[:, H]
    reverse = np.zeros((L, L))
    reverse[(-n) % L, n] = 1.0
    pick = np.zeros((4, L, 128))
    for part in range(4):
        pick[part, n, 80 + 6 * part + n % 6] = 1.0
    lane = np.arange(128)
    field = np.zeros((128, 3, 128))
    for which, at in enumerate((0, 32, 64)):
        if which < 2:
            field[at : at + 16, which] = 128.0
            at += 16
        field[at : at + 16, which] = 1.0
    ac = lane % 16
    a, c = ac // 3 - 1, ac % 3 - 1
    comb = np.zeros((2, 3, L, 128))
    extra = np.zeros((SLABS, 2, 8, 128))
    for shift in (-1, 0, 1):
        kc, ks = wave(n, [shift])
        for part in range(4):
            at = 6 * part + 2 * (shift + 1)
            if part < 3:
                comb[0, part, :, at], comb[0, part, :, at + 1] = kc[:, 0], ks[:, 0]
                comb[1, part, :, at], comb[1, part, :, at + 1] = -ks[:, 0], kc[:, 0]
            else:
                kc, ks = kc[:, 0].reshape(SLABS, 6), ks[:, 0].reshape(SLABS, 6)
                extra[:, 0, :6, at], extra[:, 0, :6, at + 1] = kc, ks
                extra[:, 1, :6, at], extra[:, 1, :6, at + 1] = -ks, kc
    turn = np.zeros((SLABS, 16, L))
    widen = np.zeros((256, 16))
    last = np.zeros((SLABS, 2, 128, 128))
    for part in range(4):
        widen[6 * part : 6 * part + 6, part] = 1.0
        widen[128 + 6 * part : 128 + 6 * part + 6, 4 + part] = 1.0
    for s in range(SLABS):
        for part in range(4):
            k = s + 64 * part if part < 3 else H
            kc, ks = wave([k], n)
            turn[s, part], turn[s, 4 + part] = kc[0], ks[0]
            ca, sa = wave([k], a)
            w = 1.0 if k in (0, H) else 2.0
            for shift in (-1, 0, 1):
                at = 6 * part + 2 * (shift + 1)
                on = w * ((ac < 9) & (c == shift))
                last[s, 0, at], last[s, 0, at + 1] = on * ca[0], -on * sa[0]
                last[s, 1, at], last[s, 1, at + 1] = -on * sa[0], -on * ca[0]
    return dict(
        forward=bf(forward),
        halves=bf(halves),
        pair=bf(pair),
        inverse_cols=bf(inverse_cols),
        inverse_rows=bf(inverse_rows),
        reverse=bf(reverse),
        pick=bf(pick.reshape(4 * L, 128)),
        field=bf(field.reshape(128, 384)),
        comb=bf(comb.reshape(6 * L, 128)),
        extra=bf(extra.reshape(SLABS, 16, 128)),
        turn=bf(turn),
        widen=bf(widen),
        last=bf(last.reshape(SLABS, 256, 128)),
    )


TAB = make_tables()


def full_spec(shape):
    zeros = (0,) * len(shape)
    return pl.BlockSpec(shape, lambda i, ids: zeros)


def iota(shape, dim):
    return lax.broadcasted_iota(jnp.int32, shape, dim)


def prepare_kernel(
    ids,
    offsets,
    choice,
    owners,
    tile_hbm,
    template_hbm,
    bank_hbm,
    forward_hbm,
    pair_hbm,
    halves_hbm,
    pick_hbm,
    msg,
    spec,
    half,
    flat,
    tile,
    template,
    ref,
    forward,
    pair,
    rows_half,
    pick,
    sems,
):
    blk, core = ids[0], ids[1]
    jobs = (
        (forward_hbm, forward),
        (tile_hbm, tile),
        (pair_hbm, pair),
        (bank_hbm.at[blk], ref),
        (pick_hbm, pick),
        (template_hbm.at[0], template),
        (halves_hbm.at[core], rows_half),
    )
    copies = [pltpu.make_async_copy(src, dst, sems.at[n]) for n, (src, dst) in enumerate(jobs)]
    for copy in copies:
        copy.start()

    r8 = iota((8, 16), 0)
    ox, oy = offsets[0:1], offsets[1:2]
    owner = owners[...]
    named = choice[...] * 8 + (owner >> 1) + 64 * ((owner & 1) ^ core)
    values = jnp.where(r8 == 4, named, 0)
    for n, value in enumerate((ox >> 7, ox & 127, oy >> 7, oy & 127)):
        values = jnp.where(r8 == n, value, values)
    wide = ((iota((16, 128), 1) & 15) == iota((16, 128), 0)).astype(BF)
    lined = dot(values.astype(F32).astype(BF), wide)
    lined = jnp.where((iota((8, 128), 1) >> 4) == iota((8, 128), 0), lined, 0.0)
    meta = jnp.sum(lined, axis=0, keepdims=True)

    rows64 = iota((SLABS, L), 0)
    owned = (iota((SLABS, L), 1) // 6) == rows64
    first_row = rows64 == 0
    for row in range(37, ROWS):
        flat[pl.ds(row, SLABS, stride=ROWS), :] = jnp.zeros((SLABS, 128), F32)
    copies[0].wait()
    lasts = []
    for which, image in enumerate((tile, ref)):
        copies[1 + 2 * which].wait()
        first = dot(forward[...], image[...]).astype(BF)
        if which == 0:
            copies[2].wait()
        second = dot(first, pair[...])
        real = second[:H, :L] - second[H:, L:]
        imag = -(second[:H, L:] + second[H:, :L])
        if which == 0:
            spec[0] = real.astype(BF)
            spec[1] = imag.astype(BF)
        for plane, (full, alone) in enumerate(((real, second[:64, :L]), (imag, -second[:64, L:]))):
            for part in range(3):
                block = full[64 * part : 64 * part + 64]
                if part == 0:
                    block = jnp.where(first_row, alone, block)
                for j in range(3):
                    row = 18 * which + 9 * plane + 3 * part + j
                    flat[pl.ds(row, SLABS, stride=ROWS), :] = block[:, 128 * j : 128 * j + 128]
        for last in (second[H : H + 1, :L], -second[H : H + 1, L:]):
            lasts.append(jnp.where(owned, jnp.broadcast_to(last, (SLABS, L)), 0.0).astype(BF))
    copies[4].wait()
    line = dot(jnp.concatenate(lasts, 1), pick[...])
    flat[pl.ds(36, SLABS, stride=ROWS), :] = line + meta
    msg[...] = flat[...].reshape(SLABS, ROWS, 128).astype(BF)

    copies[5].wait()
    copies[6].wait()
    values = template[...].astype(F32)
    count = 1.0 / (L * L)
    spread = values - jnp.sum(values) * count
    power = jnp.sum(spread * spread) * count
    scale = 1.0 / (L * jnp.sqrt(jnp.full((1, 1), power + 1e-06, F32)))
    normalized = (spread * scale).astype(BF)
    first = dot(rows_half[...], normalized).astype(BF)
    second = dot(first, pair[...])
    real = (second[:Q, :L] - second[Q:, L:]).astype(BF)
    imag = (-(second[:Q, L:] + second[Q:, :L])).astype(BF)
    for n in range(8):
        half[n, 0] = real
        half[n, 1] = imag


def prepare(ids, offsets, choice, owners, tile, templates, bank):
    held = pl.BlockSpec(memory_space=pltpu.HBM)
    return pl.pallas_call(
        prepare_kernel,
        out_shape=(
            jax.ShapeDtypeStruct((SLABS, ROWS, 128), BF),
            jax.ShapeDtypeStruct((2, H, L), BF),
            jax.ShapeDtypeStruct((8, 2, Q, L), BF),
        ),
        grid_spec=pltpu.PrefetchScalarGridSpec(
            num_scalar_prefetch=1,
            grid=(1,),
            in_specs=[full_spec((2, 16)), full_spec((1, 16)), full_spec((1, 16))] + [held] * 7,
            out_specs=[full_spec((SLABS, ROWS, 128)), full_spec((2, H, L)), full_spec((8, 2, Q, L))],
            scratch_shapes=[
                pltpu.VMEM((SLABS * ROWS, 128), F32),
                pltpu.VMEM((L, L), BF),
                pltpu.VMEM((L, L), BF),
                pltpu.VMEM((L, L), BF),
                pltpu.VMEM((L, L), BF),
                pltpu.VMEM((L, 2 * L), BF),
                pltpu.VMEM((H, L), BF),
                pltpu.VMEM((4 * L, 128), BF),
                pltpu.SemaphoreType.DMA((7,)),
            ],
        ),
        compiler_params=pltpu.CompilerParams(vmem_limit_bytes=62 * MB),
        cost_estimate=pl.CostEstimate(flops=1_000_000_000, bytes_accessed=4 * MB, transcendentals=0),
        name="prepare_spectra",
    )(
        ids, offsets, choice, owners, tile, templates, bank,
        TAB["forward"], TAB["pair"], TAB["halves"], TAB["pick"],
    )


MAIN = 6 * L
N_CAND = 1024


def refine_kernel(
    own, other, pair, field, comb, widen, turn, extra, last, slab_ref, out,
    flat, tiles, refs, waves, ref_of, wave_of, both, turned,
):
    slab = slab_ref[2]
    lane64 = iota((SLABS, 128), 1)

    def spread(base, target, rows):
        for col in range(18):
            target[rows, 128 * col : 128 * col + 128] = flat[pl.ds(base + col, SLABS, stride=ROWS), :].astype(
                target.dtype
            )
        line = flat[pl.ds(36, SLABS, stride=ROWS), :]
        for plane in range(2):
            at = 80 + (12 if base else 0) + 6 * plane
            moved = jnp.where(lane64 < 6, pltpu.roll(line, 128 - at, axis=1), 0.0)
            target[rows, MAIN + 128 * plane : MAIN + 128 * plane + 128] = moved.astype(target.dtype)
        return line

    flat[...] = other[...].astype(F32).reshape(SLABS * ROWS, 128)
    spread(18, refs, slice(64, 128))
    flat[...] = own[...].astype(F32).reshape(SLABS * ROWS, 128)
    spread(18, refs, slice(0, 64))
    meta = spread(0, tiles, slice(0, 64)).astype(BF)

    waves[:, : 2 * L] = pair[...]
    wanted = (iota((L, 128), 0) == iota((L, 128), 1) + 6 * slab).astype(BF)
    waves[:, 768:896] = dot(pair[:, :L], wanted).astype(BF)
    waves[:, 896:1024] = dot(pair[:, L:], wanted).astype(BF)
    turns = dot(widen[...], turn[0]).astype(BF)
    pad = jnp.zeros((112, 128), BF)
    ends = jnp.concatenate(
        [
            jnp.concatenate([extra[0, :8].astype(F32), jnp.zeros((8, 128), F32)], 0).astype(BF),
            pad,
            jnp.concatenate([extra[0, 8:].astype(F32), jnp.zeros((8, 128), F32)], 0).astype(BF),
            pad,
        ],
        0,
    )

    block = 256
    rowb = iota((block, 128), 0)
    laneb = iota((block, 128), 1)
    mine = (laneb & 15) == (rowb & 15)
    lanef = laneb.astype(F32)

    def gather(q, carry):
        rows = pl.ds(pl.multiple_of(block * q, block), block)
        repeat = iota((block, SLABS), 1) == 16 * q + (iota((block, SLABS), 0) >> 4)
        fields = dot(repeat.astype(BF), meta)
        spots = dot(jnp.where(mine, fields, 0.0).astype(BF), field[...])
        hot_x = jnp.concatenate([(lanef + 128.0 * j == spots[:, :128]).astype(BF) for j in range(3)], 1)
        hot_y = jnp.concatenate([(lanef + 128.0 * j == spots[:, 128:256]).astype(BF) for j in range(3)], 1)
        hot_t = (lanef == spots[:, 256:]).astype(BF)
        ref_of[rows, :] = dot(hot_t, refs[...]).astype(BF)
        wave_of[rows, :] = dot(hot_y, waves[...]).astype(BF)
        turned[rows, :] = lax.dot_general(
            hot_x, turns, (((1,), (1,)), ((), ())), preferred_element_type=F32
        ).astype(BF)
        return carry

    lax.fori_loop(0, N_CAND // block, gather, 0)

    def multiply(q, carry):
        eight = pl.ds(pl.multiple_of(8 * q, 8), 8)
        for size, wave_at, places in (
            (L, 0, tuple((L * part, 3 * L + L * part) for part in range(3))),
            (128, 2 * L, ((MAIN, MAIN + 128),)),
        ):
            for at_r, at_i in places:
                tiles_r = tiles[eight, at_r : at_r + size]
                tiles_i = tiles[eight, at_i : at_i + size]
                for j in range(8):
                    rows = pl.ds(pl.multiple_of(128 * q + 16 * j, 16), 16)
                    cos_y = wave_of[rows, wave_at : wave_at + size].astype(F32)
                    sin_y = wave_of[rows, wave_at + size : wave_at + 2 * size].astype(F32)
                    tile_r, tile_i = tiles_r[j : j + 1], tiles_i[j : j + 1]
                    ref_r = ref_of[rows, at_r : at_r + size].astype(F32)
                    ref_i = ref_of[rows, at_i : at_i + size].astype(F32)
                    prod_r = tile_r * ref_r + tile_i * ref_i
                    prod_i = tile_i * ref_r - tile_r * ref_i
                    both[rows, at_r : at_r + size] = (prod_r * cos_y - prod_i * sin_y).astype(BF)
                    both[rows, at_i : at_i + size] = (prod_r * sin_y + prod_i * cos_y).astype(BF)
        return carry

    lax.fori_loop(0, 8, multiply, 0)

    kept = (laneb >> 4) == (rowb & 7)

    def finish(q, carry):
        rows = pl.ds(pl.multiple_of(block * q, block), block)
        sums = dot(both[rows, :MAIN], comb[...]) + dot(both[rows, MAIN:], ends)
        kappa = turned[rows, :].astype(F32)
        mixed = jnp.concatenate([(sums * kappa[:, :128]).astype(BF), (sums * kappa[:, 128:]).astype(BF)], 1)
        total = jnp.where(kept, dot(mixed, last[0]) * (1.0 / (L * L)), 0.0)
        to = pl.ds(pl.multiple_of(block // 8 * q, block // 8), block // 8)
        out[to, :] = jnp.sum(total.reshape(block // 8, 8, 128), axis=1)
        return carry

    lax.fori_loop(0, N_CAND // block, finish, 0)


def refine(ids, own, other):
    by_slab = lambda i, ids: (ids[2], 0, 0)

    def kernel(ids_ref, *refs):
        refine_kernel(*refs[:9], ids_ref, *refs[9:])

    return pl.pallas_call(
        kernel,
        out_shape=jax.ShapeDtypeStruct((128, 128), F32),
        grid_spec=pltpu.PrefetchScalarGridSpec(
            num_scalar_prefetch=1,
            grid=(1,),
            in_specs=[
                full_spec((SLABS, ROWS, 128)),
                full_spec((SLABS, ROWS, 128)),
                full_spec((L, 2 * L)),
                full_spec((128, 384)),
                full_spec((MAIN, 128)),
                full_spec((256, 16)),
                pl.BlockSpec((1, 16, L), by_slab),
                pl.BlockSpec((1, 16, 128), by_slab),
                pl.BlockSpec((1, 256, 128), by_slab),
            ],
            out_specs=full_spec((128, 128)),
            scratch_shapes=[
                pltpu.VMEM((SLABS * ROWS, 128), F32),
                pltpu.VMEM((SLABS, MAIN + 256), F32),
                pltpu.VMEM((128, MAIN + 256), BF),
                pltpu.VMEM((L, 1024), BF),
                pltpu.VMEM((N_CAND, MAIN + 256), BF),
                pltpu.VMEM((N_CAND, 1024), BF),
                pltpu.VMEM((N_CAND, MAIN + 256), BF),
                pltpu.VMEM((N_CAND, 256), BF),
            ],
        ),
        compiler_params=pltpu.CompilerParams(vmem_limit_bytes=62 * MB),
        cost_estimate=pl.CostEstimate(flops=6_000_000_000, bytes_accessed=4 * MB, transcendentals=0),
        name="refine_slab",
    )(
        ids, own, other, TAB["pair"], TAB["field"], TAB["comb"], TAB["widen"], TAB["turn"], TAB["extra"], TAB["last"]
    )


def search_kernel(ids, spec, own, oth, cols, rows, reverse, mip, zmap, prod, total, square):
    core = ids[1]
    mine = pl.ds(pl.multiple_of(core * Q, Q), Q)
    yours = pl.ds(pl.multiple_of((1 - core) * Q, Q), Q)
    row16 = iota((16, L), 0)
    zero = jnp.zeros((16, L), F32)
    ends_r, ends_i = zero, zero
    for n in range(8):
        for ref, where in ((own, mine), (oth, yours)):
            tile_r, tile_i = spec[0, where, :].astype(F32), spec[1, where, :].astype(F32)
            t_r, t_i = ref[n, 0].astype(F32), ref[n, 1].astype(F32)
            prod[n, where, :L] = (tile_r * t_r + tile_i * t_i).astype(BF)
            prod[n, where, L:] = (tile_i * t_r - tile_r * t_i).astype(BF)
        top_r = jnp.where(core == 0, own[n, 0, :16].astype(F32), oth[n, 0, :16].astype(F32))
        top_i = jnp.where(core == 0, own[n, 1, :16].astype(F32), oth[n, 1, :16].astype(F32))
        ends_r = jnp.where(row16 == n, top_r[0:1], ends_r)
        ends_i = jnp.where(row16 == n, top_i[0:1], ends_i)
    ends_r = jnp.where(row16 == 8, spec[0, :16].astype(F32)[0:1], ends_r)
    ends_i = jnp.where(row16 == 8, spec[1, :16].astype(F32)[0:1], ends_i)
    back_r = dot(ends_r.astype(BF), reverse[...])
    back_i = dot(ends_i.astype(BF), reverse[...])
    low_r, low_i = 0.5 * (ends_r + back_r), 0.5 * (ends_i - back_i)
    top_r, top_i = -0.5 * (ends_i + back_i), 0.5 * (ends_r - back_r)

    def cross(a_r, a_i):
        s_r, s_i = a_r[8:9], a_i[8:9]
        return s_r * a_r + s_i * a_i, s_i * a_r - s_r * a_i

    low = cross(low_r, low_i)
    top = cross(top_r, top_i)
    line_r = low[0] - top[1]
    line_i = low[1] + top[0]
    for n in range(8):
        for at, line in ((0, line_r), (L, line_i)):
            old = prod[n, :16, at : at + L].astype(F32)
            prod[n, :16, at : at + L] = jnp.where(row16 == 0, line[n : n + 1], old).astype(BF)

    def step(pair, carry):
        both = []
        stacked = prod[pl.ds(2 * pair, 2)].reshape(2 * H, 2 * L)
        middle = dot(stacked, cols[...]).astype(BF)
        for k in range(2):
            part = middle[H * k : H * k + H]
            both.append(jnp.concatenate([part[:, :L], part[:, L:]], 0))
        corr = dot(rows[...], jnp.concatenate(both, 1)) * (1.0 / (L * L))
        one, two = corr[:, :L], corr[:, L:]
        largest = jnp.maximum(one, two)
        summed = one + two
        powers = one * one + two * two

        @pl.when(pair == 0)
        def _():
            mip[...] = largest
            total[...] = summed
            square[...] = powers

        @pl.when(pair > 0)
        def _():
            mip[...] = jnp.maximum(mip[...], largest)
            total[...] += summed
            square[...] += powers

        return carry

    lax.fori_loop(0, 4, step, 0)
    mean = total[...] * 0.125
    var = square[...] * 0.125 - mean * mean
    zmap[...] = (mip[...] - mean) * lax.rsqrt(jnp.maximum(var, 0.25))


def search(ids, spec, own, other):
    piece = full_spec((8, 2, Q, L))
    return pl.pallas_call(
        search_kernel,
        out_shape=(jax.ShapeDtypeStruct((L, L), F32), jax.ShapeDtypeStruct((L, L), F32)),
        grid_spec=pltpu.PrefetchScalarGridSpec(
            num_scalar_prefetch=1,
            grid=(1,),
            in_specs=[full_spec((2, H, L))]
            + [piece] * 2
            + [full_spec((2 * L, 2 * L)), full_spec((L, L)), full_spec((L, L))],
            out_specs=[full_spec((L, L)), full_spec((L, L))],
            scratch_shapes=[
                pltpu.VMEM((8, H, 2 * L), BF),
                pltpu.VMEM((L, L), F32),
                pltpu.VMEM((L, L), F32),
            ],
        ),
        compiler_params=pltpu.CompilerParams(vmem_limit_bytes=62 * MB),
        cost_estimate=pl.CostEstimate(flops=4_000_000_000, bytes_accessed=6 * MB, transcendentals=0),
        name="search_templates",
    )(ids, spec, own, other, TAB["inverse_cols"], TAB["inverse_rows"], TAB["reverse"])


def ring(count, step):
    return [(i, (i + step) % count) for i in range(count)]


def body(micrograph, templates, ref_bank, peak_offsets, peak_template, owners):
    blk = lax.axis_index(ROWS_OF)
    group = lax.axis_index(COLS_OF)
    core = lax.axis_index("core")
    ids = jnp.stack([blk, core, blk * 8 + group // 2]).astype(jnp.int32)

    def across(array):
        return lax.ppermute(array, "core", ring(2, 1))

    message, spec, copies = prepare(
        ids,
        peak_offsets.T,
        peak_template.reshape(1, 16),
        owners.reshape(1, 16),
        micrograph,
        templates,
        ref_bank,
    )
    arrived = lax.all_to_all(message, CHIPS, 0, 0, tiled=True)
    arrived, copies = lax.optimization_barrier((arrived, copies))
    seen = lax.all_to_all(copies, ROWS_OF, 0, 0, tiled=True)
    scores = refine(ids, arrived, across(arrived))
    scores, seen = lax.optimization_barrier((scores, seen))
    returned = lax.all_to_all(scores.reshape(SLABS, 2, 128), CHIPS, 0, 0, tiled=True)
    mip, zmap = search(ids, spec, seen, across(seen))
    returned, mip, zmap = lax.optimization_barrier((returned, mip, zmap))
    refined = jnp.sum(returned, 0).reshape(16, 16)[:, :9]
    return (mip, zmap, refined)


def solution(mesh):
    inner = Mesh(mesh.devices.reshape(2, 4, 4, 2, 2), ("zl", "y", "x", "zh", "core"))
    every = ROWS_OF + COLS_OF
    placed = (
        P(ROWS_OF, COLS_OF),
        P(ROWS_OF, None, None),
        P(COLS_OF, None, None),
        P(every, None),
        P(every),
        P(every, None),
    )
    return jax.shard_map(
        body,
        mesh=inner,
        in_specs=placed,
        out_specs=(P(ROWS_OF, COLS_OF), P(ROWS_OF, COLS_OF), P(every, None)),
        check_vma=False,
    )
```

time: 90.4 us -> 75.4 us (0.83)
  waiting for transfers between devices: 12.9 us -> 2.23 us
  Pallas kernels: 24.6 us -> 31.8 us
  local copies, waits for them, and re-layouts: 7.76 us -> 2.55 us
  starting transfers between devices: 17.3 us -> 12.2 us
  other arithmetic: 1.73 us -> 0.72 us
    ppermute x4 -> x0, waiting for transfers between devices: 12.9 us -> none  [the longest x3 7.95 us: body(): lax.ppermute(both, 'y', ring(4, step))]
    ppermute x5 -> x2, starting transfers between devices: 9.11 us -> 3.4 us  [across(): return lax.ppermute(array, 'core', ring(2, 1))]
    unnamed x32 -> x8, local copies, waits for them, and re-layouts: 6.98 us -> 1.87 us
    pallas_call x3 -> x2, Pallas kernels: 16.7 us -> 20.8 us  [the longest x1 14.1 us: refine(): pl.pallas_call(kernel, out_shape=jax.ShapeDtypeStruct((128, 128), F32), g...]
    all_to_all x0 -> x1, starting transfers between devices: none -> 3.56 us  [body(): seen = lax.all_to_all(copies, ROWS_OF, 0, 0, tiled=True)]
    ppermute x4 -> x0, starting transfers between devices: 3.41 us -> none  [the longest x3 2.82 us: body(): lax.ppermute(both, 'y', ring(4, step))]
    pallas_call x1, Pallas kernels: 7.98 us -> 11 us  [search(): pl.pallas_call(search_kernel, out_shape=(jax.ShapeDtypeStruct((L, L), F32...]
    all_to_all x0 -> x1, waiting for transfers between devices: none -> 2.22 us  [body(): seen = lax.all_to_all(copies, ROWS_OF, 0, 0, tiled=True)]
  transfers between devices with their start and end apart: 10 -> 4, of which waited for: 4 -> 1; matrix products, arithmetic and copies ran while one was open for 0% -> 0% of each run, Pallas kernels for 25% -> 33%
where the time goes in v1:
time: 75.4 us; the launch traced here: 75 us
  Pallas kernels  31.8 us (42%)
  blocking collectives  24.8 us (33%)
  starting transfers between devices  12.2 us (16%)
  local copies, waits for them, and re-layouts  2.55 us (3%)
  waiting for transfers between devices  2.23 us (3%)
    all_to_all x1, blocking collectives, body(): arrived = lax.all_to_all(message, CHIPS, 0, 0, tiled=True)  24.8 us
    pallas_call x1, Pallas kernels, refine(): pl.pallas_call(kernel, out_shape=jax.ShapeDtypeStruct((128, 128), F32), g...  14.1 us
    pallas_call x1, Pallas kernels, search(): pl.pallas_call(search_kernel, out_shape=(jax.ShapeDtypeStruct((L, L), F32...  11 us
    pallas_call x1, Pallas kernels, prepare(): pl.pallas_call(prepare_kernel, out_shape=(jax.ShapeDtypeStruct((SLABS, RO...  6.74 us
    all_to_all x1, starting transfers between devices, body(): lax.all_to_all(scores.reshape(SLABS, 2, 128), CHIPS, 0, 0, tiled=True)  5.21 us
    all_to_all x1, starting transfers between devices, body(): seen = lax.all_to_all(copies, ROWS_OF, 0, 0, tiled=True)  3.56 us
    ppermute x2, starting transfers between devices, across(): return lax.ppermute(array, 'core', ring(2, 1))  3.4 us
    all_to_all x1, waiting for transfers between devices, body(): seen = lax.all_to_all(copies, ROWS_OF, 0, 0, tiled=True)  2.22 us
  transfers between devices with their start and end apart: 4, of which 1 were waited for; matrix products, arithmetic and copies ran while one was open for 0% of the time, Pallas kernels for 33%

profile of v1, /device:TPU:1, one launch (start us, length us, event | category | flops | bytes accessed | tf_op | source)
XLA Modules:
  0.0 75.0 jit_solution(5348340638193410256)
XLA Ops:
  0.6 0.6 pad_add_fusion.ids.ids_ref
  1.3 6.7 %prepare_spectra.1 = (bf16[64,40,128]{2,1,0:T(8,128)(2,1)}, bf16[2,192,384]{2,1,0:T(8,128)(2,1)}, bf16[8,2,96,384]{3,2,1,0:T(8,128)(2,1)}) custom-call(s32[3]{0:T(128)} %pad_add_fusion.ids.ids_ref, s32[2,16]{1,0:T(2,128)} %bitcast.10, s32[1,16]{1,0:T(1,128)} %bitcast.11, s32[1,16]{1,0:T(1,128)} %bitcast.12, bf16[384,384]{1,0:T(8,128)(2,1)} %tile_hbm.1, ...), custom_call_target="tpu_custom_call" | custom-call | flops 1000000000 | bytes 4194304 | tf_op jit(solution)/shard_map/prepare_spectra/pallas_call | solution.py:229
  8.0 24.8 %all_to_all.15.refs_0_ = bf16[64,40,128]{2,1,0:T(8,128)(2,1)S(1)} all-to-all(bf16[64,40,128]{2,1,0:T(8,128)(2,1)} %get-tuple-element.15), channel_id=1, replica_groups=mesh['zl'=2,'y'=4,'x'=4,'zh'=2,'core'=2] {'zl','y','x','zh'}, dimensions={0} | all-to-all | bytes 1310720 | tf_op jit(solution)/shard_map/all_to_all | solution.py:528
  32.8 0.0 copy-start.1
  32.9 2.6 %collective-permute-start = (bf16[64,40,128]{2,1,0:T(8,128)(2,1)S(1)}, bf16[64,40,128]{2,1,0:T(8,128)(2,1)S(1)}, u32[]{:S(2)}, u32[]{:S(2)}) collective-permute-start(bf16[64,40,128]{2,1,0:T(8,128)(2,1)S(1)} %all_to_all.15.refs_0_), channel_id=1, source_target_pairs={{0,1},{1,0},{2,3},{3,2},{4,5},{5,4},{6,7},{7,6},{8,9},{9,8},{10,11... | collective-permute-start | bytes 1966088 | tf_op jit(solution)/shard_map/ppermute | solution.py:517
  35.4 0.0 copy-done.1
  35.4 3.6 %all-to-all-start.1 = ((bf16[8,2,96,384]{3,2,1,0:T(8,128)(2,1)}), bf16[8,2,96,384]{3,2,1,0:T(8,128)(2,1)S(1)}, u32[]{:S(2)}, u32[]{:S(2)}) async-start(bf16[8,2,96,384]{3,2,1,0:T(8,128)(2,1)} %get-tuple-element.18), calls=%async_computation.1 | async-start | bytes 2359296 | tf_op jit(solution)/shard_map/all_to_all | solution.py:530
  39.0 0.0 collective-permute-done.refs_1_
  39.0 0.0 copy-start.3
  39.0 0.8 %copy-done.3 = bf16[64,40,128]{2,1,0:T(8,128)(2,1)} copy-done((bf16[64,40,128]{2,1,0:T(8,128)(2,1)}, bf16[64,40,128]{2,1,0:T(8,128)(2,1)S(1)}, u32[]{:S(2)}) %copy-start.3) | copy-done | bytes 655384
  39.8 14.1 %refine_slab.1 = f32[128,128]{1,0:T(8,128)} custom-call(s32[3]{0:T(128)} %pad_add_fusion.ids.ids_ref, bf16[64,40,128]{2,1,0:T(8,128)(2,1)} %copy-done.1, bf16[64,40,128]{2,1,0:T(8,128)(2,1)} %copy-done.3, bf16[384,768]{1,0:T(8,128)(2,1)} %constant.67.clone.pair_hbm.refs_2_, bf16[128,384]{1,0:T(8,128)(2,1)} %constant.70.clone.refs_3_, ...), custom_call_target="tpu_custom_call" | custom-call | flops 6000000000 | bytes 4194304 | tf_op jit(solution)/shard_map/refine_slab/pallas_call | solution.py:375
  54.0 2.2 %all-to-all-done.1.own = bf16[8,2,96,384]{3,2,1,0:T(8,128)(2,1)S(1)} async-done(((bf16[8,2,96,384]{3,2,1,0:T(8,128)(2,1)}), bf16[8,2,96,384]{3,2,1,0:T(8,128)(2,1)S(1)}, u32[]{:S(2)}, u32[]{:S(2)}) %all-to-all-start.1) | async-done | bytes 1179680 | tf_op jit(solution)/shard_map/all_to_all | solution.py:530
  56.2 0.0 copy-start
  56.2 0.8 %collective-permute-start.1 = (bf16[8,2,96,384]{3,2,1,0:T(8,128)(2,1)S(1)}, bf16[8,2,96,384]{3,2,1,0:T(8,128)(2,1)S(1)}, u32[]{:S(2)}, u32[]{:S(2)}) collective-permute-start(bf16[8,2,96,384]{3,2,1,0:T(8,128)(2,1)S(1)} %all-to-all-done.1.own), channel_id=1, source_target_pairs={{0,1},{1,0},{2,3},{3,2},{4,5},{5,4},{6,7},{7,6},{8,9},{9,8},{10,11... | collective-permute-start | bytes 3538952 | tf_op jit(solution)/shard_map/ppermute | solution.py:517
  57.0 5.2 %all-to-all-start.2 = ((f32[64,2,128]{2,1,0:T(2,128)}), f32[64,2,128]{2,1,0:T(2,128)S(1)}, u32[]{:S(2)}, u32[]{:S(2)}) async-start(f32[64,2,128]{2,1,0:T(2,128)} %bitcast.8), calls=%async_computation.2 | async-start | bytes 131072 | tf_op jit(solution)/shard_map/all_to_all | solution.py:533
  62.2 0.0 collective-permute-done.1.oth
  62.2 0.0 copy-start.2
  62.2 1.0 %copy-done.2 = bf16[8,2,96,384]{3,2,1,0:T(8,128)(2,1)} copy-done((bf16[8,2,96,384]{3,2,1,0:T(8,128)(2,1)}, bf16[8,2,96,384]{3,2,1,0:T(8,128)(2,1)S(1)}, u32[]{:S(2)}) %copy-start.2) | copy-done | bytes 1179672
  63.3 0.0 copy-done
  63.3 11.0 %search_templates.1 = (f32[384,384]{1,0:T(8,128)}, f32[384,384]{1,0:T(8,128)}) custom-call(s32[3]{0:T(128)} %pad_add_fusion.ids.ids_ref, bf16[2,192,384]{2,1,0:T(8,128)(2,1)} %get-tuple-element.20.spec, bf16[8,2,96,384]{3,2,1,0:T(8,128)(2,1)} %copy-done, bf16[8,2,96,384]{3,2,1,0:T(8,128)(2,1)} %copy-done.2, bf16[768,768]{1,0:T(8,128)(2,1)} %constant.76.clone.cols, ...), custom_call_target="tpu_custom_call" | custom-call | flops 4000000000 | bytes 6291456 | tf_op jit(solution)/shard_map/search_templates/pallas_call | solution.py:484
  74.2 0.0 all-to-all-done.2
  74.3 0.1 reduce_sum.9
  74.3 0.7 reshape.21
Async XLA Ops:
  32.8 2.6 %copy-start.1 = (bf16[64,40,128]{2,1,0:T(8,128)(2,1)}, bf16[64,40,128]{2,1,0:T(8,128)(2,1)S(1)}, u32[]{:S(2)}) copy-start(bf16[64,40,128]{2,1,0:T(8,128)(2,1)S(1)} %all_to_all.15.refs_0_) | copy-start | bytes 1966084
  32.9 6.2 %collective-permute-start = (bf16[64,40,128]{2,1,0:T(8,128)(2,1)S(1)}, bf16[64,40,128]{2,1,0:T(8,128)(2,1)S(1)}, u32[]{:S(2)}, u32[]{:S(2)}) collective-permute-start(bf16[64,40,128]{2,1,0:T(8,128)(2,1)S(1)} %all_to_all.15.refs_0_), channel_id=1, source_target_pairs={{0,1},{1,0},{2,3},{3,2},{4,5},{5,4},{6,7},{7,6},{8,9},{9,8},{10,11... | collective-permute-start | bytes 1966088 | tf_op jit(solution)/shard_map/ppermute | solution.py:517
  35.4 20.7 %all-to-all-start.1 = ((bf16[8,2,96,384]{3,2,1,0:T(8,128)(2,1)}), bf16[8,2,96,384]{3,2,1,0:T(8,128)(2,1)S(1)}, u32[]{:S(2)}, u32[]{:S(2)}) async-start(bf16[8,2,96,384]{3,2,1,0:T(8,128)(2,1)} %get-tuple-element.18), calls=%async_computation.1 | async-start | bytes 2359296 | tf_op jit(solution)/shard_map/all_to_all | solution.py:530
  39.0 0.8 %copy-start.3 = (bf16[64,40,128]{2,1,0:T(8,128)(2,1)}, bf16[64,40,128]{2,1,0:T(8,128)(2,1)S(1)}, u32[]{:S(2)}) copy-start(bf16[64,40,128]{2,1,0:T(8,128)(2,1)S(1)} %collective-permute-done.refs_1_) | copy-start | bytes 1966084
  56.2 7.1 %copy-start = (bf16[8,2,96,384]{3,2,1,0:T(8,128)(2,1)}, bf16[8,2,96,384]{3,2,1,0:T(8,128)(2,1)S(1)}, u32[]{:S(2)}) copy-start(bf16[8,2,96,384]{3,2,1,0:T(8,128)(2,1)S(1)} %all-to-all-done.1.own) | copy-start | bytes 3538948
  56.2 6.0 %collective-permute-start.1 = (bf16[8,2,96,384]{3,2,1,0:T(8,128)(2,1)S(1)}, bf16[8,2,96,384]{3,2,1,0:T(8,128)(2,1)S(1)}, u32[]{:S(2)}, u32[]{:S(2)}) collective-permute-start(bf16[8,2,96,384]{3,2,1,0:T(8,128)(2,1)S(1)} %all-to-all-done.1.own), channel_id=1, source_target_pairs={{0,1},{1,0},{2,3},{3,2},{4,5},{5,4},{6,7},{7,6},{8,9},{9,8},{10,11... | collective-permute-start | bytes 3538952 | tf_op jit(solution)/shard_map/ppermute | solution.py:517
  57.0 17.2 %all-to-all-start.2 = ((f32[64,2,128]{2,1,0:T(2,128)}), f32[64,2,128]{2,1,0:T(2,128)S(1)}, u32[]{:S(2)}, u32[]{:S(2)}) async-start(f32[64,2,128]{2,1,0:T(2,128)} %bitcast.8), calls=%async_computation.2 | async-start | bytes 131072 | tf_op jit(solution)/shard_map/all_to_all | solution.py:533
  62.2 1.0 %copy-start.2 = (bf16[8,2,96,384]{3,2,1,0:T(8,128)(2,1)}, bf16[8,2,96,384]{3,2,1,0:T(8,128)(2,1)S(1)}, u32[]{:S(2)}) copy-start(bf16[8,2,96,384]{3,2,1,0:T(8,128)(2,1)S(1)} %collective-permute-done.1.oth) | copy-start | bytes 3538948

commit v2 on v1

v2 whole, which is shorter than its diff:
```python
import math

import jax
import jax.numpy as jnp
import numpy as np
from jax import lax
from jax.experimental import pallas as pl
from jax.experimental.pallas import tpu as pltpu
from jax.sharding import Mesh
from jax.sharding import PartitionSpec as P

L = 384
H = 192
Q = 96
SLABS = 64
ROWS = 40
WIDE = 1280
BF = jnp.bfloat16
F32 = jnp.float32
MB = 1024 * 1024
LIMIT = 62 * MB
ROWS_OF = ("zl", "y")
COLS_OF = ("x", "zh", "core")
CHIPS = ("zl", "y", "x", "zh")


def dot(a, b):
    return jnp.dot(a, b, preferred_element_type=F32)


def wave(a, b):
    angle = (np.multiply.outer(np.asarray(a), np.asarray(b)) % L) * (2.0 * math.pi / L)
    return np.cos(angle), np.sin(angle)


def bf(a):
    return np.asarray(a, np.float32).astype(jnp.bfloat16)


def make_tables():
    n = np.arange(L)
    cos, sin = wave(n, n)
    forward = np.concatenate([cos[:H], cos[H : H + 1], sin[1:H]], 0)
    halves = np.stack(
        [np.concatenate([forward[c * Q : c * Q + Q], forward[H + c * Q : H + c * Q + Q]], 0) for c in range(2)]
    )
    pair = np.concatenate([cos, sin], 1)
    inverse_cols = np.concatenate([pair, np.concatenate([-sin, cos], 1)], 0)
    weight = np.full((H,), 2.0)
    weight[0] = 1.0
    inverse_rows = np.concatenate([cos[:, :H] * weight, -2.0 * sin[:, :H]], 1)
    inverse_rows[:, H] = cos[:, H]
    reverse = np.zeros((L, L))
    reverse[(-n) % L, n] = 1.0
    pick = np.zeros((4, L, 128))
    for part in range(4):
        pick[part, n, 80 + 6 * part + n % 6] = 1.0
    lane = np.arange(128)
    field = np.zeros((128, 3, 128))
    for which, at in enumerate((0, 32, 64)):
        if which < 2:
            field[at : at + 16, which] = 128.0
            at += 16
        field[at : at + 16, which] = 1.0
    ac = lane % 16
    a, c = ac // 3 - 1, ac % 3 - 1
    comb = np.zeros((2, 3, L, 128))
    extra = np.zeros((SLABS, 2, 8, 128))
    for shift in (-1, 0, 1):
        kc, ks = wave(n, [shift])
        for part in range(4):
            at = 6 * part + 2 * (shift + 1)
            if part < 3:
                comb[0, part, :, at], comb[0, part, :, at + 1] = kc[:, 0], ks[:, 0]
                comb[1, part, :, at], comb[1, part, :, at + 1] = -ks[:, 0], kc[:, 0]
            else:
                kc, ks = kc[:, 0].reshape(SLABS, 6), ks[:, 0].reshape(SLABS, 6)
                extra[:, 0, :6, at], extra[:, 0, :6, at + 1] = kc, ks
                extra[:, 1, :6, at], extra[:, 1, :6, at + 1] = -ks, kc
    turn = np.zeros((SLABS, 16, L))
    widen = np.zeros((256, 16))
    last = np.zeros((SLABS, 2, 128, 128))
    for part in range(4):
        widen[6 * part : 6 * part + 6, part] = 1.0
        widen[128 + 6 * part : 128 + 6 * part + 6, 4 + part] = 1.0
    for s in range(SLABS):
        for part in range(4):
            k = s + 64 * part if part < 3 else H
            kc, ks = wave([k], n)
            turn[s, part], turn[s, 4 + part] = kc[0], ks[0]
            ca, sa = wave([k], a)
            w = 1.0 if k in (0, H) else 2.0
            for shift in (-1, 0, 1):
                at = 6 * part + 2 * (shift + 1)
                on = w * ((ac < 9) & (c == shift))
                last[s, 0, at], last[s, 0, at + 1] = on * ca[0], -on * sa[0]
                last[s, 1, at], last[s, 1, at + 1] = -on * sa[0], -on * ca[0]
    return dict(
        forward=bf(forward),
        halves=bf(halves),
        pair=bf(pair),
        inverse_cols=bf(inverse_cols),
        inverse_rows=bf(inverse_rows),
        reverse=bf(reverse),
        pick=bf(pick.reshape(4 * L, 128)),
        field=bf(field.reshape(128, 384)),
        comb=bf(comb.reshape(6 * L, 128)),
        extra=bf(extra.reshape(SLABS, 16, 128)),
        turn=bf(turn),
        widen=bf(widen),
        last=bf(last.reshape(SLABS, 256, 128)),
    )


TAB = make_tables()


def full_spec(shape):
    zeros = (0,) * len(shape)
    return pl.BlockSpec(shape, lambda i: zeros)


def place():
    blk = lax.axis_index("zl") * 4 + lax.axis_index("y")
    slab = blk * 8 + lax.axis_index("x") * 2 + lax.axis_index("zh")
    return blk, lax.axis_index("core"), slab


def iota(shape, dim):
    return lax.broadcasted_iota(jnp.int32, shape, dim)


def prepare_kernel(
    offsets,
    choice,
    owners,
    tile_hbm,
    bank_hbm,
    forward_hbm,
    pair_hbm,
    pick_hbm,
    msg,
    spec,
    flat,
    tile,
    ref,
    forward,
    pair,
    pick,
    sems,
):
    blk, core, _ = place()
    jobs = (
        (forward_hbm, forward),
        (tile_hbm, tile),
        (pair_hbm, pair),
        (bank_hbm.at[blk], ref),
        (pick_hbm, pick),
    )
    copies = [pltpu.make_async_copy(src, dst, sems.at[n]) for n, (src, dst) in enumerate(jobs)]
    for copy in copies:
        copy.start()

    r8 = iota((8, 16), 0)
    ox, oy = offsets[0:1], offsets[1:2]
    owner = owners[...]
    named = choice[...] * 8 + (owner >> 1) + 64 * ((owner & 1) ^ core)
    values = jnp.where(r8 == 4, named, 0)
    for n, value in enumerate((ox >> 7, ox & 127, oy >> 7, oy & 127)):
        values = jnp.where(r8 == n, value, values)
    wide = ((iota((16, 128), 1) & 15) == iota((16, 128), 0)).astype(BF)
    lined = dot(values.astype(F32).astype(BF), wide)
    lined = jnp.where((iota((8, 128), 1) >> 4) == iota((8, 128), 0), lined, 0.0)
    meta = jnp.sum(lined, axis=0, keepdims=True)

    rows64 = iota((SLABS, L), 0)
    owned = (iota((SLABS, L), 1) // 6) == rows64
    first_row = rows64 == 0
    for row in range(37, ROWS):
        flat[pl.ds(row, SLABS, stride=ROWS), :] = jnp.zeros((SLABS, 128), F32)
    copies[0].wait()
    lasts = []
    for which, image in enumerate((tile, ref)):
        copies[1 + 2 * which].wait()
        first = dot(forward[...], image[...]).astype(BF)
        if which == 0:
            copies[2].wait()
        second = dot(first, pair[...])
        real = second[:H, :L] - second[H:, L:]
        imag = -(second[:H, L:] + second[H:, :L])
        if which == 0:
            spec[0] = real.astype(BF)
            spec[1] = imag.astype(BF)
        for plane, (full, alone) in enumerate(((real, second[:64, :L]), (imag, -second[:64, L:]))):
            for part in range(3):
                block = full[64 * part : 64 * part + 64]
                if part == 0:
                    block = jnp.where(first_row, alone, block)
                for j in range(3):
                    row = 18 * which + 9 * plane + 3 * part + j
                    flat[pl.ds(row, SLABS, stride=ROWS), :] = block[:, 128 * j : 128 * j + 128]
        for last in (second[H : H + 1, :L], -second[H : H + 1, L:]):
            lasts.append(jnp.where(owned, jnp.broadcast_to(last, (SLABS, L)), 0.0).astype(BF))
    copies[4].wait()
    line = dot(jnp.concatenate(lasts, 1), pick[...])
    flat[pl.ds(36, SLABS, stride=ROWS), :] = line + meta
    msg[...] = flat[...].reshape(SLABS, ROWS, 128).astype(BF)


def prepare(offsets, choice, owners, tile, bank):
    held = pl.BlockSpec(memory_space=pltpu.HBM)
    return pl.pallas_call(
        prepare_kernel,
        out_shape=(
            jax.ShapeDtypeStruct((SLABS, ROWS, 128), BF),
            jax.ShapeDtypeStruct((2, H, L), BF),
        ),
        grid=(1,),
        in_specs=[full_spec((2, 16)), full_spec((1, 16)), full_spec((1, 16))] + [held] * 5,
        out_specs=[full_spec((SLABS, ROWS, 128)), full_spec((2, H, L))],
        scratch_shapes=[
            pltpu.VMEM((SLABS * ROWS, 128), F32),
            pltpu.VMEM((L, L), BF),
            pltpu.VMEM((L, L), BF),
            pltpu.VMEM((L, L), BF),
            pltpu.VMEM((L, 2 * L), BF),
            pltpu.VMEM((4 * L, 128), BF),
            pltpu.SemaphoreType.DMA((5,)),
        ],
        compiler_params=pltpu.CompilerParams(vmem_limit_bytes=LIMIT),
        cost_estimate=pl.CostEstimate(flops=1_000_000_000, bytes_accessed=4 * MB, transcendentals=0),
        name="prepare_spectra",
    )(offsets, choice, owners, tile, bank, TAB["forward"], TAB["pair"], TAB["pick"])


def template_kernel(template_hbm, halves_hbm, pair_hbm, half, template, rows_half, pair, sems):
    core = lax.axis_index("core")
    jobs = ((template_hbm.at[0], template), (halves_hbm.at[core], rows_half), (pair_hbm, pair))
    copies = [pltpu.make_async_copy(src, dst, sems.at[n]) for n, (src, dst) in enumerate(jobs)]
    for copy in copies:
        copy.start()
    copies[0].wait()
    values = template[...].astype(F32)
    count = 1.0 / (L * L)
    spread = values - jnp.sum(values) * count
    power = jnp.sum(spread * spread) * count
    scale = 1.0 / (L * jnp.sqrt(jnp.full((1, 1), power + 1e-06, F32)))
    normalized = (spread * scale).astype(BF)
    copies[1].wait()
    first = dot(rows_half[...], normalized).astype(BF)
    copies[2].wait()
    second = dot(first, pair[...])
    half[0] = (second[:Q, :L] - second[Q:, L:]).astype(BF)
    half[1] = (-(second[:Q, L:] + second[Q:, :L])).astype(BF)


def template_half(templates):
    held = pl.BlockSpec(memory_space=pltpu.HBM)
    return pl.pallas_call(
        template_kernel,
        out_shape=jax.ShapeDtypeStruct((2, Q, L), BF),
        grid=(1,),
        in_specs=[held] * 3,
        out_specs=full_spec((2, Q, L)),
        scratch_shapes=[
            pltpu.VMEM((L, L), BF),
            pltpu.VMEM((H, L), BF),
            pltpu.VMEM((L, 2 * L), BF),
            pltpu.SemaphoreType.DMA((3,)),
        ],
        compiler_params=pltpu.CompilerParams(vmem_limit_bytes=LIMIT),
        cost_estimate=pl.CostEstimate(flops=400_000_000, bytes_accessed=4 * MB, transcendentals=0),
        name="template_spectrum",
    )(templates, TAB["halves"], TAB["pair"])


MAIN = 6 * L
N_CAND = 1024


def refine_kernel(
    own_hbm, other_hbm, pair_hbm, field_hbm, comb_hbm, widen_hbm, turn_hbm, extra_hbm, last_hbm, out,
    own, other, pair, field, comb, widen, turn, extra, last,
    flat, tiles, refs, waves, ref_of, wave_of, both, turned, sems,
):
    slab = place()[2]
    jobs = (
        (other_hbm, other),
        (own_hbm, own),
        (pair_hbm, pair),
        (widen_hbm, widen),
        (turn_hbm.at[pl.ds(slab, 1)], turn),
        (extra_hbm.at[pl.ds(slab, 1)], extra),
        (field_hbm, field),
        (comb_hbm, comb),
        (last_hbm.at[pl.ds(slab, 1)], last),
    )
    copies = [pltpu.make_async_copy(src, dst, sems.at[n]) for n, (src, dst) in enumerate(jobs)]
    for copy in copies:
        copy.start()
    lane64 = iota((SLABS, 128), 1)

    def spread(base, target, rows):
        for col in range(18):
            target[rows, 128 * col : 128 * col + 128] = flat[pl.ds(base + col, SLABS, stride=ROWS), :].astype(
                target.dtype
            )
        line = flat[pl.ds(36, SLABS, stride=ROWS), :]
        for plane in range(2):
            at = 80 + (12 if base else 0) + 6 * plane
            moved = jnp.where(lane64 < 6, pltpu.roll(line, 128 - at, axis=1), 0.0)
            target[rows, MAIN + 128 * plane : MAIN + 128 * plane + 128] = moved.astype(target.dtype)
        return line

    copies[0].wait()
    flat[...] = other[...].astype(F32).reshape(SLABS * ROWS, 128)
    spread(18, refs, slice(64, 128))
    copies[1].wait()
    flat[...] = own[...].astype(F32).reshape(SLABS * ROWS, 128)
    spread(18, refs, slice(0, 64))
    meta = spread(0, tiles, slice(0, 64)).astype(BF)

    copies[2].wait()
    waves[:, : 2 * L] = pair[...]
    wanted = (iota((L, 128), 0) == iota((L, 128), 1) + 6 * slab).astype(BF)
    waves[:, 768:896] = dot(pair[:, :L], wanted).astype(BF)
    waves[:, 896:1024] = dot(pair[:, L:], wanted).astype(BF)
    copies[3].wait()
    copies[4].wait()
    copies[5].wait()
    turns = dot(widen[...], turn[0]).astype(BF)
    pad = jnp.zeros((112, 128), BF)
    ends = jnp.concatenate(
        [
            jnp.concatenate([extra[0, :8].astype(F32), jnp.zeros((8, 128), F32)], 0).astype(BF),
            pad,
            jnp.concatenate([extra[0, 8:].astype(F32), jnp.zeros((8, 128), F32)], 0).astype(BF),
            pad,
        ],
        0,
    )

    block = 256
    rowb = iota((block, 128), 0)
    laneb = iota((block, 128), 1)
    mine = (laneb & 15) == (rowb & 15)
    lanef = laneb.astype(F32)

    def gather(q):
        rows = pl.ds(block * q, block)
        repeat = iota((block, SLABS), 1) == 16 * q + (iota((block, SLABS), 0) >> 4)
        fields = dot(repeat.astype(BF), meta)
        spots = dot(jnp.where(mine, fields, 0.0).astype(BF), field[...])
        hot_x = jnp.concatenate([(lanef + 128.0 * j == spots[:, :128]).astype(BF) for j in range(3)], 1)
        hot_y = jnp.concatenate([(lanef + 128.0 * j == spots[:, 128:256]).astype(BF) for j in range(3)], 1)
        hot_t = (lanef == spots[:, 256:]).astype(BF)
        ref_of[rows, :] = dot(hot_t, refs[...]).astype(BF)
        wave_of[rows, :] = dot(hot_y, waves[...]).astype(BF)
        turned[rows, :] = lax.dot_general(
            hot_x, turns, (((1,), (1,)), ((), ())), preferred_element_type=F32
        ).astype(BF)

    def multiply(q):
        eight = pl.ds(8 * q, 8)
        for size, wave_at, places in (
            (L, 0, tuple((L * part, 3 * L + L * part) for part in range(3))),
            (128, 2 * L, ((MAIN, MAIN + 128),)),
        ):
            for at_r, at_i in places:
                tiles_r = tiles[eight, at_r : at_r + size]
                tiles_i = tiles[eight, at_i : at_i + size]
                for j in range(8):
                    rows = pl.ds(128 * q + 16 * j, 16)
                    cos_y = wave_of[rows, wave_at : wave_at + size].astype(F32)
                    sin_y = wave_of[rows, wave_at + size : wave_at + 2 * size].astype(F32)
                    tile_r, tile_i = tiles_r[j : j + 1], tiles_i[j : j + 1]
                    ref_r = ref_of[rows, at_r : at_r + size].astype(F32)
                    ref_i = ref_of[rows, at_i : at_i + size].astype(F32)
                    prod_r = tile_r * ref_r + tile_i * ref_i
                    prod_i = tile_i * ref_r - tile_r * ref_i
                    both[rows, at_r : at_r + size] = (prod_r * cos_y - prod_i * sin_y).astype(BF)
                    both[rows, at_i : at_i + size] = (prod_r * sin_y + prod_i * cos_y).astype(BF)

    kept = (laneb >> 4) == (rowb & 7)

    def finish(q):
        rows = pl.ds(block * q, block)
        sums = dot(both[rows, :MAIN], comb[...]) + dot(both[rows, MAIN:], ends)
        kappa = turned[rows, :].astype(F32)
        mixed = jnp.concatenate([(sums * kappa[:, :128]).astype(BF), (sums * kappa[:, 128:]).astype(BF)], 1)
        total = jnp.where(kept, dot(mixed, last[0]) * (1.0 / (L * L)), 0.0)
        to = pl.ds(block // 8 * q, block // 8)
        out[to, :] = jnp.sum(total.reshape(block // 8, 8, 128), axis=1)

    count = N_CAND // block
    for n in (6, 7, 8):
        copies[n].wait()
    gather(0)
    for q in range(count):
        if q + 1 < count:
            gather(q + 1)
        for p in range(block // 128):
            multiply(block // 128 * q + p)
        finish(q)


def refine(own, other):
    held = pl.BlockSpec(memory_space=pltpu.HBM)
    return pl.pallas_call(
        refine_kernel,
        out_shape=jax.ShapeDtypeStruct((128, 128), F32),
        grid=(1,),
        in_specs=[held] * 9,
        out_specs=full_spec((128, 128)),
        scratch_shapes=[
            pltpu.VMEM((SLABS, ROWS, 128), BF),
            pltpu.VMEM((SLABS, ROWS, 128), BF),
            pltpu.VMEM((L, 2 * L), BF),
            pltpu.VMEM((128, 384), BF),
            pltpu.VMEM((MAIN, 128), BF),
            pltpu.VMEM((256, 16), BF),
            pltpu.VMEM((1, 16, L), BF),
            pltpu.VMEM((1, 16, 128), BF),
            pltpu.VMEM((1, 256, 128), BF),
            pltpu.VMEM((SLABS * ROWS, 128), F32),
            pltpu.VMEM((SLABS, MAIN + 256), F32),
            pltpu.VMEM((128, MAIN + 256), BF),
            pltpu.VMEM((L, 1024), BF),
            pltpu.VMEM((N_CAND, MAIN + 256), BF),
            pltpu.VMEM((N_CAND, 1024), BF),
            pltpu.VMEM((N_CAND, MAIN + 256), BF),
            pltpu.VMEM((N_CAND, 256), BF),
            pltpu.SemaphoreType.DMA((9,)),
        ],
        compiler_params=pltpu.CompilerParams(vmem_limit_bytes=LIMIT),
        cost_estimate=pl.CostEstimate(flops=9_000_000_000, bytes_accessed=4 * MB, transcendentals=0),
        name="refine_slab",
    )(own, other, TAB["pair"], TAB["field"], TAB["comb"], TAB["widen"], TAB["turn"], TAB["extra"], TAB["last"])


def search_kernel(
    spec_hbm, o0, o1, o2, o3, p0, p1, p2, p3, cols_hbm, rows_hbm, reverse_hbm, mip, zmap,
    spec, own, oth, own_top, oth_top, cols, rows, reverse, prod, total, square, sems,
):
    core = lax.axis_index("core")
    owns, others = (o0, o1, o2, o3), (p0, p1, p2, p3)
    jobs = [(spec_hbm, spec), (reverse_hbm, reverse)]
    for p in range(4):
        jobs.append((owns[p].at[:, :, pl.ds(0, 16), :], own_top.at[pl.ds(2 * p, 2)]))
        jobs.append((others[p].at[:, :, pl.ds(0, 16), :], oth_top.at[pl.ds(2 * p, 2)]))
    tops = len(jobs)
    for p in range(4):
        jobs.append((owns[p], own.at[pl.ds(2 * p, 2)]))
        jobs.append((others[p], oth.at[pl.ds(2 * p, 2)]))
        if p == 0:
            jobs += [(cols_hbm, cols), (rows_hbm, rows)]
    copies = [pltpu.make_async_copy(src, dst, sems.at[n]) for n, (src, dst) in enumerate(jobs)]
    for copy in copies:
        copy.start()

    row16 = iota((16, L), 0)
    zero = jnp.zeros((16, L), F32)
    ends_r, ends_i = zero, zero
    for n in range(tops):
        copies[n].wait()
    for n in range(8):
        top_r = jnp.where(core == 0, own_top[n, 0].astype(F32), oth_top[n, 0].astype(F32))
        top_i = jnp.where(core == 0, own_top[n, 1].astype(F32), oth_top[n, 1].astype(F32))
        ends_r = jnp.where(row16 == n, top_r[0:1], ends_r)
        ends_i = jnp.where(row16 == n, top_i[0:1], ends_i)
    ends_r = jnp.where(row16 == 8, spec[0, :16].astype(F32)[0:1], ends_r)
    ends_i = jnp.where(row16 == 8, spec[1, :16].astype(F32)[0:1], ends_i)
    back = dot(jnp.concatenate([ends_r, ends_i], 0).astype(BF), reverse[...])
    back_r, back_i = back[:16], back[16:]
    low_r, low_i = 0.5 * (ends_r + back_r), 0.5 * (ends_i - back_i)
    top_r, top_i = -0.5 * (ends_i + back_i), 0.5 * (ends_r - back_r)

    def cross(a_r, a_i):
        s_r, s_i = a_r[8:9], a_i[8:9]
        return s_r * a_r + s_i * a_i, s_i * a_r - s_r * a_i

    low = cross(low_r, low_i)
    top = cross(top_r, top_i)
    line_r = low[0] - top[1]
    line_i = low[1] + top[0]

    def products(p):
        for n in (2 * p, 2 * p + 1):
            for ref, half in ((own, core), (oth, 1 - core)):
                for r in range(0, Q, 16):
                    where = pl.ds(pl.multiple_of(half * Q + r, 16), 16)
                    tile_r, tile_i = spec[0, where, :].astype(F32), spec[1, where, :].astype(F32)
                    t_r, t_i = ref[n, 0, r : r + 16].astype(F32), ref[n, 1, r : r + 16].astype(F32)
                    p_r = tile_r * t_r + tile_i * t_i
                    p_i = tile_i * t_r - tile_r * t_i
                    if r == 0:
                        lead = (row16 + half) == 0
                        p_r = jnp.where(lead, line_r[n : n + 1], p_r)
                        p_i = jnp.where(lead, line_i[n : n + 1], p_i)
                    prod[n, where, :L] = p_r.astype(BF)
                    prod[n, where, L:] = p_i.astype(BF)

    copies[tops].wait()
    copies[tops + 1].wait()
    products(0)
    copies[tops + 2].wait()
    copies[tops + 3].wait()
    for p in range(4):
        if p < 3:
            copies[tops + 4 + 2 * p].wait()
            copies[tops + 5 + 2 * p].wait()
            products(p + 1)
        middle = dot(prod[2 * p : 2 * p + 2].reshape(2 * H, 2 * L), cols[...]).astype(BF)
        both = []
        for k in range(2):
            part = middle[H * k : H * k + H]
            both.append(jnp.concatenate([part[:, :L], part[:, L:]], 0))
        corr = dot(rows[...], jnp.concatenate(both, 1)) * (1.0 / (L * L))
        one, two = corr[:, :L], corr[:, L:]
        largest = jnp.maximum(one, two)
        summed = one + two
        powers = one * one + two * two
        if p == 0:
            mip[...] = largest
            total[...] = summed
            square[...] = powers
        elif p < 3:
            mip[...] = jnp.maximum(mip[...], largest)
            total[...] += summed
            square[...] += powers
        else:
            largest = jnp.maximum(mip[...], largest)
            mean = (total[...] + summed) * 0.125
            var = (square[...] + powers) * 0.125 - mean * mean
            mip[...] = largest
            zmap[...] = (largest - mean) * lax.rsqrt(jnp.maximum(var, 0.25))


def search(spec, owns, others):
    held = pl.BlockSpec(memory_space=pltpu.HBM)
    return pl.pallas_call(
        search_kernel,
        out_shape=(jax.ShapeDtypeStruct((L, L), F32), jax.ShapeDtypeStruct((L, L), F32)),
        grid=(1,),
        in_specs=[held] * 12,
        out_specs=[full_spec((L, L)), full_spec((L, L))],
        scratch_shapes=[
            pltpu.VMEM((2, H, L), BF),
            pltpu.VMEM((8, 2, Q, L), BF),
            pltpu.VMEM((8, 2, Q, L), BF),
            pltpu.VMEM((8, 2, 16, L), BF),
            pltpu.VMEM((8, 2, 16, L), BF),
            pltpu.VMEM((2 * L, 2 * L), BF),
            pltpu.VMEM((L, L), BF),
            pltpu.VMEM((L, L), BF),
            pltpu.VMEM((8, H, 2 * L), BF),
            pltpu.VMEM((L, L), F32),
            pltpu.VMEM((L, L), F32),
            pltpu.SemaphoreType.DMA((20,)),
        ],
        compiler_params=pltpu.CompilerParams(vmem_limit_bytes=LIMIT),
        cost_estimate=pl.CostEstimate(flops=4_000_000_000, bytes_accessed=6 * MB, transcendentals=0),
        name="search_templates",
    )(spec, *owns, *others, TAB["inverse_cols"], TAB["inverse_rows"], TAB["reverse"])


def ring(count, step):
    return [(i, (i + step) % count) for i in range(count)]


def body(micrograph, templates, ref_bank, peak_offsets, peak_template, owners):
    def across(array):
        return lax.ppermute(array, "core", ring(2, 1))

    message, spec = prepare(
        peak_offsets.T, peak_template.reshape(1, 16), owners.reshape(1, 16), micrograph, ref_bank
    )
    arrived = lax.all_to_all(message, CHIPS, 0, 0, tiled=True)
    half = template_half(templates)
    near = lax.ppermute(half, "zl", ring(2, 1))
    arrived, half, near = lax.optimization_barrier((arrived, half, near))
    both = jnp.stack([half, near])
    owns = [both] + [lax.ppermute(both, "y", ring(4, step)) for step in (1, 3, 2)]
    scores = refine(arrived, across(arrived))
    after, owns = lax.optimization_barrier((scores, owns))
    returned = lax.all_to_all(scores.reshape(SLABS, 2, 128), CHIPS, 0, 0, tiled=True)
    mip, zmap = search(spec, owns, [across(one) for one in owns])
    returned, mip, zmap, after = lax.optimization_barrier((returned, mip, zmap, after))
    refined = jnp.sum(returned, 0).reshape(16, 16)[:, :9]
    return (mip, zmap, refined)


def solution(mesh):
    inner = Mesh(mesh.devices.reshape(2, 4, 4, 2, 2), ("zl", "y", "x", "zh", "core"))
    every = ROWS_OF + COLS_OF
    placed = (
        P(ROWS_OF, COLS_OF),
        P(ROWS_OF, None, None),
        P(COLS_OF, None, None),
        P(every, None),
        P(every),
        P(every, None),
    )
    return jax.shard_map(
        body,
        mesh=inner,
        in_specs=placed,
        out_specs=(P(ROWS_OF, COLS_OF), P(ROWS_OF, COLS_OF), P(every, None)),
        check_vma=False,
    )
```

time: 75.4 us -> 70 us (0.928)
  blocking collectives: 24.8 us -> 0 us
  starting transfers between devices: 12.2 us -> 26 us
  waiting for transfers between devices: 2.23 us -> 12 us
  Pallas kernels: 31.8 us -> 27.4 us
    all_to_all x1 -> x0, blocking collectives: 24.8 us -> none  [body(): arrived = lax.all_to_all(message, CHIPS, 0, 0, tiled=True)]
    ppermute x0 -> x4, waiting for transfers between devices: none -> 11.9 us  [the longest x1 9.92 us: body(): near = lax.ppermute(half, 'zl', ring(2, 1))]
    all_to_all x1, starting transfers between devices: 3.56 us -> 12 us  [body(): arrived = lax.all_to_all(message, CHIPS, 0, 0, tiled=True)]
    ppermute x0 -> x4, starting transfers between devices: none -> 4.1 us  [the longest x3 2.91 us: body(): lax.ppermute(both, 'y', ring(4, step))]
    pallas_call x1, Pallas kernels: 11 us -> 8.67 us  [search(): pl.pallas_call(search_kernel, out_shape=(jax.ShapeDtypeStruct((L, L), F32...]
    all_to_all x1, starting transfers between devices: 5.21 us -> 7.47 us  [body(): lax.all_to_all(scores.reshape(SLABS, 2, 128), CHIPS, 0, 0, tiled=True)]
    all_to_all x1, waiting for transfers between devices: 2.22 us -> 0.01 us  [body(): arrived = lax.all_to_all(message, CHIPS, 0, 0, tiled=True)]
    pallas_call x1, Pallas kernels: 6.74 us -> 4.69 us  [prepare(): pl.pallas_call(prepare_kernel, out_shape=(jax.ShapeDtypeStruct((SLABS, RO...]
  transfers between devices with their start and end apart: 4 -> 11, of which waited for: 1 -> 2; matrix products, arithmetic and copies ran while one was open for 0% -> 1% of each run, Pallas kernels for 33% -> 33%
where the time goes in v2:
time: 70 us; the launch traced here: 69.6 us
  Pallas kernels  27.4 us (39%)
  starting transfers between devices  26 us (37%)
  waiting for transfers between devices  12 us (17%)
  local copies, waits for them, and re-layouts  2.49 us (4%)
  other arithmetic  1.02 us (1%)
  between operations  0.82 us (1%)
    all_to_all x1, starting transfers between devices, body(): arrived = lax.all_to_all(message, CHIPS, 0, 0, tiled=True)  12 us
    pallas_call x1, Pallas kernels, refine(): pl.pallas_call(refine_kernel, out_shape=jax.ShapeDtypeStruct((128, 128),...  11.1 us
    ppermute x1, waiting for transfers between devices, body(): near = lax.ppermute(half, 'zl', ring(2, 1))  9.92 us
    pallas_call x1, Pallas kernels, search(): pl.pallas_call(search_kernel, out_shape=(jax.ShapeDtypeStruct((L, L), F32...  8.67 us
    all_to_all x1, starting transfers between devices, body(): lax.all_to_all(scores.reshape(SLABS, 2, 128), CHIPS, 0, 0, tiled=True)  7.47 us
    pallas_call x1, Pallas kernels, prepare(): pl.pallas_call(prepare_kernel, out_shape=(jax.ShapeDtypeStruct((SLABS, RO...  4.69 us
    ppermute x3, starting transfers between devices, body(): lax.ppermute(both, 'y', ring(4, step))  2.91 us
    pallas_call x1, Pallas kernels, template_half(): pl.pallas_call(template_kernel, out_shape=jax.ShapeDtypeStruct((2, Q, L),...  2.9 us
  transfers between devices with their start and end apart: 11, of which 2 were waited for; matrix products, arithmetic and copies ran while one was open for 1% of the time, Pallas kernels for 33%

profile of v2, /device:TPU:1, one launch (start us, length us, event | category | flops | bytes accessed | tf_op | source)
XLA Modules:
  0.0 69.6 jit_solution(9122700630923337358)
XLA Ops:
  0.6 4.7 %prepare_spectra.1 = (bf16[64,40,128]{2,1,0:T(8,128)(2,1)}, bf16[2,192,384]{2,1,0:T(8,128)(2,1)}) custom-call(s32[2,16]{1,0:T(2,128)} %bitcast.11, s32[1,16]{1,0:T(1,128)} %bitcast.12, s32[1,16]{1,0:T(1,128)} %bitcast.13, bf16[384,384]{1,0:T(8,128)(2,1)} %tile_hbm.1, bf16[8,384,384]{2,1,0:T(8,128)(2,1)} %bank_hbm.1, ...), custom_call_target="tpu_custom_call" | custom-call | flops 1000000000 | bytes 4194304 | tf_op jit(solution)/shard_map/prepare_spectra/pallas_call | solution.py:212
  5.3 12.0 %all-to-all-start = ((bf16[64,40,128]{2,1,0:T(8,128)(2,1)}), bf16[64,40,128]{2,1,0:T(8,128)(2,1)S(1)}, u32[]{:S(2)}, u32[]{:S(2)}) async-start(bf16[64,40,128]{2,1,0:T(8,128)(2,1)} %get-tuple-element.17), calls=%async_computation | async-start | bytes 1310720 | tf_op jit(solution)/shard_map/all_to_all | solution.py:578
  17.3 2.9 %template_spectrum.1 = bf16[2,96,384]{2,1,0:T(8,128)(2,1)} custom-call(bf16[1,384,384]{2,1,0:T(8,128)(2,1)} %template_hbm.1, bf16[2,192,384]{2,1,0:T(8,128)(2,1)} %constant.31.clone.halves_hbm, bf16[384,768]{1,0:T(8,128)(2,1)} %constant.29.clone.pair_hbm), custom_call_target="tpu_custom_call" | custom-call | flops 400000000 | bytes 4194304 | tf_op jit(solution)/shard_map/template_spectrum/pallas_call | solution.py:259
  20.2 1.2 %collective-permute-start = (bf16[2,96,384]{2,1,0:T(8,128)(2,1)}, bf16[2,96,384]{2,1,0:T(8,128)(2,1)S(1)}, u32[]{:S(2)}, u32[]{:S(2)}) collective-permute-start(bf16[2,96,384]{2,1,0:T(8,128)(2,1)} %template_spectrum.1), channel_id=1, source_target_pairs={{0,64},{64,0},{1,65},{65,1},{2,66},{66,2},{3,67},{67,3},{4,68},{68... | collective-permute-start | bytes 442376 | tf_op jit(solution)/shard_map/ppermute | solution.py:580
  21.4 9.9 %collective-permute-done = bf16[2,96,384]{2,1,0:T(8,128)(2,1)S(1)} collective-permute-done((bf16[2,96,384]{2,1,0:T(8,128)(2,1)}, bf16[2,96,384]{2,1,0:T(8,128)(2,1)S(1)}, u32[]{:S(2)}, u32[]{:S(2)}) %collective-permute-start) | collective-permute-done | bytes 147488 | tf_op jit(solution)/shard_map/ppermute | solution.py:580
  31.3 1.4 %collective-permute-start.1 = (bf16[64,40,128]{2,1,0:T(8,128)(2,1)S(1)}, bf16[64,40,128]{2,1,0:T(8,128)(2,1)S(1)}, u32[]{:S(2)}, u32[]{:S(2)}) collective-permute-start(bf16[64,40,128]{2,1,0:T(8,128)(2,1)S(1)} %all-to-all-done.own_hbm), channel_id=1, source_target_pairs={{0,1},{1,0},{2,3},{3,2},{4,5},{5,4},{6,7},{7,6},{8,9},{9,8},{10,11... | collective-permute-start | bytes 1966088 | tf_op jit(solution)/shard_map/ppermute | solution.py:573
  32.7 0.9 %pad_maximum_fusion.o0 = bf16[2,2,96,384]{3,2,1,0:T(8,128)(2,1)S(1)} fusion(bf16[1,2,96,384]{3,2,1,0:T(8,128)(2,1)S(1)} %bitcast.8, bf16[1,2,96,384]{3,2,1,0:T(8,128)(2,1)} %bitcast.7), kind=kLoop, calls=%fused_computation | loop fusion | flops 147456 | bytes 589824 | tf_op jit(solution)/shard_map/stack | solution.py:582
  33.7 1.3 %collective-permute-start.4 = (bf16[2,2,96,384]{3,2,1,0:T(8,128)(2,1)S(1)}, bf16[2,2,96,384]{3,2,1,0:T(8,128)(2,1)S(1)}, u32[]{:S(2)}, u32[]{:S(2)}) collective-permute-start(bf16[2,2,96,384]{3,2,1,0:T(8,128)(2,1)S(1)} %pad_maximum_fusion.o0), channel_id=1, source_target_pairs={{0,32},{16,48},{32,0},{48,16},{1,33},{17,49},{33,1},{49,17},{2,34}... | collective-permute-start | bytes 884744 | tf_op jit(solution)/shard_map/ppermute | solution.py:583
  35.0 1.6 %collective-permute-start.3 = (bf16[2,2,96,384]{3,2,1,0:T(8,128)(2,1)S(1)}, bf16[2,2,96,384]{3,2,1,0:T(8,128)(2,1)}, u32[]{:S(2)}, u32[]{:S(2)}) collective-permute-start(bf16[2,2,96,384]{3,2,1,0:T(8,128)(2,1)S(1)} %pad_maximum_fusion.o0), channel_id=1, source_target_pairs={{0,48},{16,0},{32,16},{48,32},{1,49},{17,1},{33,17},{49,33},{2,50}... | collective-permute-start | bytes 884744 | tf_op jit(solution)/shard_map/ppermute | solution.py:583
  36.6 0.9 %copy-done.2 = bf16[64,40,128]{2,1,0:T(8,128)(2,1)} copy-done((bf16[64,40,128]{2,1,0:T(8,128)(2,1)}, bf16[64,40,128]{2,1,0:T(8,128)(2,1)S(1)}, u32[]{:S(2)}) %copy-start.2) | copy-done | bytes 655384
  37.5 11.1 %refine_slab.1 = f32[128,128]{1,0:T(8,128)} custom-call(bf16[64,40,128]{2,1,0:T(8,128)(2,1)} %copy-done, bf16[64,40,128]{2,1,0:T(8,128)(2,1)} %copy-done.2, bf16[384,768]{1,0:T(8,128)(2,1)} %constant.29.clone.pair_hbm, bf16[128,384]{1,0:T(8,128)(2,1)} %constant.32.clone.field_hbm, bf16[2304,128]{1,0:T(8,128)(2,1)} %constant.33.clone.comb_hbm, ...), custom_call_target="tpu_custom_call" | custom-call | flops 8999999488 | bytes 4194304 | tf_op jit(solution)/shard_map/refine_slab/pallas_call | solution.py:409
  48.6 2.0 %collective-permute-done.2.o1 = bf16[2,2,96,384]{3,2,1,0:T(8,128)(2,1)} collective-permute-done((bf16[2,2,96,384]{3,2,1,0:T(8,128)(2,1)S(1)}, bf16[2,2,96,384]{3,2,1,0:T(8,128)(2,1)}, u32[]{:S(2)}, u32[]{:S(2)}) %collective-permute-start.2) | collective-permute-done | bytes 294944 | tf_op jit(solution)/shard_map/ppermute | solution.py:583
  50.6 0.5 collective-permute-start.5
  51.1 0.0 collective-permute-start.6
  51.1 0.5 collective-permute-start.7
  51.6 0.0 collective-permute-start.8
  51.7 7.5 %all-to-all-start.1 = ((f32[64,2,128]{2,1,0:T(2,128)}), f32[64,2,128]{2,1,0:T(2,128)S(1)}, u32[]{:S(2)}, u32[]{:S(2)}) async-start(f32[64,2,128]{2,1,0:T(2,128)} %bitcast.9), calls=%async_computation.1 | async-start | bytes 131072 | tf_op jit(solution)/shard_map/all_to_all | solution.py:586
  59.2 0.6 copy-done.4
  59.9 0.1 copy-done.5
  60.0 0.1 copy-done.6
  60.1 0.1 copy-done.7
  60.2 8.7 %search_templates.1 = (f32[384,384]{1,0:T(8,128)}, f32[384,384]{1,0:T(8,128)}) custom-call(bf16[2,192,384]{2,1,0:T(8,128)(2,1)} %get-tuple-element.19.spec_hbm, bf16[2,2,96,384]{3,2,1,0:T(8,128)(2,1)} %copy-done.1, bf16[2,2,96,384]{3,2,1,0:T(8,128)(2,1)} %collective-permute-done.2.o1, bf16[2,2,96,384]{3,2,1,0:T(8,128)(2,1)} %collective-permute-done.3.o2, ...), custom_call_target="tpu_custom_call" | custom-call | flops 4000000000 | bytes 6291456 | tf_op jit(solution)/shard_map/search_templates/pallas_call | solution.py:541
  68.9 0.1 reduce_sum.9
  68.9 0.7 reshape.21
  (21 shorter events, 0.0 us)
Async XLA Ops:
  5.3 26.0 %all-to-all-start = ((bf16[64,40,128]{2,1,0:T(8,128)(2,1)}), bf16[64,40,128]{2,1,0:T(8,128)(2,1)S(1)}, u32[]{:S(2)}, u32[]{:S(2)}) async-start(bf16[64,40,128]{2,1,0:T(8,128)(2,1)} %get-tuple-element.17), calls=%async_computation | async-start | bytes 1310720 | tf_op jit(solution)/shard_map/all_to_all | solution.py:578
  20.2 11.1 %collective-permute-start = (bf16[2,96,384]{2,1,0:T(8,128)(2,1)}, bf16[2,96,384]{2,1,0:T(8,128)(2,1)S(1)}, u32[]{:S(2)}, u32[]{:S(2)}) collective-permute-start(bf16[2,96,384]{2,1,0:T(8,128)(2,1)} %template_spectrum.1), channel_id=1, source_target_pairs={{0,64},{64,0},{1,65},{65,1},{2,66},{66,2},{3,67},{67,3},{4,68},{68... | collective-permute-start | bytes 442376 | tf_op jit(solution)/shard_map/ppermute | solution.py:580
  31.3 5.3 %copy-start = (bf16[64,40,128]{2,1,0:T(8,128)(2,1)}, bf16[64,40,128]{2,1,0:T(8,128)(2,1)S(1)}, u32[]{:S(2)}) copy-start(bf16[64,40,128]{2,1,0:T(8,128)(2,1)S(1)} %all-to-all-done.own_hbm) | copy-start | bytes 1966084
  31.3 5.3 %collective-permute-start.1 = (bf16[64,40,128]{2,1,0:T(8,128)(2,1)S(1)}, bf16[64,40,128]{2,1,0:T(8,128)(2,1)S(1)}, u32[]{:S(2)}, u32[]{:S(2)}) collective-permute-start(bf16[64,40,128]{2,1,0:T(8,128)(2,1)S(1)} %all-to-all-done.own_hbm), channel_id=1, source_target_pairs={{0,1},{1,0},{2,3},{3,2},{4,5},{5,4},{6,7},{7,6},{8,9},{9,8},{10,11... | collective-permute-start | bytes 1966088 | tf_op jit(solution)/shard_map/ppermute | solution.py:573
  33.7 17.0 %copy-start.1 = (bf16[2,2,96,384]{3,2,1,0:T(8,128)(2,1)}, bf16[2,2,96,384]{3,2,1,0:T(8,128)(2,1)S(1)}, u32[]{:S(2)}) copy-start(bf16[2,2,96,384]{3,2,1,0:T(8,128)(2,1)S(1)} %pad_maximum_fusion.o0) | copy-start | bytes 884740
  33.7 14.9 %collective-permute-start.4 = (bf16[2,2,96,384]{3,2,1,0:T(8,128)(2,1)S(1)}, bf16[2,2,96,384]{3,2,1,0:T(8,128)(2,1)S(1)}, u32[]{:S(2)}, u32[]{:S(2)}) collective-permute-start(bf16[2,2,96,384]{3,2,1,0:T(8,128)(2,1)S(1)} %pad_maximum_fusion.o0), channel_id=1, source_target_pairs={{0,32},{16,48},{32,0},{48,16},{1,33},{17,49},{33,1},{49,17},{2,34}... | collective-permute-start | bytes 884744 | tf_op jit(solution)/shard_map/ppermute | solution.py:583
  35.0 13.7 %collective-permute-start.3 = (bf16[2,2,96,384]{3,2,1,0:T(8,128)(2,1)S(1)}, bf16[2,2,96,384]{3,2,1,0:T(8,128)(2,1)}, u32[]{:S(2)}, u32[]{:S(2)}) collective-permute-start(bf16[2,2,96,384]{3,2,1,0:T(8,128)(2,1)S(1)} %pad_maximum_fusion.o0), channel_id=1, source_target_pairs={{0,48},{16,0},{32,16},{48,32},{1,49},{17,1},{33,17},{49,33},{2,50}... | collective-permute-start | bytes 884744 | tf_op jit(solution)/shard_map/ppermute | solution.py:583
  36.6 14.0 %collective-permute-start.2 = (bf16[2,2,96,384]{3,2,1,0:T(8,128)(2,1)S(1)}, bf16[2,2,96,384]{3,2,1,0:T(8,128)(2,1)}, u32[]{:S(2)}, u32[]{:S(2)}) collective-permute-start(bf16[2,2,96,384]{3,2,1,0:T(8,128)(2,1)S(1)} %pad_maximum_fusion.o0), channel_id=1, source_target_pairs={{0,16},{16,32},{32,48},{48,0},{1,17},{17,33},{33,49},{49,1},{2,18}... | collective-permute-start | bytes 884744 | tf_op jit(solution)/shard_map/ppermute | solution.py:583
  36.6 0.9 %copy-start.2 = (bf16[64,40,128]{2,1,0:T(8,128)(2,1)}, bf16[64,40,128]{2,1,0:T(8,128)(2,1)S(1)}, u32[]{:S(2)}) copy-start(bf16[64,40,128]{2,1,0:T(8,128)(2,1)S(1)} %collective-permute-done.1.other_hbm) | copy-start | bytes 1966084
  48.6 10.6 %copy-start.3 = (bf16[2,2,96,384]{3,2,1,0:T(8,128)(2,1)}, bf16[2,2,96,384]{3,2,1,0:T(8,128)(2,1)S(1)}, u32[]{:S(2)}) copy-start(bf16[2,2,96,384]{3,2,1,0:T(8,128)(2,1)S(1)} %collective-permute-done.4.o3) | copy-start | bytes 884740
  50.6 8.5 %collective-permute-start.5 = (bf16[2,2,96,384]{3,2,1,0:T(8,128)(2,1)S(1)}, bf16[2,2,96,384]{3,2,1,0:T(8,128)(2,1)S(1)}, u32[]{:S(2)}, u32[]{:S(2)}) collective-permute-start(bf16[2,2,96,384]{3,2,1,0:T(8,128)(2,1)S(1)} %pad_maximum_fusion.o0), channel_id=1, source_target_pairs={{0,1},{1,0},{2,3},{3,2},{4,5},{5,4},{6,7},{7,6},{8,9},{9,8},{10,11... | collective-permute-start | bytes 884744 | tf_op jit(solution)/shard_map/ppermute | solution.py:573
  51.1 8.0 %collective-permute-start.6 = (bf16[2,2,96,384]{3,2,1,0:T(8,128)(2,1)}, bf16[2,2,96,384]{3,2,1,0:T(8,128)(2,1)S(1)}, u32[]{:S(2)}, u32[]{:S(2)}) collective-permute-start(bf16[2,2,96,384]{3,2,1,0:T(8,128)(2,1)} %collective-permute-done.2.o1), channel_id=1, source_target_pairs={{0,1},{1,0},{2,3},{3,2},{4,5},{5,4},{6,7},{7,6},{8,9},{9,8},{10,11... | collective-permute-start | bytes 884744 | tf_op jit(solution)/shard_map/ppermute | solution.py:573
  51.1 8.0 %collective-permute-start.7 = (bf16[2,2,96,384]{3,2,1,0:T(8,128)(2,1)}, bf16[2,2,96,384]{3,2,1,0:T(8,128)(2,1)S(1)}, u32[]{:S(2)}, u32[]{:S(2)}) collective-permute-start(bf16[2,2,96,384]{3,2,1,0:T(8,128)(2,1)} %collective-permute-done.3.o2), channel_id=1, source_target_pairs={{0,1},{1,0},{2,3},{3,2},{4,5},{5,4},{6,7},{7,6},{8,9},{9,8},{10,11... | collective-permute-start | bytes 884744 | tf_op jit(solution)/shard_map/ppermute | solution.py:573
  51.6 7.6 %collective-permute-start.8 = (bf16[2,2,96,384]{3,2,1,0:T(8,128)(2,1)S(1)}, bf16[2,2,96,384]{3,2,1,0:T(8,128)(2,1)S(1)}, u32[]{:S(2)}, u32[]{:S(2)}) collective-permute-start(bf16[2,2,96,384]{3,2,1,0:T(8,128)(2,1)S(1)} %collective-permute-done.4.o3), channel_id=1, source_target_pairs={{0,1},{1,0},{2,3},{3,2},{4,5},{5,4},{6,7},{7,6},{8,9},{9,8},{10,11... | collective-permute-start | bytes 884744 | tf_op jit(solution)/shard_map/ppermute | solution.py:573
  51.7 17.2 %all-to-all-start.1 = ((f32[64,2,128]{2,1,0:T(2,128)}), f32[64,2,128]{2,1,0:T(2,128)S(1)}, u32[]{:S(2)}, u32[]{:S(2)}) async-start(f32[64,2,128]{2,1,0:T(2,128)} %bitcast.9), calls=%async_computation.1 | async-start | bytes 131072 | tf_op jit(solution)/shard_map/all_to_all | solution.py:586
  59.2 0.7 %copy-start.4 = (bf16[2,2,96,384]{3,2,1,0:T(8,128)(2,1)}, bf16[2,2,96,384]{3,2,1,0:T(8,128)(2,1)S(1)}, u32[]{:S(2)}) copy-start(bf16[2,2,96,384]{3,2,1,0:T(8,128)(2,1)S(1)} %collective-permute-done.5.p0) | copy-start | bytes 884740
  59.2 0.8 %copy-start.5 = (bf16[2,2,96,384]{3,2,1,0:T(8,128)(2,1)}, bf16[2,2,96,384]{3,2,1,0:T(8,128)(2,1)S(1)}, u32[]{:S(2)}) copy-start(bf16[2,2,96,384]{3,2,1,0:T(8,128)(2,1)S(1)} %collective-permute-done.6.p1) | copy-start | bytes 884740
  59.2 0.9 %copy-start.6 = (bf16[2,2,96,384]{3,2,1,0:T(8,128)(2,1)}, bf16[2,2,96,384]{3,2,1,0:T(8,128)(2,1)S(1)}, u32[]{:S(2)}) copy-start(bf16[2,2,96,384]{3,2,1,0:T(8,128)(2,1)S(1)} %collective-permute-done.7.p2) | copy-start | bytes 884740
  59.2 0.9 %copy-start.7 = (bf16[2,2,96,384]{3,2,1,0:T(8,128)(2,1)}, bf16[2,2,96,384]{3,2,1,0:T(8,128)(2,1)S(1)}, u32[]{:S(2)}) copy-start(bf16[2,2,96,384]{3,2,1,0:T(8,128)(2,1)S(1)} %collective-permute-done.8.p3) | copy-start | bytes 884740

commit v3 on v2

--- a/solution.py
+++ b/solution.py
@@ -40,7 +40,8 @@
 def make_tables():
     n = np.arange(L)
     cos, sin = wave(n, n)
-    forward = np.concatenate([cos[:H], cos[H : H + 1], sin[1:H]], 0)
+    order = np.concatenate([np.arange(0, H, 2), np.arange(1, H, 2)])
+    forward = np.concatenate([cos[order], cos[H : H + 1], sin[order[1:]]], 0)
     halves = np.stack(
         [np.concatenate([forward[c * Q : c * Q + Q], forward[H + c * Q : H + c * Q + Q]], 0) for c in range(2)]
     )
@@ -48,8 +49,11 @@
     inverse_cols = np.concatenate([pair, np.concatenate([-sin, cos], 1)], 0)
     weight = np.full((H,), 2.0)
     weight[0] = 1.0
-    inverse_rows = np.concatenate([cos[:, :H] * weight, -2.0 * sin[:, :H]], 1)
-    inverse_rows[:, H] = cos[:, H]
+    back_cos, back_sin = cos[:H, order] * weight, -2.0 * sin[:H, order]
+    back_sin[:, 0] = cos[:H, H]
+    inverse_rows = np.stack(
+        [np.concatenate([back_cos[:, Q * c : Q * c + Q], back_sin[:, Q * c : Q * c + Q]], 1) for c in range(2)]
+    )
     reverse = np.zeros((L, L))
     reverse[(-n) % L, n] = 1.0
     pick = np.zeros((4, L, 128))
@@ -85,7 +89,7 @@
         widen[128 + 6 * part : 128 + 6 * part + 6, 4 + part] = 1.0
     for s in range(SLABS):
         for part in range(4):
-            k = s + 64 * part if part < 3 else H
+            k = order[s + 64 * part] if part < 3 else H
             kc, ks = wave([k], n)
             turn[s, part], turn[s, 4 + part] = kc[0], ks[0]
             ca, sa = wave([k], a)
@@ -227,7 +231,7 @@
             pltpu.VMEM((4 * L, 128), BF),
             pltpu.SemaphoreType.DMA((5,)),
         ],
-        compiler_params=pltpu.CompilerParams(vmem_limit_bytes=LIMIT),
+        compiler_params=pltpu.CompilerParams(vmem_limit_bytes=62 * MB),
         cost_estimate=pl.CostEstimate(flops=1_000_000_000, bytes_accessed=4 * MB, transcendentals=0),
         name="prepare_spectra",
     )(offsets, choice, owners, tile, bank, TAB["forward"], TAB["pair"], TAB["pick"])
@@ -268,7 +272,7 @@
             pltpu.VMEM((L, 2 * L), BF),
             pltpu.SemaphoreType.DMA((3,)),
         ],
-        compiler_params=pltpu.CompilerParams(vmem_limit_bytes=LIMIT),
+        compiler_params=pltpu.CompilerParams(vmem_limit_bytes=36 * MB),
         cost_estimate=pl.CostEstimate(flops=400_000_000, bytes_accessed=4 * MB, transcendentals=0),
         name="template_spectrum",
     )(templates, TAB["halves"], TAB["pair"])
@@ -285,12 +289,12 @@
 ):
     slab = place()[2]
     jobs = (
-        (other_hbm, other),
-        (own_hbm, own),
         (pair_hbm, pair),
         (widen_hbm, widen),
         (turn_hbm.at[pl.ds(slab, 1)], turn),
         (extra_hbm.at[pl.ds(slab, 1)], extra),
+        (other_hbm, other),
+        (own_hbm, own),
         (field_hbm, field),
         (comb_hbm, comb),
         (last_hbm.at[pl.ds(slab, 1)], last),
@@ -313,21 +317,13 @@
         return line
 
     copies[0].wait()
-    flat[...] = other[...].astype(F32).reshape(SLABS * ROWS, 128)
-    spread(18, refs, slice(64, 128))
-    copies[1].wait()
-    flat[...] = own[...].astype(F32).reshape(SLABS * ROWS, 128)
-    spread(18, refs, slice(0, 64))
-    meta = spread(0, tiles, slice(0, 64)).astype(BF)
-
-    copies[2].wait()
     waves[:, : 2 * L] = pair[...]
     wanted = (iota((L, 128), 0) == iota((L, 128), 1) + 6 * slab).astype(BF)
     waves[:, 768:896] = dot(pair[:, :L], wanted).astype(BF)
     waves[:, 896:1024] = dot(pair[:, L:], wanted).astype(BF)
+    copies[1].wait()
+    copies[2].wait()
     copies[3].wait()
-    copies[4].wait()
-    copies[5].wait()
     turns = dot(widen[...], turn[0]).astype(BF)
     pad = jnp.zeros((112, 128), BF)
     ends = jnp.concatenate(
@@ -340,6 +336,14 @@
         0,
     )
 
+    copies[4].wait()
+    flat[...] = other[...].astype(F32).reshape(SLABS * ROWS, 128)
+    spread(18, refs, slice(64, 128))
+    copies[5].wait()
+    flat[...] = own[...].astype(F32).reshape(SLABS * ROWS, 128)
+    spread(18, refs, slice(0, 64))
+    meta = spread(0, tiles, slice(0, 64)).astype(BF)
+
     block = 256
     rowb = iota((block, 128), 0)
     laneb = iota((block, 128), 1)
@@ -354,32 +358,32 @@
         hot_x = jnp.concatenate([(lanef + 128.0 * j == spots[:, :128]).astype(BF) for j in range(3)], 1)
         hot_y = jnp.concatenate([(lanef + 128.0 * j == spots[:, 128:256]).astype(BF) for j in range(3)], 1)
         hot_t = (lanef == spots[:, 256:]).astype(BF)
-        ref_of[rows, :] = dot(hot_t, refs[...]).astype(BF)
-        wave_of[rows, :] = dot(hot_y, waves[...]).astype(BF)
+        ref_of[rows, :] = dot(hot_t, refs[...])
+        wave_of[rows, :] = dot(hot_y, waves[...])
         turned[rows, :] = lax.dot_general(
             hot_x, turns, (((1,), (1,)), ((), ())), preferred_element_type=F32
         ).astype(BF)
 
     def multiply(q):
-        eight = pl.ds(8 * q, 8)
         for size, wave_at, places in (
             (L, 0, tuple((L * part, 3 * L + L * part) for part in range(3))),
             (128, 2 * L, ((MAIN, MAIN + 128),)),
         ):
-            for at_r, at_i in places:
-                tiles_r = tiles[eight, at_r : at_r + size]
-                tiles_i = tiles[eight, at_i : at_i + size]
-                for j in range(8):
-                    rows = pl.ds(128 * q + 16 * j, 16)
-                    cos_y = wave_of[rows, wave_at : wave_at + size].astype(F32)
-                    sin_y = wave_of[rows, wave_at + size : wave_at + 2 * size].astype(F32)
-                    tile_r, tile_i = tiles_r[j : j + 1], tiles_i[j : j + 1]
-                    ref_r = ref_of[rows, at_r : at_r + size].astype(F32)
-                    ref_i = ref_of[rows, at_i : at_i + size].astype(F32)
-                    prod_r = tile_r * ref_r + tile_i * ref_i
-                    prod_i = tile_i * ref_r - tile_r * ref_i
-                    both[rows, at_r : at_r + size] = (prod_r * cos_y - prod_i * sin_y).astype(BF)
-                    both[rows, at_i : at_i + size] = (prod_r * sin_y + prod_i * cos_y).astype(BF)
+            for j in range(8):
+                rows = pl.ds(128 * q + 16 * j, 16)
+                for m in range(0, size, 128):
+                    cos_y = wave_of[rows, wave_at + m : wave_at + m + 128].astype(F32)
+                    sin_y = wave_of[rows, wave_at + size + m : wave_at + size + m + 128].astype(F32)
+                    for at_r, at_i in places:
+                        lanes_r, lanes_i = slice(at_r + m, at_r + m + 128), slice(at_i + m, at_i + m + 128)
+                        tile_r = tiles[8 * q + j : 8 * q + j + 1, lanes_r]
+                        tile_i = tiles[8 * q + j : 8 * q + j + 1, lanes_i]
+                        ref_r = ref_of[rows, lanes_r].astype(F32)
+                        ref_i = ref_of[rows, lanes_i].astype(F32)
+                        prod_r = tile_r * ref_r + tile_i * ref_i
+                        prod_i = tile_i * ref_r - tile_r * ref_i
+                        both[rows, lanes_r] = (prod_r * cos_y - prod_i * sin_y).astype(BF)
+                        both[rows, lanes_i] = (prod_r * sin_y + prod_i * cos_y).astype(BF)
 
     kept = (laneb >> 4) == (rowb & 7)
 
@@ -410,7 +414,7 @@
         refine_kernel,
         out_shape=jax.ShapeDtypeStruct((128, 128), F32),
         grid=(1,),
-        in_specs=[held] * 9,
+        in_specs=[pl.BlockSpec(memory_space=pl.ANY)] * 2 + [held] * 7,
         out_specs=full_spec((128, 128)),
         scratch_shapes=[
             pltpu.VMEM((SLABS, ROWS, 128), BF),
@@ -426,13 +430,13 @@
             pltpu.VMEM((SLABS, MAIN + 256), F32),
             pltpu.VMEM((128, MAIN + 256), BF),
             pltpu.VMEM((L, 1024), BF),
-            pltpu.VMEM((N_CAND, MAIN + 256), BF),
-            pltpu.VMEM((N_CAND, 1024), BF),
+            pltpu.VMEM((N_CAND, MAIN + 256), F32),
+            pltpu.VMEM((N_CAND, 1024), F32),
             pltpu.VMEM((N_CAND, MAIN + 256), BF),
             pltpu.VMEM((N_CAND, 256), BF),
             pltpu.SemaphoreType.DMA((9,)),
         ],
-        compiler_params=pltpu.CompilerParams(vmem_limit_bytes=LIMIT),
+        compiler_params=pltpu.CompilerParams(vmem_limit_bytes=62 * MB),
         cost_estimate=pl.CostEstimate(flops=9_000_000_000, bytes_accessed=4 * MB, transcendentals=0),
         name="refine_slab",
     )(own, other, TAB["pair"], TAB["field"], TAB["comb"], TAB["widen"], TAB["turn"], TAB["extra"], TAB["last"])
@@ -511,29 +515,32 @@
             copies[tops + 5 + 2 * p].wait()
             products(p + 1)
         middle = dot(prod[2 * p : 2 * p + 2].reshape(2 * H, 2 * L), cols[...]).astype(BF)
-        both = []
-        for k in range(2):
-            part = middle[H * k : H * k + H]
-            both.append(jnp.concatenate([part[:, :L], part[:, L:]], 0))
-        corr = dot(rows[...], jnp.concatenate(both, 1)) * (1.0 / (L * L))
-        one, two = corr[:, :L], corr[:, L:]
-        largest = jnp.maximum(one, two)
-        summed = one + two
-        powers = one * one + two * two
-        if p == 0:
-            mip[...] = largest
-            total[...] = summed
-            square[...] = powers
-        elif p < 3:
-            mip[...] = jnp.maximum(mip[...], largest)
-            total[...] += summed
-            square[...] += powers
-        else:
-            largest = jnp.maximum(mip[...], largest)
-            mean = (total[...] + summed) * 0.125
-            var = (square[...] + powers) * 0.125 - mean * mean
-            mip[...] = largest
-            zmap[...] = (largest - mean) * lax.rsqrt(jnp.maximum(var, 0.25))
+        kinds = []
+        for c in range(2):
+            both = []
+            for k in range(2):
+                part = middle[H * k + Q * c : H * k + Q * c + Q]
+                both.append(jnp.concatenate([part[:, :L], part[:, L:]], 0))
+            kinds.append(dot(rows[c], jnp.concatenate(both, 1)) * (1.0 / (L * L)))
+        for at, corr in ((slice(0, H), kinds[0] + kinds[1]), (slice(H, L), kinds[0] - kinds[1])):
+            one, two = corr[:, :L], corr[:, L:]
+            largest = jnp.maximum(one, two)
+            summed = one + two
+            powers = one * one + two * two
+            if p == 0:
+                mip[at] = largest
+                total[at] = summed
+                square[at] = powers
+            elif p < 3:
+                mip[at] = jnp.maximum(mip[at], largest)
+                total[at] += summed
+                square[at] += powers
+            else:
+                largest = jnp.maximum(mip[at], largest)
+                mean = (total[at] + summed) * 0.125
+                var = (square[at] + powers) * 0.125 - mean * mean
+                mip[at] = largest
+                zmap[at] = (largest - mean) * lax.rsqrt(jnp.maximum(var, 0.25))
 
 
 def search(spec, owns, others):
@@ -542,7 +549,7 @@
         search_kernel,
         out_shape=(jax.ShapeDtypeStruct((L, L), F32), jax.ShapeDtypeStruct((L, L), F32)),
         grid=(1,),
-        in_specs=[held] * 12,
+        in_specs=[held] + [pl.BlockSpec(memory_space=pl.ANY)] * 8 + [held] * 3,
         out_specs=[full_spec((L, L)), full_spec((L, L))],
         scratch_shapes=[
             pltpu.VMEM((2, H, L), BF),
@@ -551,14 +558,14 @@
             pltpu.VMEM((8, 2, 16, L), BF),
             pltpu.VMEM((8, 2, 16, L), BF),
             pltpu.VMEM((2 * L, 2 * L), BF),
-            pltpu.VMEM((L, L), BF),
+            pltpu.VMEM((2, H, H), BF),
             pltpu.VMEM((L, L), BF),
             pltpu.VMEM((8, H, 2 * L), BF),
             pltpu.VMEM((L, L), F32),
             pltpu.VMEM((L, L), F32),
             pltpu.SemaphoreType.DMA((20,)),
         ],
-        compiler_params=pltpu.CompilerParams(vmem_limit_bytes=LIMIT),
+        compiler_params=pltpu.CompilerParams(vmem_limit_bytes=56 * MB),
         cost_estimate=pl.CostEstimate(flops=4_000_000_000, bytes_accessed=6 * MB, transcendentals=0),
         name="search_templates",
     )(spec, *owns, *others, TAB["inverse_cols"], TAB["inverse_rows"], TAB["reverse"])
@@ -568,6 +575,11 @@
     return [(i, (i + step) % count) for i in range(count)]
 
 
+def z_ring(step):
+    index = [(z % 2) * 2 + z // 2 for z in range(4)]
+    return [(index[z], index[(z + step) % 4]) for z in range(4)]
+
+
 def body(micrograph, templates, ref_bank, peak_offsets, peak_template, owners):
     def across(array):
         return lax.ppermute(array, "core", ring(2, 1))
@@ -577,14 +589,21 @@
     )
     arrived = lax.all_to_all(message, CHIPS, 0, 0, tiled=True)
     half = template_half(templates)
-    near = lax.ppermute(half, "zl", ring(2, 1))
-    arrived, half, near = lax.optimization_barrier((arrived, half, near))
-    both = jnp.stack([half, near])
-    owns = [both] + [lax.ppermute(both, "y", ring(4, step)) for step in (1, 3, 2)]
+    along = [lax.ppermute(half, "y", ring(4, step)) for step in (1, 3, 2)]
+    arrived, half, along = lax.optimization_barrier((arrived, half, along))
+    lower, upper = jnp.stack([half, along[0]]), jnp.stack(along[1:])
+    owns = [
+        lower,
+        upper,
+        lax.ppermute(lower, ("zl", "zh"), z_ring(1)),
+        lax.ppermute(upper, ("zl", "zh"), z_ring(3)),
+    ]
     scores = refine(arrived, across(arrived))
-    after, owns = lax.optimization_barrier((scores, owns))
+    first = [across(one) for one in owns[:2]]
+    after, last = lax.optimization_barrier((scores, owns[2:]))
+    owns = owns[:2] + last
     returned = lax.all_to_all(scores.reshape(SLABS, 2, 128), CHIPS, 0, 0, tiled=True)
-    mip, zmap = search(spec, owns, [across(one) for one in owns])
+    mip, zmap = search(spec, owns, first + [across(one) for one in last])
     returned, mip, zmap, after = lax.optimization_barrier((returned, mip, zmap, after))
     refined = jnp.sum(returned, 0).reshape(16, 16)[:, :9]
     return (mip, zmap, refined)

time: 70 us -> 68.4 us (0.977)
  Pallas kernels: 27.4 us -> 24.5 us
  starting transfers between devices: 26 us -> 28.8 us
  other arithmetic: 1.02 us -> 0.15 us
    ppermute x4 -> x5, starting transfers between devices: 4.1 us -> 6.68 us  [the longest x3 4.07 us: body(): along = [lax.ppermute(half, 'y', ring(4, step)) for step in (1, 3, 2)]]
    pallas_call x1, Pallas kernels: 2.9 us -> 1.66 us  [template_half(): pl.pallas_call(template_kernel, out_shape=jax.ShapeDtypeStruct((2, Q, L),...]
    pallas_call x1, Pallas kernels: 11.1 us -> 10 us  [refine(): pl.pallas_call(refine_kernel, out_shape=jax.ShapeDtypeStruct((128, 128),...]
    another operation x1 -> x2, other arithmetic: 0.94 us -> 0.07 us  [body(): lower, upper = (jnp.stack([half, along[0]]), jnp.stack(along[1:]))]
    ppermute x4 -> x5, waiting for transfers between devices: 11.9 us -> 11.5 us  [the longest x3 11.5 us: body(): along = [lax.ppermute(half, 'y', ring(4, step)) for step in (1, 3, 2)]]
    unnamed x16 -> x18, local copies, waits for them, and re-layouts: 1.8 us -> 1.66 us
  transfers between devices with their start and end apart: 11 -> 12, of which waited for: 2 -> 3; matrix products, arithmetic and copies ran while one was open for 1% -> 0% of each run, Pallas kernels for 33% -> 29%
where the time goes in v3:
time: 68.4 us; the launch traced here: 68.1 us
  starting transfers between devices  28.8 us (42%)
  Pallas kernels  24.5 us (36%)
  waiting for transfers between devices  11.5 us (17%)
  local copies, waits for them, and re-layouts  2.34 us (3%)
  between operations  0.86 us (1%)
    all_to_all x1, starting transfers between devices, body(): arrived = lax.all_to_all(message, CHIPS, 0, 0, tiled=True)  12 us
    ppermute x3, waiting for transfers between devices, body(): along = [lax.ppermute(half, 'y', ring(4, step)) for step in (1, 3, 2)]  11.5 us
    pallas_call x1, Pallas kernels, refine(): pl.pallas_call(refine_kernel, out_shape=jax.ShapeDtypeStruct((128, 128),...  10 us
    all_to_all x1, starting transfers between devices, body(): lax.all_to_all(scores.reshape(SLABS, 2, 128), CHIPS, 0, 0, tiled=True)  8.14 us
    pallas_call x1, Pallas kernels, search(): pl.pallas_call(search_kernel, out_shape=(jax.ShapeDtypeStruct((L, L), F32...  8.09 us
    pallas_call x1, Pallas kernels, prepare(): pl.pallas_call(prepare_kernel, out_shape=(jax.ShapeDtypeStruct((SLABS, RO...  4.79 us
    ppermute x3, starting transfers between devices, body(): along = [lax.ppermute(half, 'y', ring(4, step)) for step in (1, 3, 2)]  4.07 us
    ppermute x1, starting transfers between devices, body(): lax.ppermute(upper, ('zl', 'zh'), z_ring(3))  2.6 us
  transfers between devices with their start and end apart: 12, of which 3 were waited for; matrix products, arithmetic and copies ran while one was open for 0% of the time, Pallas kernels for 29%

profile of v3, /device:TPU:1, one launch (start us, length us, event | category | flops | bytes accessed | tf_op | source)
XLA Modules:
  0.0 68.1 jit_solution(33688956482894361)
XLA Ops:
  0.6 0.0 copy-start
  0.7 4.8 %prepare_spectra.1 = (bf16[64,40,128]{2,1,0:T(8,128)(2,1)}, bf16[2,192,384]{2,1,0:T(8,128)(2,1)}) custom-call(s32[2,16]{1,0:T(2,128)} %bitcast.15, s32[1,16]{1,0:T(1,128)} %bitcast.16, s32[1,16]{1,0:T(1,128)} %bitcast.17, bf16[384,384]{1,0:T(8,128)(2,1)} %tile_hbm.1, bf16[8,384,384]{2,1,0:T(8,128)(2,1)} %bank_hbm.1, ...), custom_call_target="tpu_custom_call" | custom-call | flops 1000000000 | bytes 4194304 | tf_op jit(solution)/shard_map/prepare_spectra/pallas_call | solution.py:216
  5.5 12.0 %all-to-all-start = ((bf16[64,40,128]{2,1,0:T(8,128)(2,1)}), bf16[64,40,128]{2,1,0:T(8,128)(2,1)S(1)}, u32[]{:S(2)}, u32[]{:S(2)}) async-start(bf16[64,40,128]{2,1,0:T(8,128)(2,1)} %get-tuple-element.17), calls=%async_computation | async-start | bytes 1310720 | tf_op jit(solution)/shard_map/all_to_all | solution.py:590
  17.5 1.7 %template_spectrum.1 = bf16[2,96,384]{2,1,0:T(8,128)(2,1)S(1)} custom-call(bf16[1,384,384]{2,1,0:T(8,128)(2,1)S(1)} %copy-done.1, bf16[2,192,384]{2,1,0:T(8,128)(2,1)S(1)} %copy-done.2, bf16[384,768]{1,0:T(8,128)(2,1)S(1)} %copy-done), custom_call_target="tpu_custom_call" | custom-call | flops 400000000 | bytes 4194304 | tf_op jit(solution)/shard_map/template_spectrum/pallas_call | solution.py:263
  19.2 2.6 %collective-permute-start.2 = (bf16[2,96,384]{2,1,0:T(8,128)(2,1)S(1)}, bf16[2,96,384]{2,1,0:T(8,128)(2,1)S(1)}, u32[]{:S(2)}, u32[]{:S(2)}) collective-permute-start(bf16[2,96,384]{2,1,0:T(8,128)(2,1)S(1)} %template_spectrum.1), channel_id=1, source_target_pairs={{0,32},{16,48},{32,0},{48,16},{1,33},{17,49},{33,1},{49,17},{2,34}... | collective-permute-start | bytes 442376 | tf_op jit(solution)/shard_map/ppermute | solution.py:592
  21.8 0.9 %collective-permute-start.1 = (bf16[2,96,384]{2,1,0:T(8,128)(2,1)S(1)}, bf16[2,96,384]{2,1,0:T(8,128)(2,1)S(1)}, u32[]{:S(2)}, u32[]{:S(2)}) collective-permute-start(bf16[2,96,384]{2,1,0:T(8,128)(2,1)S(1)} %template_spectrum.1), channel_id=1, source_target_pairs={{0,48},{16,0},{32,16},{48,32},{1,49},{17,1},{33,17},{49,33},{2,50}... | collective-permute-start | bytes 442376 | tf_op jit(solution)/shard_map/ppermute | solution.py:592
  22.6 0.6 collective-permute-start
  23.2 8.3 %collective-permute-done.2 = bf16[2,96,384]{2,1,0:T(8,128)(2,1)S(1)} collective-permute-done((bf16[2,96,384]{2,1,0:T(8,128)(2,1)S(1)}, bf16[2,96,384]{2,1,0:T(8,128)(2,1)S(1)}, u32[]{:S(2)}, u32[]{:S(2)}) %collective-permute-start.2) | collective-permute-done | bytes 147488 | tf_op jit(solution)/shard_map/ppermute | solution.py:592
  31.5 1.3 %collective-permute-done.1 = bf16[2,96,384]{2,1,0:T(8,128)(2,1)S(1)} collective-permute-done((bf16[2,96,384]{2,1,0:T(8,128)(2,1)S(1)}, bf16[2,96,384]{2,1,0:T(8,128)(2,1)S(1)}, u32[]{:S(2)}, u32[]{:S(2)}) %collective-permute-start.1) | collective-permute-done | bytes 147488 | tf_op jit(solution)/shard_map/ppermute | solution.py:592
  32.8 1.9 %collective-permute-done = bf16[2,96,384]{2,1,0:T(8,128)(2,1)S(1)} collective-permute-done((bf16[2,96,384]{2,1,0:T(8,128)(2,1)S(1)}, bf16[2,96,384]{2,1,0:T(8,128)(2,1)S(1)}, u32[]{:S(2)}, u32[]{:S(2)}) %collective-permute-start) | collective-permute-done | bytes 147488 | tf_op jit(solution)/shard_map/ppermute | solution.py:592
  34.7 0.4 collective-permute-start.3
  35.2 0.2 collective-permute-start.7
  35.3 2.6 %collective-permute-start.5 = (bf16[2,2,96,384]{3,2,1,0:T(8,128)(2,1)S(1)}, bf16[2,2,96,384]{3,2,1,0:T(8,128)(2,1)}, u32[]{:S(2)}, u32[]{:S(2)}) collective-permute-start(bf16[2,2,96,384]{3,2,1,0:T(8,128)(2,1)S(1)} %pad_maximum_fusion.1.o1), channel_id=1, source_target_pairs={{0,66},{64,0},{2,64},{66,2},{1,67},{65,1},{3,65},{67,3},{4,70},{68... | collective-permute-start | bytes 884744 | tf_op jit(solution)/shard_map/ppermute | solution.py:599
  38.0 0.8 %collective-permute-start.6 = (bf16[2,2,96,384]{3,2,1,0:T(8,128)(2,1)S(1)}, bf16[2,2,96,384]{3,2,1,0:T(8,128)(2,1)}, u32[]{:S(2)}, u32[]{:S(2)}) collective-permute-start(bf16[2,2,96,384]{3,2,1,0:T(8,128)(2,1)S(1)} %pad_maximum_fusion.o0), channel_id=1, source_target_pairs={{0,1},{1,0},{2,3},{3,2},{4,5},{5,4},{6,7},{7,6},{8,9},{9,8},{10,11... | collective-permute-start | bytes 884744 | tf_op jit(solution)/shard_map/ppermute | solution.py:585
  38.8 0.8 %copy-done.6 = bf16[64,40,128]{2,1,0:T(8,128)(2,1)} copy-done((bf16[64,40,128]{2,1,0:T(8,128)(2,1)}, bf16[64,40,128]{2,1,0:T(8,128)(2,1)S(1)}, u32[]{:S(2)}) %copy-start.6) | copy-done | bytes 655384
  39.6 10.0 %refine_slab.1 = f32[128,128]{1,0:T(8,128)} custom-call(bf16[64,40,128]{2,1,0:T(8,128)(2,1)} %copy-done.3, bf16[64,40,128]{2,1,0:T(8,128)(2,1)} %copy-done.6, bf16[384,768]{1,0:T(8,128)(2,1)} %constant.29.clone.pair_hbm, bf16[128,384]{1,0:T(8,128)(2,1)} %constant.32.clone.field_hbm, bf16[2304,128]{1,0:T(8,128)(2,1)} %constant.33.clone.comb_hbm, ...), custom_call_target="tpu_custom_call" | custom-call | flops 8999999488 | bytes 4194304 | tf_op jit(solution)/shard_map/refine_slab/pallas_call | solution.py:413
  49.7 0.4 collective-permute-start.8
  50.1 0.2 collective-permute-start.9
  50.3 8.1 %all-to-all-start.1 = ((f32[64,2,128]{2,1,0:T(2,128)}), f32[64,2,128]{2,1,0:T(2,128)S(1)}, u32[]{:S(2)}, u32[]{:S(2)}) async-start(f32[64,2,128]{2,1,0:T(2,128)} %bitcast.13), calls=%async_computation.1 | async-start | bytes 131072 | tf_op jit(solution)/shard_map/all_to_all | solution.py:605
  58.5 0.7 %copy-done.7 = bf16[2,2,96,384]{3,2,1,0:T(8,128)(2,1)} copy-done((bf16[2,2,96,384]{3,2,1,0:T(8,128)(2,1)}, bf16[2,2,96,384]{3,2,1,0:T(8,128)(2,1)S(1)}, u32[]{:S(2)}) %copy-start.7) | copy-done | bytes 294936
  59.2 0.1 copy-done.8
  59.3 8.1 %search_templates.1 = (f32[384,384]{1,0:T(8,128)}, f32[384,384]{1,0:T(8,128)}) custom-call(bf16[2,192,384]{2,1,0:T(8,128)(2,1)} %get-tuple-element.19.spec_hbm, bf16[2,2,96,384]{3,2,1,0:T(8,128)(2,1)} %copy-done.5, bf16[2,2,96,384]{3,2,1,0:T(8,128)(2,1)} %copy-done.4, bf16[2,2,96,384]{3,2,1,0:T(8,128)(2,1)} %collective-permute-done.4.o2, ...), custom_call_target="tpu_custom_call" | custom-call | flops 4000000000 | bytes 6291456 | tf_op jit(solution)/shard_map/search_templates/pallas_call | solution.py:548
  67.4 0.1 reduce_sum.9
  67.5 0.7 %reshape.21 = f32[16,16]{1,0:T(8,128)} reshape(f32[2,128]{1,0:T(2,128)S(1)} %reduce_sum.9) | data formatting | bytes 2048 | tf_op jit(solution)/shard_map/reshape | solution.py:608
  (26 shorter events, 0.1 us)
Async XLA Ops:
  0.6 16.8 %copy-start = (bf16[384,768]{1,0:T(8,128)(2,1)S(1)}, bf16[384,768]{1,0:T(8,128)(2,1)}, u32[]{:S(2)}) copy-start(bf16[384,768]{1,0:T(8,128)(2,1)} %constant.29.clone.pair_hbm) | copy-start | bytes 1769476
  0.6 16.8 %copy-start.1 = (bf16[1,384,384]{2,1,0:T(8,128)(2,1)S(1)}, bf16[1,384,384]{2,1,0:T(8,128)(2,1)}, u32[]{:S(2)}) copy-start(bf16[1,384,384]{2,1,0:T(8,128)(2,1)} %template_hbm.1) | copy-start | bytes 884740
  0.7 16.8 %copy-start.2 = (bf16[2,192,384]{2,1,0:T(8,128)(2,1)S(1)}, bf16[2,192,384]{2,1,0:T(8,128)(2,1)}, u32[]{:S(2)}) copy-start(bf16[2,192,384]{2,1,0:T(8,128)(2,1)} %constant.31.clone.halves_hbm) | copy-start | bytes 884740
  5.5 29.2 %all-to-all-start = ((bf16[64,40,128]{2,1,0:T(8,128)(2,1)}), bf16[64,40,128]{2,1,0:T(8,128)(2,1)S(1)}, u32[]{:S(2)}, u32[]{:S(2)}) async-start(bf16[64,40,128]{2,1,0:T(8,128)(2,1)} %get-tuple-element.17), calls=%async_computation | async-start | bytes 1310720 | tf_op jit(solution)/shard_map/all_to_all | solution.py:590
  19.2 12.4 %collective-permute-start.2 = (bf16[2,96,384]{2,1,0:T(8,128)(2,1)S(1)}, bf16[2,96,384]{2,1,0:T(8,128)(2,1)S(1)}, u32[]{:S(2)}, u32[]{:S(2)}) collective-permute-start(bf16[2,96,384]{2,1,0:T(8,128)(2,1)S(1)} %template_spectrum.1), channel_id=1, source_target_pairs={{0,32},{16,48},{32,0},{48,16},{1,33},{17,49},{33,1},{49,17},{2,34}... | collective-permute-start | bytes 442376 | tf_op jit(solution)/shard_map/ppermute | solution.py:592
  21.8 11.1 %collective-permute-start.1 = (bf16[2,96,384]{2,1,0:T(8,128)(2,1)S(1)}, bf16[2,96,384]{2,1,0:T(8,128)(2,1)S(1)}, u32[]{:S(2)}, u32[]{:S(2)}) collective-permute-start(bf16[2,96,384]{2,1,0:T(8,128)(2,1)S(1)} %template_spectrum.1), channel_id=1, source_target_pairs={{0,48},{16,0},{32,16},{48,32},{1,49},{17,1},{33,17},{49,33},{2,50}... | collective-permute-start | bytes 442376 | tf_op jit(solution)/shard_map/ppermute | solution.py:592
  22.6 12.1 %collective-permute-start = (bf16[2,96,384]{2,1,0:T(8,128)(2,1)S(1)}, bf16[2,96,384]{2,1,0:T(8,128)(2,1)S(1)}, u32[]{:S(2)}, u32[]{:S(2)}) collective-permute-start(bf16[2,96,384]{2,1,0:T(8,128)(2,1)S(1)} %template_spectrum.1), channel_id=1, source_target_pairs={{0,16},{16,32},{32,48},{48,0},{1,17},{17,33},{33,49},{49,1},{2,18}... | collective-permute-start | bytes 442376 | tf_op jit(solution)/shard_map/ppermute | solution.py:592
  34.7 4.1 %copy-start.3 = (bf16[64,40,128]{2,1,0:T(8,128)(2,1)}, bf16[64,40,128]{2,1,0:T(8,128)(2,1)S(1)}, u32[]{:S(2)}) copy-start(bf16[64,40,128]{2,1,0:T(8,128)(2,1)S(1)} %all-to-all-done.own_hbm) | copy-start | bytes 1966084
  34.7 4.1 %collective-permute-start.3 = (bf16[64,40,128]{2,1,0:T(8,128)(2,1)S(1)}, bf16[64,40,128]{2,1,0:T(8,128)(2,1)S(1)}, u32[]{:S(2)}, u32[]{:S(2)}) collective-permute-start(bf16[64,40,128]{2,1,0:T(8,128)(2,1)S(1)} %all-to-all-done.own_hbm), channel_id=1, source_target_pairs={{0,1},{1,0},{2,3},{3,2},{4,5},{5,4},{6,7},{7,6},{8,9},{9,8},{10,11... | collective-permute-start | bytes 1966088 | tf_op jit(solution)/shard_map/ppermute | solution.py:585
  35.2 14.5 %copy-start.4 = (bf16[2,2,96,384]{3,2,1,0:T(8,128)(2,1)}, bf16[2,2,96,384]{3,2,1,0:T(8,128)(2,1)S(1)}, u32[]{:S(2)}) copy-start(bf16[2,2,96,384]{3,2,1,0:T(8,128)(2,1)S(1)} %pad_maximum_fusion.1.o1) | copy-start | bytes 884740
  35.2 23.2 %collective-permute-start.7 = (bf16[2,2,96,384]{3,2,1,0:T(8,128)(2,1)S(1)}, bf16[2,2,96,384]{3,2,1,0:T(8,128)(2,1)}, u32[]{:S(2)}, u32[]{:S(2)}) collective-permute-start(bf16[2,2,96,384]{3,2,1,0:T(8,128)(2,1)S(1)} %pad_maximum_fusion.1.o1), channel_id=1, source_target_pairs={{0,1},{1,0},{2,3},{3,2},{4,5},{5,4},{6,7},{7,6},{8,9},{9,8},{10,11... | collective-permute-start | bytes 884744 | tf_op jit(solution)/shard_map/ppermute | solution.py:585
  35.3 14.3 %collective-permute-start.5 = (bf16[2,2,96,384]{3,2,1,0:T(8,128)(2,1)S(1)}, bf16[2,2,96,384]{3,2,1,0:T(8,128)(2,1)}, u32[]{:S(2)}, u32[]{:S(2)}) collective-permute-start(bf16[2,2,96,384]{3,2,1,0:T(8,128)(2,1)S(1)} %pad_maximum_fusion.1.o1), channel_id=1, source_target_pairs={{0,66},{64,0},{2,64},{66,2},{1,67},{65,1},{3,65},{67,3},{4,70},{68... | collective-permute-start | bytes 884744 | tf_op jit(solution)/shard_map/ppermute | solution.py:599
  38.0 11.7 %copy-start.5 = (bf16[2,2,96,384]{3,2,1,0:T(8,128)(2,1)}, bf16[2,2,96,384]{3,2,1,0:T(8,128)(2,1)S(1)}, u32[]{:S(2)}) copy-start(bf16[2,2,96,384]{3,2,1,0:T(8,128)(2,1)S(1)} %pad_maximum_fusion.o0) | copy-start | bytes 884740
  38.0 20.4 %collective-permute-start.6 = (bf16[2,2,96,384]{3,2,1,0:T(8,128)(2,1)S(1)}, bf16[2,2,96,384]{3,2,1,0:T(8,128)(2,1)}, u32[]{:S(2)}, u32[]{:S(2)}) collective-permute-start(bf16[2,2,96,384]{3,2,1,0:T(8,128)(2,1)S(1)} %pad_maximum_fusion.o0), channel_id=1, source_target_pairs={{0,1},{1,0},{2,3},{3,2},{4,5},{5,4},{6,7},{7,6},{8,9},{9,8},{10,11... | collective-permute-start | bytes 884744 | tf_op jit(solution)/shard_map/ppermute | solution.py:585
  38.8 10.9 %collective-permute-start.4 = (bf16[2,2,96,384]{3,2,1,0:T(8,128)(2,1)S(1)}, bf16[2,2,96,384]{3,2,1,0:T(8,128)(2,1)}, u32[]{:S(2)}, u32[]{:S(2)}) collective-permute-start(bf16[2,2,96,384]{3,2,1,0:T(8,128)(2,1)S(1)} %pad_maximum_fusion.o0), channel_id=1, source_target_pairs={{0,64},{64,2},{2,66},{66,0},{1,65},{65,3},{3,67},{67,1},{4,68},{68... | collective-permute-start | bytes 884744 | tf_op jit(solution)/shard_map/ppermute | solution.py:598
  38.8 0.8 %copy-start.6 = (bf16[64,40,128]{2,1,0:T(8,128)(2,1)}, bf16[64,40,128]{2,1,0:T(8,128)(2,1)S(1)}, u32[]{:S(2)}) copy-start(bf16[64,40,128]{2,1,0:T(8,128)(2,1)S(1)} %collective-permute-done.3.other_hbm) | copy-start | bytes 1966084
  49.7 8.8 %collective-permute-start.8 = (bf16[2,2,96,384]{3,2,1,0:T(8,128)(2,1)}, bf16[2,2,96,384]{3,2,1,0:T(8,128)(2,1)S(1)}, u32[]{:S(2)}, u32[]{:S(2)}) collective-permute-start(bf16[2,2,96,384]{3,2,1,0:T(8,128)(2,1)} %collective-permute-done.4.o2), channel_id=1, source_target_pairs={{0,1},{1,0},{2,3},{3,2},{4,5},{5,4},{6,7},{7,6},{8,9},{9,8},{10,11... | collective-permute-start | bytes 884744 | tf_op jit(solution)/shard_map/ppermute | solution.py:585
  50.1 8.4 %collective-permute-start.9 = (bf16[2,2,96,384]{3,2,1,0:T(8,128)(2,1)}, bf16[2,2,96,384]{3,2,1,0:T(8,128)(2,1)S(1)}, u32[]{:S(2)}, u32[]{:S(2)}) collective-permute-start(bf16[2,2,96,384]{3,2,1,0:T(8,128)(2,1)} %collective-permute-done.5.o3), channel_id=1, source_target_pairs={{0,1},{1,0},{2,3},{3,2},{4,5},{5,4},{6,7},{7,6},{8,9},{9,8},{10,11... | collective-permute-start | bytes 884744 | tf_op jit(solution)/shard_map/ppermute | solution.py:585
  50.3 17.1 %all-to-all-start.1 = ((f32[64,2,128]{2,1,0:T(2,128)}), f32[64,2,128]{2,1,0:T(2,128)S(1)}, u32[]{:S(2)}, u32[]{:S(2)}) async-start(f32[64,2,128]{2,1,0:T(2,128)} %bitcast.13), calls=%async_computation.1 | async-start | bytes 131072 | tf_op jit(solution)/shard_map/all_to_all | solution.py:605
  58.5 0.7 %copy-start.7 = (bf16[2,2,96,384]{3,2,1,0:T(8,128)(2,1)}, bf16[2,2,96,384]{3,2,1,0:T(8,128)(2,1)S(1)}, u32[]{:S(2)}) copy-start(bf16[2,2,96,384]{3,2,1,0:T(8,128)(2,1)S(1)} %collective-permute-done.8.p2) | copy-start | bytes 884740
  58.5 0.8 %copy-start.8 = (bf16[2,2,96,384]{3,2,1,0:T(8,128)(2,1)}, bf16[2,2,96,384]{3,2,1,0:T(8,128)(2,1)S(1)}, u32[]{:S(2)}) copy-start(bf16[2,2,96,384]{3,2,1,0:T(8,128)(2,1)S(1)} %collective-permute-done.9.p3) | copy-start | bytes 884740

commit v4 on v3

--- a/solution.py
+++ b/solution.py
@@ -99,13 +99,13 @@
                 on = w * ((ac < 9) & (c == shift))
                 last[s, 0, at], last[s, 0, at + 1] = on * ca[0], -on * sa[0]
                 last[s, 1, at], last[s, 1, at + 1] = -on * sa[0], -on * ca[0]
+    tail = np.concatenate([reverse, inverse_rows.reshape(L, H), np.zeros((L, H))], 1)
+    bundle = np.concatenate([inverse_cols, tail], 0)
     return dict(
+        bundle=bf(bundle),
         forward=bf(forward),
         halves=bf(halves),
         pair=bf(pair),
-        inverse_cols=bf(inverse_cols),
-        inverse_rows=bf(inverse_rows),
-        reverse=bf(reverse),
         pick=bf(pick.reshape(4 * L, 128)),
         field=bf(field.reshape(128, 384)),
         comb=bf(comb.reshape(6 * L, 128)),
@@ -443,12 +443,13 @@
 
 
 def search_kernel(
-    spec_hbm, o0, o1, o2, o3, p0, p1, p2, p3, cols_hbm, rows_hbm, reverse_hbm, mip, zmap,
+    spec_hbm, o0, o1, o2, o3, p0, p1, p2, p3, bundle_hbm, mip, zmap,
     spec, own, oth, own_top, oth_top, cols, rows, reverse, prod, total, square, sems,
 ):
     core = lax.axis_index("core")
     owns, others = (o0, o1, o2, o3), (p0, p1, p2, p3)
-    jobs = [(spec_hbm, spec), (reverse_hbm, reverse)]
+    lower = pl.ds(2 * L, L)
+    jobs = [(spec_hbm, spec), (bundle_hbm.at[lower, pl.ds(0, L)], reverse)]
     for p in range(4):
         jobs.append((owns[p].at[:, :, pl.ds(0, 16), :], own_top.at[pl.ds(2 * p, 2)]))
         jobs.append((others[p].at[:, :, pl.ds(0, 16), :], oth_top.at[pl.ds(2 * p, 2)]))
@@ -457,7 +458,7 @@
         jobs.append((owns[p], own.at[pl.ds(2 * p, 2)]))
         jobs.append((others[p], oth.at[pl.ds(2 * p, 2)]))
         if p == 0:
-            jobs += [(cols_hbm, cols), (rows_hbm, rows)]
+            jobs += [(bundle_hbm.at[pl.ds(0, 2 * L)], cols), (bundle_hbm.at[lower, pl.ds(L, 256)], rows)]
     copies = [pltpu.make_async_copy(src, dst, sems.at[n]) for n, (src, dst) in enumerate(jobs)]
     for copy in copies:
         copy.start()
@@ -521,7 +522,7 @@
             for k in range(2):
                 part = middle[H * k + Q * c : H * k + Q * c + Q]
                 both.append(jnp.concatenate([part[:, :L], part[:, L:]], 0))
-            kinds.append(dot(rows[c], jnp.concatenate(both, 1)) * (1.0 / (L * L)))
+            kinds.append(dot(rows[H * c : H * c + H, :H], jnp.concatenate(both, 1)) * (1.0 / (L * L)))
         for at, corr in ((slice(0, H), kinds[0] + kinds[1]), (slice(H, L), kinds[0] - kinds[1])):
             one, two = corr[:, :L], corr[:, L:]
             largest = jnp.maximum(one, two)
@@ -549,7 +550,7 @@
         search_kernel,
         out_shape=(jax.ShapeDtypeStruct((L, L), F32), jax.ShapeDtypeStruct((L, L), F32)),
         grid=(1,),
-        in_specs=[held] + [pl.BlockSpec(memory_space=pl.ANY)] * 8 + [held] * 3,
+        in_specs=[held] + [pl.BlockSpec(memory_space=pl.ANY)] * 8 + [held],
         out_specs=[full_spec((L, L)), full_spec((L, L))],
         scratch_shapes=[
             pltpu.VMEM((2, H, L), BF),
@@ -558,17 +559,17 @@
             pltpu.VMEM((8, 2, 16, L), BF),
             pltpu.VMEM((8, 2, 16, L), BF),
             pltpu.VMEM((2 * L, 2 * L), BF),
-            pltpu.VMEM((2, H, H), BF),
+            pltpu.VMEM((L, 256), BF),
             pltpu.VMEM((L, L), BF),
             pltpu.VMEM((8, H, 2 * L), BF),
             pltpu.VMEM((L, L), F32),
             pltpu.VMEM((L, L), F32),
             pltpu.SemaphoreType.DMA((20,)),
         ],
-        compiler_params=pltpu.CompilerParams(vmem_limit_bytes=56 * MB),
+        compiler_params=pltpu.CompilerParams(vmem_limit_bytes=46 * MB),
         cost_estimate=pl.CostEstimate(flops=4_000_000_000, bytes_accessed=6 * MB, transcendentals=0),
         name="search_templates",
-    )(spec, *owns, *others, TAB["inverse_cols"], TAB["inverse_rows"], TAB["reverse"])
+    )(spec, *owns, *others, TAB["bundle"])
 
 
 def ring(count, step):

time: 68.4 us -> 67.7 us (0.990)
    unnamed x18 -> x12, local copies, waits for them, and re-layouts: 1.66 us -> 1.5 us
  transfers between devices with their start and end apart: 12 -> 12, of which waited for: 3 -> 3; matrix products, arithmetic and copies ran while one was open for 0% -> 0% of each run, Pallas kernels for 29% -> 28%
where the time goes in v4:
time: 67.7 us; the launch traced here: 67.4 us
  starting transfers between devices  28.8 us (43%)
  Pallas kernels  23.9 us (35%)
  waiting for transfers between devices  11.5 us (17%)
  local copies, waits for them, and re-layouts  2.18 us (3%)
  between operations  0.83 us (1%)
    all_to_all x1, starting transfers between devices, body(): arrived = lax.all_to_all(message, CHIPS, 0, 0, tiled=True)  12 us
    ppermute x3, waiting for transfers between devices, body(): along = [lax.ppermute(half, 'y', ring(4, step)) for step in (1, 3, 2)]  11.5 us
    pallas_call x1, Pallas kernels, refine(): pl.pallas_call(refine_kernel, out_shape=jax.ShapeDtypeStruct((128, 128),...  10 us
    all_to_all x1, starting transfers between devices, body(): lax.all_to_all(scores.reshape(SLABS, 2, 128), CHIPS, 0, 0, tiled=True)  8.02 us
    pallas_call x1, Pallas kernels, search(): pl.pallas_call(search_kernel, out_shape=(jax.ShapeDtypeStruct((L, L), F32...  7.51 us
    pallas_call x1, Pallas kernels, prepare(): pl.pallas_call(prepare_kernel, out_shape=(jax.ShapeDtypeStruct((SLABS, RO...  4.77 us
    ppermute x3, starting transfers between devices, body(): along = [lax.ppermute(half, 'y', ring(4, step)) for step in (1, 3, 2)]  4.07 us
    ppermute x1, starting transfers between devices, body(): lax.ppermute(upper, ('zl', 'zh'), z_ring(3))  2.6 us
  transfers between devices with their start and end apart: 12, of which 3 were waited for; matrix products, arithmetic and copies ran while one was open for 0% of the time, Pallas kernels for 28%

profile of v4, /device:TPU:1, one launch (start us, length us, event | category | flops | bytes accessed | tf_op | source)
XLA Modules:
  0.0 67.4 jit_solution(7767126721016898418)
XLA Ops:
  0.6 0.0 copy-start
  0.7 0.0 copy-start.4
  0.7 4.8 %prepare_spectra.1 = (bf16[64,40,128]{2,1,0:T(8,128)(2,1)}, bf16[2,192,384]{2,1,0:T(8,128)(2,1)}) custom-call(s32[2,16]{1,0:T(2,128)} %bitcast.15, s32[1,16]{1,0:T(1,128)} %bitcast.16, s32[1,16]{1,0:T(1,128)} %bitcast.17, bf16[384,384]{1,0:T(8,128)(2,1)} %tile_hbm.1, bf16[8,384,384]{2,1,0:T(8,128)(2,1)} %bank_hbm.1, ...), custom_call_target="tpu_custom_call" | custom-call | flops 1000000000 | bytes 4194304 | tf_op jit(solution)/shard_map/prepare_spectra/pallas_call | solution.py:216
  5.4 12.0 %all-to-all-start = ((bf16[64,40,128]{2,1,0:T(8,128)(2,1)}), bf16[64,40,128]{2,1,0:T(8,128)(2,1)S(1)}, u32[]{:S(2)}, u32[]{:S(2)}) async-start(bf16[64,40,128]{2,1,0:T(8,128)(2,1)} %get-tuple-element.17), calls=%async_computation | async-start | bytes 1310720 | tf_op jit(solution)/shard_map/all_to_all | solution.py:591
  17.5 1.7 %template_spectrum.1 = bf16[2,96,384]{2,1,0:T(8,128)(2,1)S(1)} custom-call(bf16[1,384,384]{2,1,0:T(8,128)(2,1)S(1)} %copy-done.1, bf16[2,192,384]{2,1,0:T(8,128)(2,1)S(1)} %copy-done.4, bf16[384,768]{1,0:T(8,128)(2,1)S(1)} %copy-done), custom_call_target="tpu_custom_call" | custom-call | flops 400000000 | bytes 4194304 | tf_op jit(solution)/shard_map/template_spectrum/pallas_call | solution.py:263
  19.1 2.6 %collective-permute-start.2 = (bf16[2,96,384]{2,1,0:T(8,128)(2,1)S(1)}, bf16[2,96,384]{2,1,0:T(8,128)(2,1)S(1)}, u32[]{:S(2)}, u32[]{:S(2)}) collective-permute-start(bf16[2,96,384]{2,1,0:T(8,128)(2,1)S(1)} %template_spectrum.1), channel_id=1, source_target_pairs={{0,32},{16,48},{32,0},{48,16},{1,33},{17,49},{33,1},{49,17},{2,34}... | collective-permute-start | bytes 442376 | tf_op jit(solution)/shard_map/ppermute | solution.py:593
  21.7 0.9 %collective-permute-start.1 = (bf16[2,96,384]{2,1,0:T(8,128)(2,1)S(1)}, bf16[2,96,384]{2,1,0:T(8,128)(2,1)S(1)}, u32[]{:S(2)}, u32[]{:S(2)}) collective-permute-start(bf16[2,96,384]{2,1,0:T(8,128)(2,1)S(1)} %template_spectrum.1), channel_id=1, source_target_pairs={{0,48},{16,0},{32,16},{48,32},{1,49},{17,1},{33,17},{49,33},{2,50}... | collective-permute-start | bytes 442376 | tf_op jit(solution)/shard_map/ppermute | solution.py:593
  22.6 0.6 collective-permute-start
  23.2 8.3 %collective-permute-done.2 = bf16[2,96,384]{2,1,0:T(8,128)(2,1)S(1)} collective-permute-done((bf16[2,96,384]{2,1,0:T(8,128)(2,1)S(1)}, bf16[2,96,384]{2,1,0:T(8,128)(2,1)S(1)}, u32[]{:S(2)}, u32[]{:S(2)}) %collective-permute-start.2) | collective-permute-done | bytes 147488 | tf_op jit(solution)/shard_map/ppermute | solution.py:593
  31.5 1.3 %collective-permute-done.1 = bf16[2,96,384]{2,1,0:T(8,128)(2,1)S(1)} collective-permute-done((bf16[2,96,384]{2,1,0:T(8,128)(2,1)S(1)}, bf16[2,96,384]{2,1,0:T(8,128)(2,1)S(1)}, u32[]{:S(2)}, u32[]{:S(2)}) %collective-permute-start.1) | collective-permute-done | bytes 147488 | tf_op jit(solution)/shard_map/ppermute | solution.py:593
  32.8 1.9 %collective-permute-done = bf16[2,96,384]{2,1,0:T(8,128)(2,1)S(1)} collective-permute-done((bf16[2,96,384]{2,1,0:T(8,128)(2,1)S(1)}, bf16[2,96,384]{2,1,0:T(8,128)(2,1)S(1)}, u32[]{:S(2)}, u32[]{:S(2)}) %collective-permute-start) | collective-permute-done | bytes 147488 | tf_op jit(solution)/shard_map/ppermute | solution.py:593
  34.7 0.4 collective-permute-start.3
  35.2 0.2 collective-permute-start.7
  35.3 2.6 %collective-permute-start.5 = (bf16[2,2,96,384]{3,2,1,0:T(8,128)(2,1)S(1)}, bf16[2,2,96,384]{3,2,1,0:T(8,128)(2,1)S(1)}, u32[]{:S(2)}, u32[]{:S(2)}) collective-permute-start(bf16[2,2,96,384]{3,2,1,0:T(8,128)(2,1)S(1)} %pad_maximum_fusion.1.o1), channel_id=1, source_target_pairs={{0,66},{64,0},{2,64},{66,2},{1,67},{65,1},{3,65},{67,3},{4,70},{68... | collective-permute-start | bytes 884744 | tf_op jit(solution)/shard_map/ppermute | solution.py:600
  38.0 0.0 copy-start.2
  38.0 0.8 %collective-permute-start.6 = (bf16[2,2,96,384]{3,2,1,0:T(8,128)(2,1)S(1)}, bf16[2,2,96,384]{3,2,1,0:T(8,128)(2,1)S(1)}, u32[]{:S(2)}, u32[]{:S(2)}) collective-permute-start(bf16[2,2,96,384]{3,2,1,0:T(8,128)(2,1)S(1)} %pad_maximum_fusion.o0), channel_id=1, source_target_pairs={{0,1},{1,0},{2,3},{3,2},{4,5},{5,4},{6,7},{7,6},{8,9},{9,8},{10,11... | collective-permute-start | bytes 884744 | tf_op jit(solution)/shard_map/ppermute | solution.py:586
  38.8 10.0 %refine_slab.1 = f32[128,128]{1,0:T(8,128)} custom-call(bf16[64,40,128]{2,1,0:T(8,128)(2,1)} %copy-done.5, bf16[64,40,128]{2,1,0:T(8,128)(2,1)} %collective-permute-done.3.other_hbm, bf16[384,768]{1,0:T(8,128)(2,1)} %constant.25.clone.pair_hbm, bf16[128,384]{1,0:T(8,128)(2,1)} %constant.28.clone.field_hbm, bf16[2304,128]{1,0:T(8,128)(2,1)} %constant.29.clone.comb_hbm, ...), custom_call_target="tpu_custom_call" | custom-call | flops 8999999488 | bytes 4194304 | tf_op jit(solution)/shard_map/refine_slab/pallas_call | solution.py:413
  48.8 0.7 %collective-permute-start.8 = (bf16[2,2,96,384]{3,2,1,0:T(8,128)(2,1)}, bf16[2,2,96,384]{3,2,1,0:T(8,128)(2,1)S(1)}, u32[]{:S(2)}, u32[]{:S(2)}) collective-permute-start(bf16[2,2,96,384]{3,2,1,0:T(8,128)(2,1)} %collective-permute-done.4.o2), channel_id=1, source_target_pairs={{0,1},{1,0},{2,3},{3,2},{4,5},{5,4},{6,7},{7,6},{8,9},{9,8},{10,11... | collective-permute-start | bytes 884744 | tf_op jit(solution)/shard_map/ppermute | solution.py:586
  49.5 8.0 %all-to-all-start.1 = ((f32[64,2,128]{2,1,0:T(2,128)}), f32[64,2,128]{2,1,0:T(2,128)S(1)}, u32[]{:S(2)}, u32[]{:S(2)}) async-start(f32[64,2,128]{2,1,0:T(2,128)} %bitcast.13), calls=%async_computation.1 | async-start | bytes 131072 | tf_op jit(solution)/shard_map/all_to_all | solution.py:606
  57.6 0.0 copy-start.3
  57.6 1.5 %copy-done.3 = bf16[1152,768]{1,0:T(8,128)(2,1)S(1)} copy-done((bf16[1152,768]{1,0:T(8,128)(2,1)S(1)}, bf16[1152,768]{1,0:T(8,128)(2,1)}, u32[]{:S(2)}) %copy-start.3) | copy-done | bytes 1769496
  59.1 7.5 %search_templates.1 = (f32[384,384]{1,0:T(8,128)}, f32[384,384]{1,0:T(8,128)}) custom-call(bf16[2,192,384]{2,1,0:T(8,128)(2,1)S(1)} %copy-done.2, bf16[2,2,96,384]{3,2,1,0:T(8,128)(2,1)S(1)} %pad_maximum_fusion.o0, bf16[2,2,96,384]{3,2,1,0:T(8,128)(2,1)S(1)} %pad_maximum_fusion.1.o1, bf16[2,2,96,384]{3,2,1,0:T(8,128)(2,1)} %collective-permute-done.4.o2, ...), custom_call_target="tpu_custom_call" | custom-call | flops 4000000000 | bytes 6291456 | tf_op jit(solution)/shard_map/search_templates/pallas_call | solution.py:549
  66.6 0.1 reduce_sum.9
  66.7 0.7 %reshape.21 = f32[16,16]{1,0:T(8,128)} reshape(f32[2,128]{1,0:T(2,128)S(1)} %reduce_sum.9) | data formatting | bytes 2048 | tf_op jit(solution)/shard_map/reshape | solution.py:609
  (20 shorter events, 0.1 us)
Async XLA Ops:
  0.6 16.8 %copy-start = (bf16[384,768]{1,0:T(8,128)(2,1)S(1)}, bf16[384,768]{1,0:T(8,128)(2,1)}, u32[]{:S(2)}) copy-start(bf16[384,768]{1,0:T(8,128)(2,1)} %constant.25.clone.pair_hbm) | copy-start | bytes 1769476
  0.6 16.8 %copy-start.1 = (bf16[1,384,384]{2,1,0:T(8,128)(2,1)S(1)}, bf16[1,384,384]{2,1,0:T(8,128)(2,1)}, u32[]{:S(2)}) copy-start(bf16[1,384,384]{2,1,0:T(8,128)(2,1)} %template_hbm.1) | copy-start | bytes 884740
  0.7 16.8 %copy-start.4 = (bf16[2,192,384]{2,1,0:T(8,128)(2,1)S(1)}, bf16[2,192,384]{2,1,0:T(8,128)(2,1)}, u32[]{:S(2)}) copy-start(bf16[2,192,384]{2,1,0:T(8,128)(2,1)} %constant.27.clone.halves_hbm) | copy-start | bytes 884740
  5.4 29.2 %all-to-all-start = ((bf16[64,40,128]{2,1,0:T(8,128)(2,1)}), bf16[64,40,128]{2,1,0:T(8,128)(2,1)S(1)}, u32[]{:S(2)}, u32[]{:S(2)}) async-start(bf16[64,40,128]{2,1,0:T(8,128)(2,1)} %get-tuple-element.17), calls=%async_computation | async-start | bytes 1310720 | tf_op jit(solution)/shard_map/all_to_all | solution.py:591
  19.1 12.4 %collective-permute-start.2 = (bf16[2,96,384]{2,1,0:T(8,128)(2,1)S(1)}, bf16[2,96,384]{2,1,0:T(8,128)(2,1)S(1)}, u32[]{:S(2)}, u32[]{:S(2)}) collective-permute-start(bf16[2,96,384]{2,1,0:T(8,128)(2,1)S(1)} %template_spectrum.1), channel_id=1, source_target_pairs={{0,32},{16,48},{32,0},{48,16},{1,33},{17,49},{33,1},{49,17},{2,34}... | collective-permute-start | bytes 442376 | tf_op jit(solution)/shard_map/ppermute | solution.py:593
  21.7 11.1 %collective-permute-start.1 = (bf16[2,96,384]{2,1,0:T(8,128)(2,1)S(1)}, bf16[2,96,384]{2,1,0:T(8,128)(2,1)S(1)}, u32[]{:S(2)}, u32[]{:S(2)}) collective-permute-start(bf16[2,96,384]{2,1,0:T(8,128)(2,1)S(1)} %template_spectrum.1), channel_id=1, source_target_pairs={{0,48},{16,0},{32,16},{48,32},{1,49},{17,1},{33,17},{49,33},{2,50}... | collective-permute-start | bytes 442376 | tf_op jit(solution)/shard_map/ppermute | solution.py:593
  22.6 12.1 %collective-permute-start = (bf16[2,96,384]{2,1,0:T(8,128)(2,1)S(1)}, bf16[2,96,384]{2,1,0:T(8,128)(2,1)S(1)}, u32[]{:S(2)}, u32[]{:S(2)}) collective-permute-start(bf16[2,96,384]{2,1,0:T(8,128)(2,1)S(1)} %template_spectrum.1), channel_id=1, source_target_pairs={{0,16},{16,32},{32,48},{48,0},{1,17},{17,33},{33,49},{49,1},{2,18}... | collective-permute-start | bytes 442376 | tf_op jit(solution)/shard_map/ppermute | solution.py:593
  34.7 3.3 %copy-start.5 = (bf16[64,40,128]{2,1,0:T(8,128)(2,1)}, bf16[64,40,128]{2,1,0:T(8,128)(2,1)S(1)}, u32[]{:S(2)}) copy-start(bf16[64,40,128]{2,1,0:T(8,128)(2,1)S(1)} %all-to-all-done.own_hbm) | copy-start | bytes 1966084
  34.7 4.1 %collective-permute-start.3 = (bf16[64,40,128]{2,1,0:T(8,128)(2,1)S(1)}, bf16[64,40,128]{2,1,0:T(8,128)(2,1)}, u32[]{:S(2)}, u32[]{:S(2)}) collective-permute-start(bf16[64,40,128]{2,1,0:T(8,128)(2,1)S(1)} %all-to-all-done.own_hbm), channel_id=1, source_target_pairs={{0,1},{1,0},{2,3},{3,2},{4,5},{5,4},{6,7},{7,6},{8,9},{9,8},{10,11... | collective-permute-start | bytes 1966088 | tf_op jit(solution)/shard_map/ppermute | solution.py:586
  35.2 22.4 %collective-permute-start.7 = (bf16[2,2,96,384]{3,2,1,0:T(8,128)(2,1)S(1)}, bf16[2,2,96,384]{3,2,1,0:T(8,128)(2,1)S(1)}, u32[]{:S(2)}, u32[]{:S(2)}) collective-permute-start(bf16[2,2,96,384]{3,2,1,0:T(8,128)(2,1)S(1)} %pad_maximum_fusion.1.o1), channel_id=1, source_target_pairs={{0,1},{1,0},{2,3},{3,2},{4,5},{5,4},{6,7},{7,6},{8,9},{9,8},{10,11... | collective-permute-start | bytes 884744 | tf_op jit(solution)/shard_map/ppermute | solution.py:586
  35.3 13.5 %collective-permute-start.5 = (bf16[2,2,96,384]{3,2,1,0:T(8,128)(2,1)S(1)}, bf16[2,2,96,384]{3,2,1,0:T(8,128)(2,1)S(1)}, u32[]{:S(2)}, u32[]{:S(2)}) collective-permute-start(bf16[2,2,96,384]{3,2,1,0:T(8,128)(2,1)S(1)} %pad_maximum_fusion.1.o1), channel_id=1, source_target_pairs={{0,66},{64,0},{2,64},{66,2},{1,67},{65,1},{3,65},{67,3},{4,70},{68... | collective-permute-start | bytes 884744 | tf_op jit(solution)/shard_map/ppermute | solution.py:600
  38.0 19.6 %copy-start.2 = (bf16[2,192,384]{2,1,0:T(8,128)(2,1)S(1)}, bf16[2,192,384]{2,1,0:T(8,128)(2,1)}, u32[]{:S(2)}) copy-start(bf16[2,192,384]{2,1,0:T(8,128)(2,1)} %get-tuple-element.19.spec_hbm) | copy-start | bytes 884740
  38.0 19.6 %collective-permute-start.6 = (bf16[2,2,96,384]{3,2,1,0:T(8,128)(2,1)S(1)}, bf16[2,2,96,384]{3,2,1,0:T(8,128)(2,1)S(1)}, u32[]{:S(2)}, u32[]{:S(2)}) collective-permute-start(bf16[2,2,96,384]{3,2,1,0:T(8,128)(2,1)S(1)} %pad_maximum_fusion.o0), channel_id=1, source_target_pairs={{0,1},{1,0},{2,3},{3,2},{4,5},{5,4},{6,7},{7,6},{8,9},{9,8},{10,11... | collective-permute-start | bytes 884744 | tf_op jit(solution)/shard_map/ppermute | solution.py:586
  38.8 10.0 %collective-permute-start.4 = (bf16[2,2,96,384]{3,2,1,0:T(8,128)(2,1)S(1)}, bf16[2,2,96,384]{3,2,1,0:T(8,128)(2,1)}, u32[]{:S(2)}, u32[]{:S(2)}) collective-permute-start(bf16[2,2,96,384]{3,2,1,0:T(8,128)(2,1)S(1)} %pad_maximum_fusion.o0), channel_id=1, source_target_pairs={{0,64},{64,2},{2,66},{66,0},{1,65},{65,3},{3,67},{67,1},{4,68},{68... | collective-permute-start | bytes 884744 | tf_op jit(solution)/shard_map/ppermute | solution.py:599
  48.8 8.8 %collective-permute-start.8 = (bf16[2,2,96,384]{3,2,1,0:T(8,128)(2,1)}, bf16[2,2,96,384]{3,2,1,0:T(8,128)(2,1)S(1)}, u32[]{:S(2)}, u32[]{:S(2)}) collective-permute-start(bf16[2,2,96,384]{3,2,1,0:T(8,128)(2,1)} %collective-permute-done.4.o2), channel_id=1, source_target_pairs={{0,1},{1,0},{2,3},{3,2},{4,5},{5,4},{6,7},{7,6},{8,9},{9,8},{10,11... | collective-permute-start | bytes 884744 | tf_op jit(solution)/shard_map/ppermute | solution.py:586
  49.5 8.1 %collective-permute-start.9 = (bf16[2,2,96,384]{3,2,1,0:T(8,128)(2,1)S(1)}, bf16[2,2,96,384]{3,2,1,0:T(8,128)(2,1)S(1)}, u32[]{:S(2)}, u32[]{:S(2)}) collective-permute-start(bf16[2,2,96,384]{3,2,1,0:T(8,128)(2,1)S(1)} %collective-permute-done.5.o3), channel_id=1, source_target_pairs={{0,1},{1,0},{2,3},{3,2},{4,5},{5,4},{6,7},{7,6},{8,9},{9,8},{10,11... | collective-permute-start | bytes 884744 | tf_op jit(solution)/shard_map/ppermute | solution.py:586
  49.5 17.1 %all-to-all-start.1 = ((f32[64,2,128]{2,1,0:T(2,128)}), f32[64,2,128]{2,1,0:T(2,128)S(1)}, u32[]{:S(2)}, u32[]{:S(2)}) async-start(f32[64,2,128]{2,1,0:T(2,128)} %bitcast.13), calls=%async_computation.1 | async-start | bytes 131072 | tf_op jit(solution)/shard_map/all_to_all | solution.py:606
  57.6 1.5 %copy-start.3 = (bf16[1152,768]{1,0:T(8,128)(2,1)S(1)}, bf16[1152,768]{1,0:T(8,128)(2,1)}, u32[]{:S(2)}) copy-start(bf16[1152,768]{1,0:T(8,128)(2,1)} %constant.34.clone.bundle_hbm) | copy-start | bytes 5308420
